TPU v7x, 512 devices: a whole 4x4x16 slice. The times are simulated.
512 devices in a mesh: section: 32 (over z_lo, y, core), tensor: 16 (over z_hi, x).
Axes of the slice: x: 4, y: 4, z: 16 (z_hi: 4, z_lo: 4; z = z_hi * 4 + z_lo), core: 2. Of those that a mesh axis runs over, the one named last changes fastest.
Arguments:
- layer_input: bfloat16 [768, 8192], P(None, 'section'), may hold values from -6 to 6
- w_up: bfloat16 [8192, 16384], P('section', 'tensor'), may hold values from -0.09375 to 0.09375
- w_down: bfloat16 [8192, 16384], P('section', 'tensor'), may hold values from -0.046875 to 0.046875
- parked_codes: bfloat16 [1536, 16384], P('section', 'tensor'), may hold values from -127 to 127, as said below
- parked_scales: bfloat16 [1536], P('section'), may hold values from 0.0039978027 to 0.029907227
- parked_rows: int32 [1536], P('section'), may hold values from 0 to 767, as said below
- incoming: bfloat16 [768, 8192], P(None, 'section'), may hold values from -6 to 6
Outputs:
- grad_up: bfloat16 [8192, 16384], P('section', 'tensor')
- grad_down: bfloat16 [8192, 16384], P('section', 'tensor')
- passed: bfloat16 [768, 8192], P(None, 'section')
Inputs may be any that keep to these rules, and one draw needn't show every extreme that they name: `parked_codes`: integer values. `parked_rows`: each aligned block of 768 entries (one section) is a permutation of 0 to 767.
All inputs are finite; a program needn't handle non-finite values.
Results may differ from a plain program's by a relative error of at most 0.005.
Values may be sent and summed in bfloat16 or wider, within the bound.
No kernel may reach another device: no remote copies, remote signals or barrier semaphores. Data moves between devices by JAX's collectives and lax.ppermute only.
A program may use at most 64 MiB of HBM per device.

v0:
```python
import jax
import jax.numpy as jnp
from jax import lax
from jax.sharding import PartitionSpec as P

SECTIONS = 2


def partner(value, axis, apart):
    mask = 2**apart
    pairs = [(source, source ^ mask) for source in range(lax.axis_size(axis))]
    return lax.ppermute(value, axis, pairs)


def as_sent(shard):

    def short(part):
        return part.astype(jnp.bfloat16) if part.dtype == jnp.float32 else part

    return jax.tree.map(short, shard)


def passed_along(shard, axis, by):
    count = lax.axis_size(axis)
    pairs = [(i, i + by) for i in range(count) if 0 <= i + by < count]
    return lax.ppermute(shard, axis, pairs)


def shards(layer_input, w_up, w_down, parked_codes, parked_scales, parked_rows, incoming):
    group = lax.axis_size("section") // SECTIONS
    group_bits = group.bit_length() - 1
    section_bits = lax.axis_size("section").bit_length() - 1
    position = lax.axis_index("section")
    bundle = (parked_codes, parked_scales, parked_rows)
    bit_index = 4
    bundle = partner((bundle[0], bundle[1], bundle[2]), "section", bit_index)
    for bit_index in range(group_bits):
        received = jax.tree.map(
            lambda part, own: part.astype(own.dtype),
            partner(as_sent(bundle), "section", bit_index),
            bundle,
        )
        upper = position >> bit_index & 1 == 1
        bundle = tuple(
            (
                jnp.where(upper, jnp.concatenate([got, mine]), jnp.concatenate([mine, got]))
                for got, mine in zip(received, bundle)
            )
        )
    codes, scales, rows = bundle
    values = codes.astype(jnp.float32) * scales.astype(jnp.float32)[:, None]
    hidden_in = jnp.zeros(values.shape, jnp.float32).at[rows].set(values)
    activated = jax.nn.gelu(hidden_in, approximate=False).astype(jnp.bfloat16)
    density = jnp.exp(-0.5 * hidden_in * hidden_in) * 0.3989422804014327
    cumulative = 0.5 * (1.0 + lax.erf(hidden_in * 0.7071067811865476))
    slope = cumulative + hidden_in * density
    partial_act = jnp.dot(incoming, w_down, preferred_element_type=jnp.float32)
    act_grad = partial_act
    for bit_index in range(group_bits):
        act_grad = act_grad + partner(act_grad, "section", bit_index)
    hidden_grad = (act_grad * slope).astype(jnp.bfloat16)
    grad_down = jnp.dot(incoming.T, activated, preferred_element_type=jnp.float32).astype(
        jnp.bfloat16
    )
    grad_up = jnp.dot(layer_input.T, hidden_grad, preferred_element_type=jnp.float32).astype(
        jnp.bfloat16
    )
    partial_grad = jnp.dot(hidden_grad, w_up.T, preferred_element_type=jnp.float32)
    summed = lax.psum(partial_grad, "tensor")
    section_grad = (incoming.astype(jnp.float32) + summed).astype(jnp.bfloat16)
    passed = passed_along(section_grad, "section", -group)
    return (grad_up, grad_down, passed)


def solution(mesh):
    return jax.shard_map(
        shards,
        mesh=mesh,
        in_specs=(
            P(None, "section"),
            P("section", "tensor"),
            P("section", "tensor"),
            P("section", "tensor"),
            P("section"),
            P("section"),
            P(None, "section"),
        ),
        out_specs=(P("section", "tensor"), P("section", "tensor"), P(None, "section")),
        check_vma=False,
    )
```

profile of v0, /device:TPU:24, one launch (start us, length us, event | category | flops | bytes accessed | tf_op | source)
XLA Modules:
  0.0 544.4 jit_solution(13200061014190172996)
XLA Ops:
  7.2 0.0 copy-start
  7.2 0.0 all-reduce.2.cloned.1.call-start
  7.2 1.0 copy-done
  8.2 1.6 fusion.68
  9.8 1.9 collective-permute-start
  11.7 5.6 %collective-permute-done = f32[768,1024]{1,0:T(8,128)S(1)} collective-permute-done((f32[768,1024]{1,0:T(8,128)S(1)}, f32[768,1024]{1,0:T(8,128)S(1)}, u32[]{:S(2)}, u32[]{:S(2)}) %collective-permute-start) | collective-permute-done | bytes 3145760 | tf_op jit(solution)/shard_map/ppermute | solution.py:12
  17.3 1.0 add.36
  18.3 2.7 collective-permute-start.1
  21.0 69.4 %collective-permute-done.1 = f32[768,1024]{1,0:T(8,128)S(1)} collective-permute-done((f32[768,1024]{1,0:T(8,128)S(1)}, f32[768,1024]{1,0:T(8,128)S(1)}, u32[]{:S(2)}, u32[]{:S(2)}) %collective-permute-start.1) | collective-permute-done | bytes 3145760 | tf_op jit(solution)/shard_map/ppermute | solution.py:12
  90.3 1.0 add.37
  91.3 0.0 copy-start.3
  91.3 0.0 copy-start.4
  91.3 0.0 copy-start.5
  91.3 7.4 %collective-permute-start.2 = (f32[768,1024]{1,0:T(8,128)S(1)}, f32[768,1024]{1,0:T(8,128)S(1)}, u32[]{:S(2)}, u32[]{:S(2)}) collective-permute-start(f32[768,1024]{1,0:T(8,128)S(1)} %add.37), channel_id=1, source_target_pairs={{0,64},{16,80},{32,96},{48,112},{64,0},{80,16},{96,32},{112,48},{1... | collective-permute-start | bytes 9437192 | tf_op jit(solution)/shard_map/ppermute | solution.py:12
  98.7 67.9 %collective-permute-done.2 = f32[768,1024]{1,0:T(8,128)S(1)} collective-permute-done((f32[768,1024]{1,0:T(8,128)S(1)}, f32[768,1024]{1,0:T(8,128)S(1)}, u32[]{:S(2)}, u32[]{:S(2)}) %collective-permute-start.2) | collective-permute-done | bytes 3145760 | tf_op jit(solution)/shard_map/ppermute | solution.py:12
  166.6 2.6 add.38
  169.2 1.9 collective-permute-start.3
  171.2 4.7 collective-permute-start.9
  175.8 64.4 %collective-permute-done.9 = bf16[48,1024]{1,0:T(8,128)(2,1)S(1)} collective-permute-done((bf16[48,1024]{1,0:T(8,128)(2,1)S(1)}, bf16[48,1024]{1,0:T(8,128)(2,1)S(1)}, u32[]{:S(2)}, u32[]{:S(2)}) %collective-permute-start.9) | collective-permute-done | bytes 98336 | tf_op jit(solution)/shard_map/ppermute | solution.py:12
  240.3 1.9 collective-permute-start.10
  242.2 1.3 collective-permute-done.10
  243.5 2.4 collective-permute-start.11
  245.9 6.5 %collective-permute-done.11 = bf16[96,1024]{1,0:T(8,128)(2,1)S(1)} collective-permute-done((bf16[96,1024]{1,0:T(8,128)(2,1)S(1)}, bf16[96,1024]{1,0:T(8,128)(2,1)S(1)}, u32[]{:S(2)}, u32[]{:S(2)}) %collective-permute-start.11) | collective-permute-done | bytes 196640 | tf_op jit(solution)/shard_map/ppermute | solution.py:12
  252.4 0.1 maximum_select_fusion.3
  252.5 4.8 collective-permute-start.12
  257.3 5.3 collective-permute-start.14
  262.6 1.9 collective-permute-start.4
  264.6 1.9 collective-permute-start.15
  266.5 2.5 collective-permute-done.4
  268.9 1.9 collective-permute-start.5
  270.9 0.0 collective-permute-done.12
  270.9 0.3 maximum_select_fusion.2
  271.2 1.9 collective-permute-start.13
  273.1 0.0 collective-permute-done.15
  273.1 0.1 broadcast_select_fusion.1
  273.2 2.4 collective-permute-start.16
  275.6 0.1 broadcast_select_fusion.2
  275.7 3.5 collective-permute-start.6
  279.1 0.0 collective-permute-done.16
  279.1 0.1 broadcast_select_fusion.3
  279.2 2.7 collective-permute-start.17
  281.9 0.1 add_select_fusion.1
  282.0 4.7 collective-permute-start.7
  286.6 0.0 collective-permute-done.17
  286.6 0.1 maximum_select_fusion.6
  286.7 3.9 collective-permute-start.18
  290.7 0.1 add_select_fusion
  290.7 2.0 collective-permute-start.8
  292.8 0.3 collective-permute-done.18
  293.1 3.1 collective-permute-done.8
  296.2 9.4 %scatter_custom_fusion = f32[768,1024]{1,0:T(8,128)} fusion(s32[768]{0:T(1024)S(1)} %fusion.36, bf16[384,1024]{1,0:T(8,128)(2,1)S(1)} %maximum_select_fusion.2, bf16[]{:T(256)} %constant.85, bf16[384,1024]{1,0:T(8,128)(2,1)S(1)} %collective-permute-done.13, f32[768]{0:T(1024)S(1)} %fusion.37, f32[]{:T(128)} %constant.39.clone.1, pred[]{:T(512)S(6)} %eq.12), kind=kCustom, calls=%fused_computation.25 | custom fusion | flops 8650752 | bytes 4722695 | tf_op jit(solution)/shard_map/scatter | solution.py:52
  305.7 4.5 fusion.5
  310.2 0.0 copy-start.1
  310.2 1.5 fusion.69
  311.7 0.0 all-reduce.2.cloned.1.call-update
  311.7 208.2 %all-reduce.2.cloned.1.call-done = f32[768,256]{1,0:T(8,128)} async-done(((f32[768,256]{1,0:T(8,128)}), f32[768,256]{1,0:T(8,128)}) %all-reduce.2.cloned.1.call-update) | async-done | bytes 786448 | tf_op jit(solution)/shard_map/psum | solution.py:69
  519.9 2.0 add_convert_fusion
  521.9 1.5 collective-permute-start.19
  523.4 8.5 %fusion.33 = bf16[256,1024]{0,1:T(8,128)(2,1)S(1)} fusion(bf16[768,256]{1,0:T(8,128)(2,1)S(1)} %copy-done.1, f32[768,1024]{1,0:T(8,128)} %scatter_custom_fusion), kind=kOutput, calls=%fused_computation.43 | convolution fusion | flops 454033408 | bytes 4063232 | tf_op jit(solution)/shard_map/dot_general | solution.py:62
  531.9 1.0 copy.13
  532.9 1.6 fusion.32
  534.5 1.0 copy.12
  535.5 1.3 collective-permute-done.19
  536.8 0.7 copy.16
  (17 shorter events, 0.1 us)
Async XLA Ops:
  7.2 1.0 copy-start
  7.2 512.8 %all-reduce.2.cloned.1.call-start = ((), (), s32[]{:S(2)}) async-start(), calls=%async_computation | async-start | bytes 1572864 | tf_op jit(solution)/shard_map/psum | solution.py:69
  9.8 7.6 %collective-permute-start = (f32[768,1024]{1,0:T(8,128)S(1)}, f32[768,1024]{1,0:T(8,128)S(1)}, u32[]{:S(2)}, u32[]{:S(2)}) collective-permute-start(f32[768,1024]{1,0:T(8,128)S(1)} %fusion.68), channel_id=1, source_target_pairs={{0,16},{16,0},{32,48},{48,32},{64,80},{80,64},{96,112},{112,96},{1... | collective-permute-start | bytes 9437192 | tf_op jit(solution)/shard_map/ppermute | solution.py:12
  18.3 72.0 %collective-permute-start.1 = (f32[768,1024]{1,0:T(8,128)S(1)}, f32[768,1024]{1,0:T(8,128)S(1)}, u32[]{:S(2)}, u32[]{:S(2)}) collective-permute-start(f32[768,1024]{1,0:T(8,128)S(1)} %add.36), channel_id=1, source_target_pairs={{0,32},{16,48},{32,0},{48,16},{64,96},{80,112},{96,64},{112,80},{1... | collective-permute-start | bytes 9437192 | tf_op jit(solution)/shard_map/ppermute | solution.py:12
  91.3 79.8 %copy-start.3 = (bf16[48,1024]{1,0:T(8,128)(2,1)S(1)}, bf16[48,1024]{1,0:T(8,128)(2,1)}, u32[]{:S(2)}) copy-start(bf16[48,1024]{1,0:T(8,128)(2,1)} %param.10) | copy-start | bytes 294916
  91.3 166.0 %copy-start.4 = (bf16[48]{0:T(256)(128)(2,1)S(1)}, bf16[48]{0:T(256)(128)(2,1)}, u32[]{:S(2)}) copy-start(bf16[48]{0:T(256)(128)(2,1)} %param.11) | copy-start | bytes 292
  91.3 171.3 %copy-start.5 = (s32[48]{0:T(128)S(1)}, s32[48]{0:T(128)}, u32[]{:S(2)}) copy-start(s32[48]{0:T(128)} %param.12) | copy-start | bytes 580
  91.3 75.2 %collective-permute-start.2 = (f32[768,1024]{1,0:T(8,128)S(1)}, f32[768,1024]{1,0:T(8,128)S(1)}, u32[]{:S(2)}, u32[]{:S(2)}) collective-permute-start(f32[768,1024]{1,0:T(8,128)S(1)} %add.37), channel_id=1, source_target_pairs={{0,64},{16,80},{32,96},{48,112},{64,0},{80,16},{96,32},{112,48},{1... | collective-permute-start | bytes 9437192 | tf_op jit(solution)/shard_map/ppermute | solution.py:12
  169.2 136.4 %collective-permute-start.3 = (f32[768,1024]{1,0:T(8,128)}, f32[768,1024]{1,0:T(8,128)}, u32[]{:S(2)}, u32[]{:S(2)}) collective-permute-start(f32[768,1024]{1,0:T(8,128)} %add.38), channel_id=1, source_target_pairs={{0,128},{16,144},{32,160},{48,176},{64,192},{80,208},{96,224},{112... | collective-permute-start | bytes 9437192 | tf_op jit(solution)/shard_map/ppermute | solution.py:12
  171.2 69.1 %collective-permute-start.9 = (bf16[48,1024]{1,0:T(8,128)(2,1)S(1)}, bf16[48,1024]{1,0:T(8,128)(2,1)S(1)}, u32[]{:S(2)}, u32[]{:S(2)}) collective-permute-start(bf16[48,1024]{1,0:T(8,128)(2,1)S(1)} %copy-done.3), channel_id=1, source_target_pairs={{0,256},{16,272},{32,288},{48,304},{64,320},{80,336},{96,352},{112... | collective-permute-start | bytes 294920 | tf_op jit(solution)/shard_map/ppermute | solution.py:12
  240.3 3.2 collective-permute-start.10
  243.5 8.9 %collective-permute-start.11 = (bf16[96,1024]{1,0:T(8,128)(2,1)S(1)}, bf16[96,1024]{1,0:T(8,128)(2,1)S(1)}, u32[]{:S(2)}, u32[]{:S(2)}) collective-permute-start(bf16[96,1024]{1,0:T(8,128)(2,1)S(1)} %maximum_select_fusion.4), channel_id=1, source_target_pairs={{0,32},{16,48},{32,0},{48,16},{64,96},{80,112},{96,64},{112,80},{1... | collective-permute-start | bytes 589832 | tf_op jit(solution)/shard_map/ppermute | solution.py:12
  252.5 18.4 %collective-permute-start.12 = (bf16[192,1024]{1,0:T(8,128)(2,1)S(1)}, bf16[192,1024]{1,0:T(8,128)(2,1)S(1)}, u32[]{:S(2)}, u32[]{:S(2)}) collective-permute-start(bf16[192,1024]{1,0:T(8,128)(2,1)S(1)} %maximum_select_fusion.3), channel_id=1, source_target_pairs={{0,64},{16,80},{32,96},{48,112},{64,0},{80,16},{96,32},{112,48},{1... | collective-permute-start | bytes 1179656 | tf_op jit(solution)/shard_map/ppermute | solution.py:12
  257.3 7.2 %collective-permute-start.14 = (bf16[48]{0:T(256)(128)(2,1)S(1)}, bf16[48]{0:T(256)(128)(2,1)S(1)}, u32[]{:S(2)}, u32[]{:S(2)}) collective-permute-start(bf16[48]{0:T(256)(128)(2,1)S(1)} %copy-done.4), channel_id=1, source_target_pairs={{0,256},{16,272},{32,288},{48,304},{64,320},{80,336},{96,352},{112... | collective-permute-start | bytes 296 | tf_op jit(solution)/shard_map/ppermute | solution.py:12
  262.6 6.3 %collective-permute-start.4 = (s32[48]{0:T(128)S(1)}, s32[48]{0:T(128)S(1)}, u32[]{:S(2)}, u32[]{:S(2)}) collective-permute-start(s32[48]{0:T(128)S(1)} %copy-done.5), channel_id=1, source_target_pairs={{0,256},{16,272},{32,288},{48,304},{64,320},{80,336},{96,352},{112... | collective-permute-start | bytes 584 | tf_op jit(solution)/shard_map/ppermute | solution.py:12
  264.6 8.5 %collective-permute-start.15 = (bf16[48]{0:T(256)(128)(2,1)S(1)}, bf16[48]{0:T(256)(128)(2,1)S(1)}, u32[]{:S(2)}, u32[]{:S(2)}) collective-permute-start(bf16[48]{0:T(256)(128)(2,1)S(1)} %collective-permute-done.14), channel_id=1, source_target_pairs={{0,16},{16,0},{32,48},{48,32},{64,80},{80,64},{96,112},{112,96},{1... | collective-permute-start | bytes 296 | tf_op jit(solution)/shard_map/ppermute | solution.py:12
  268.9 6.6 %collective-permute-start.5 = (s32[48]{0:T(128)S(1)}, s32[48]{0:T(128)S(1)}, u32[]{:S(2)}, u32[]{:S(2)}) collective-permute-start(s32[48]{0:T(128)S(1)} %collective-permute-done.4), channel_id=1, source_target_pairs={{0,16},{16,0},{32,48},{48,32},{64,80},{80,64},{96,112},{112,96},{1... | collective-permute-start | bytes 584 | tf_op jit(solution)/shard_map/ppermute | solution.py:12
  271.2 25.1 %collective-permute-start.13 = (bf16[384,1024]{1,0:T(8,128)(2,1)S(1)}, bf16[384,1024]{1,0:T(8,128)(2,1)S(1)}, u32[]{:S(2)}, u32[]{:S(2)}) collective-permute-start(bf16[384,1024]{1,0:T(8,128)(2,1)S(1)} %maximum_select_fusion.2), channel_id=1, source_target_pairs={{0,128},{16,144},{32,160},{48,176},{64,192},{80,208},{96,224},{112... | collective-permute-start | bytes 2359304 | tf_op jit(solution)/shard_map/ppermute | solution.py:12
  273.2 5.9 %collective-permute-start.16 = (bf16[96]{0:T(256)(128)(2,1)S(1)}, bf16[96]{0:T(256)(128)(2,1)S(1)}, u32[]{:S(2)}, u32[]{:S(2)}) collective-permute-start(bf16[96]{0:T(256)(128)(2,1)S(1)} %broadcast_select_fusion.1), channel_id=1, source_target_pairs={{0,32},{16,48},{32,0},{48,16},{64,96},{80,112},{96,64},{112,80},{1... | collective-permute-start | bytes 584 | tf_op jit(solution)/shard_map/ppermute | solution.py:12
  275.7 6.2 %collective-permute-start.6 = (s32[96]{0:T(128)S(1)}, s32[96]{0:T(128)S(1)}, u32[]{:S(2)}, u32[]{:S(2)}) collective-permute-start(s32[96]{0:T(128)S(1)} %broadcast_select_fusion.2), channel_id=1, source_target_pairs={{0,32},{16,48},{32,0},{48,16},{64,96},{80,112},{96,64},{112,80},{1... | collective-permute-start | bytes 1160 | tf_op jit(solution)/shard_map/ppermute | solution.py:12
  279.2 7.4 %collective-permute-start.17 = (bf16[192]{0:T(256)(128)(2,1)S(1)}, bf16[192]{0:T(256)(128)(2,1)S(1)}, u32[]{:S(2)}, u32[]{:S(2)}) collective-permute-start(bf16[192]{0:T(256)(128)(2,1)S(1)} %broadcast_select_fusion.3), channel_id=1, source_target_pairs={{0,64},{16,80},{32,96},{48,112},{64,0},{80,16},{96,32},{112,48},{1... | collective-permute-start | bytes 1160 | tf_op jit(solution)/shard_map/ppermute | solution.py:12
  282.0 8.7 %collective-permute-start.7 = (s32[192]{0:T(256)S(1)}, s32[192]{0:T(256)S(1)}, u32[]{:S(2)}, u32[]{:S(2)}) collective-permute-start(s32[192]{0:T(256)S(1)} %add_select_fusion.1), channel_id=1, source_target_pairs={{0,64},{16,80},{32,96},{48,112},{64,0},{80,16},{96,32},{112,48},{1... | collective-permute-start | bytes 2312 | tf_op jit(solution)/shard_map/ppermute | solution.py:12
  286.7 6.3 %collective-permute-start.18 = (bf16[384]{0:T(512)(128)(2,1)S(1)}, bf16[384]{0:T(512)(128)(2,1)S(1)}, u32[]{:S(2)}, u32[]{:S(2)}) collective-permute-start(bf16[384]{0:T(512)(128)(2,1)S(1)} %maximum_select_fusion.6), channel_id=1, source_target_pairs={{0,128},{16,144},{32,160},{48,176},{64,192},{80,208},{96,224},{112... | collective-permute-start | bytes 2312 | tf_op jit(solution)/shard_map/ppermute | solution.py:12
  290.7 5.5 %collective-permute-start.8 = (s32[384]{0:T(512)S(1)}, s32[384]{0:T(512)S(1)}, u32[]{:S(2)}, u32[]{:S(2)}) collective-permute-start(s32[384]{0:T(512)S(1)} %add_select_fusion), channel_id=1, source_target_pairs={{0,128},{16,144},{32,160},{48,176},{64,192},{80,208},{96,224},{112... | collective-permute-start | bytes 4616 | tf_op jit(solution)/shard_map/ppermute | solution.py:12
  305.7 4.5 copy-start.2
  310.2 209.8 %copy-start.1 = (bf16[768,256]{1,0:T(8,128)(2,1)S(1)}, bf16[768,256]{1,0:T(8,128)(2,1)}, u32[]{:S(2)}) copy-start(bf16[768,256]{1,0:T(8,128)(2,1)} %param.13) | copy-start | bytes 1179652
  521.9 14.9 %collective-permute-start.19 = (bf16[768,256]{1,0:T(8,128)(2,1)}, bf16[768,256]{1,0:T(8,128)(2,1)S(1)}, u32[]{:S(2)}, u32[]{:S(2)}) collective-permute-start(bf16[768,256]{1,0:T(8,128)(2,1)} %add_convert_fusion), channel_id=1, source_target_pairs={{256,0},{272,16},{288,32},{304,48},{320,64},{336,80},{352,96},{368... | collective-permute-start | bytes 1179656 | tf_op jit(solution)/shard_map/ppermute | solution.py:26
Sparse Core Ops, SparseCore 0:
  311.8 208.0 all-reduce.1
where the time goes:
time: 545 us; the launch traced here: 544 us
  waiting for transfers between devices  430 us (79%)
  starting transfers between devices  61.2 us (11%)
  other arithmetic  21.3 us (4%)
  between operations  14.4 us (3%)
  matrix products  13.2 us (2%)
    ppermute x19, waiting for transfers between devices, partner(): return lax.ppermute(value, axis, pairs)  221 us
    psum x1, waiting for transfers between devices, shards(): summed = lax.psum(partial_grad, 'tensor')  208 us
    ppermute x19, starting transfers between devices, partner(): return lax.ppermute(value, axis, pairs)  59.7 us
  transfers between devices with their start and end apart: 21, of which 11 were waited for; matrix products, arithmetic and copies ran while one was open for 4% of the time, Pallas kernels for 0%

commit v1 on v0

v1 whole, which is shorter than its diff:
```python
import functools
import math

import jax
import jax.numpy as jnp
from jax import lax
from jax.experimental import pallas as pl
from jax.experimental.pallas import tpu as pltpu
from jax.sharding import Mesh, PartitionSpec as P

SHAPE = (2, 2, 4, 2, 4, 4)
NAMES = ("half", "zb", "y", "core", "zh", "x")
SECTION = ("half", "zb", "y", "core")
TENSOR = ("zh", "x")
CHIPS = ("zb", "y")
F32 = jnp.float32
BF16 = jnp.bfloat16
TOK = 768
HALF = 384
OWN = 48
PACK = 64
SMEM = pl.BlockSpec(memory_space=pltpu.SMEM)
VMEM = pl.BlockSpec(memory_space=pltpu.VMEM)
PARAMS = pltpu.CompilerParams(vmem_limit_bytes=48 * 1024 * 1024)


def call(kernel, shape, dtype, ins, scratch=(), flops=0, nbytes=0):
    return pl.pallas_call(
        kernel,
        out_shape=jax.ShapeDtypeStruct(shape, dtype),
        in_specs=[SMEM] + [VMEM] * (len(ins) - 1),
        out_specs=VMEM,
        scratch_shapes=list(scratch),
        compiler_params=PARAMS,
        cost_estimate=pl.CostEstimate(flops=flops, bytes_accessed=nbytes, transcendentals=0),
    )(*ins)


def swap(value, axis):
    return lax.ppermute(value, axis, [(0, 1), (1, 0)])


def dot(a, b, ca, cb):
    return lax.dot_general(a, b, (((ca,), (cb,)), ((), ())), preferred_element_type=F32)


def front(pos, g, g_far, v, v_far, pack, pack_far, out):
    core = pos[0]
    mine = g[pl.ds(pl.multiple_of(core * HALF, HALF), HALF), :]
    far = g_far[...]
    for j in range(4):
        cols = slice(256 * j, 256 * j + 256)
        part = dot(mine, v[:, cols], 1, 0) + dot(far, v_far[:, cols], 1, 0)
        part = part.astype(BF16)
        out[2 * j, :HALF, :] = part[:, :128]
        out[2 * j + 1, :HALF, :] = part[:, 128:]
    near_at = pl.multiple_of(HALF + PACK * core, PACK)
    far_at = pl.multiple_of(HALF + PACK * (1 - core), PACK)
    for i in range(8):
        cols = slice(128 * i, 128 * i + 128)
        out[i, pl.ds(near_at, PACK), :] = pack[:, cols]
        out[i, pl.ds(far_at, PACK), :] = pack_far[:, cols]


def rows_of(near, far):
    lane = lax.broadcasted_iota(jnp.int32, (1, 128), 1)
    low = lane < PACK

    def line(k):
        return jnp.where(low, near[k : k + 1, :].astype(F32), far[k : k + 1, :].astype(F32))

    token = (line(0) * 32.0 + line(1)).astype(jnp.int32)
    valid = (lane % PACK) < OWN
    return jnp.where(valid, token, -1), line(2)


def slope(pos, recv, out):
    core = pos[0]
    act = jnp.zeros((HALF, 128), F32)
    hidden = jnp.zeros((HALF, 128), F32)
    scale = jnp.zeros((HALF, 128), F32)
    token = lax.broadcasted_iota(jnp.int32, (HALF, 128), 0) + core * HALF
    for i in range(8):
        act = act + recv[i, :HALF, :].astype(F32)
        near = recv[i, HALF + OWN : HALF + PACK, :]
        far = recv[i, HALF + PACK + OWN : HALF + 2 * PACK, :]
        rows, scales = rows_of(near, far)
        hit = token == rows
        one = jnp.where(hit, 1.0, 0.0).astype(BF16)
        hidden = hidden + dot(one, recv[i, HALF:, :], 1, 0)
        scale = scale + jnp.where(hit, scales, 0.0)
    hidden = hidden * jnp.sum(scale, axis=1, keepdims=True)
    density = jnp.exp(-0.5 * hidden * hidden) * 0.3989422804014327
    cumulative = 0.5 * (1.0 + lax.erf(hidden * 0.7071067811865476))
    grad = (act * (cumulative + hidden * density)).astype(BF16)
    for i in range(8):
        out[i] = grad


def input_part(pos, hg, u, u_far, out):
    core = pos[0]
    rows = jnp.concatenate([hg[i] for i in range(8)], axis=1)
    near_at = pl.multiple_of(256 * core, 256)
    far_at = pl.multiple_of(256 * (1 - core), 256)
    out[:, pl.ds(near_at, 256)] = dot(rows, u[...], 1, 1).astype(BF16)
    out[:, pl.ds(far_at, 256)] = dot(rows, u_far[...], 1, 1).astype(BF16)


def add_x(pos, recv, g, g_far, out):
    core, x, first = pos[0], pos[1], pos[2] == 0
    total = recv[0].astype(F32)
    for i in range(1, 4):
        total = total + recv[i].astype(F32)
    near_at = pl.multiple_of(256 * core, 256)
    far_at = pl.multiple_of(256 * (1 - core), 256)
    mine = g[pl.ds(pl.multiple_of(core * HALF + x * 96, 96), 96), :].astype(F32)
    far = g_far[pl.ds(pl.multiple_of(x * 96, 96), 96), :].astype(F32)
    out[...] = total.astype(BF16)

    @pl.when(first)
    def _():
        both = jnp.where(core == 0, jnp.concatenate([mine, far], 1), jnp.concatenate([far, mine], 1))
        out[...] = (total + both).astype(BF16)


def add_z(pos, a, b, c, d, out):
    total = a[...].astype(F32) + b[...].astype(F32) + c[...].astype(F32) + d[...].astype(F32)
    total = total.astype(BF16)
    for i in range(4):
        out[i] = total[:, :256]
        out[4 + i] = total[:, 256:]


def down(pos, recv, g, act, out, held):
    token = lax.broadcasted_iota(jnp.int32, (TOK, 128), 0)
    for i in range(8):
        near = recv[i, HALF + OWN : HALF + PACK, :]
        far = recv[i, HALF + PACK + OWN : HALF + 2 * PACK, :]
        rows, _ = rows_of(near, far)
        one = jnp.where(token == rows, 1.0, 0.0).astype(BF16)
        moved = dot(one, g[...], 0, 0).astype(BF16)
        held[96 * i : 96 * i + OWN, :] = moved[:OWN]
        held[96 * i + OWN : 96 * i + 96, :] = moved[PACK : PACK + OWN]
    turned = held[...].T
    for j in range(4):
        cols = slice(256 * j, 256 * j + 256)
        out[:, cols] = dot(turned, act[:, cols], 1, 0).astype(BF16)


def up(pos, x, hg, hg_far, out):
    core = pos[0]
    mine = x[pl.ds(pl.multiple_of(core * HALF, HALF), HALF), :].T
    far = x[pl.ds(pl.multiple_of((1 - core) * HALF, HALF), HALF), :].T
    for j in range(4):
        near_hg = jnp.concatenate([hg[2 * j], hg[2 * j + 1]], axis=1)
        far_hg = jnp.concatenate([hg_far[2 * j], hg_far[2 * j + 1]], axis=1)
        part = dot(mine, near_hg, 1, 0) + dot(far, far_hg, 1, 0)
        out[:, 256 * j : 256 * j + 256] = part.astype(BF16)


def shards(layer_input, w_up, w_down, parked_codes, parked_scales, parked_rows, incoming):
    core = lax.axis_index("core")
    x = lax.axis_index("x")
    zh = lax.axis_index("zh")
    pos = jnp.stack([core, x, zh]).astype(jnp.int32)

    gap = PACK - OWN
    lines = jnp.stack(
        [
            (parked_rows >> 5).astype(BF16),
            (parked_rows & 31).astype(BF16),
            parked_scales,
        ]
    )
    lines = jnp.tile(jnp.pad(lines, ((0, gap - 3), (0, gap))), (1, 16))
    pack = swap(jnp.concatenate([parked_codes, lines], axis=0), "half")
    pack_far = swap(pack, "core")
    g_far = swap(lax.dynamic_slice(incoming, ((1 - core) * HALF, 0), (HALF, 256)), "core")
    v_far = swap(w_down, "core")
    u_far = swap(w_up, "core")

    scales = pack[OWN + 2, :OWN].astype(F32)
    values = pack[:OWN].astype(F32) * scales[:, None]
    act = jax.nn.gelu(values, approximate=False).astype(BF16)
    act = lax.all_gather(act, ("zb", "y", "core"), tiled=True)

    partial_act = call(
        front, (8, HALF + 2 * PACK, 128), BF16, (pos, incoming, g_far, w_down, v_far, pack, pack_far),
        flops=2 * HALF * 512 * 1024, nbytes=4 << 20,
    )
    recv = lax.all_to_all(partial_act, CHIPS, 0, 0, tiled=True)
    hg = call(slope, (8, HALF, 128), BF16, (pos, recv), flops=1 << 27, nbytes=2 << 20)
    hg = lax.all_to_all(hg, CHIPS, 0, 0, tiled=True)
    hg_far = swap(hg, "core")

    part = call(
        input_part, (HALF, 512), BF16, (pos, hg, w_up, u_far),
        flops=2 * HALF * 512 * 1024, nbytes=3 << 20,
    )
    part = lax.all_to_all(part.reshape(4, 96, 512), "x", 0, 0, tiled=True)
    summed = call(add_x, (96, 512), BF16, (pos, part, incoming, g_far), nbytes=1 << 20)
    got = [
        lax.ppermute(summed, ("half", "zh"), [(4 + i, (i + k) % 4) for i in range(4)])
        for k in range(4)
    ]
    whole = call(add_z, (8, 96, 256), BF16, (pos, *got), nbytes=1 << 20)
    passed = lax.all_to_all(whole, ("core", "x"), 0, 0, tiled=True).reshape(TOK, 256)

    grad_down = call(
        down, (256, 1024), BF16, (pos, recv, incoming, act),
        scratch=(pltpu.VMEM((TOK, 256), BF16),), flops=2 * TOK * 256 * 1792, nbytes=4 << 20,
    )
    grad_up = call(
        up, (256, 1024), BF16, (pos, layer_input, hg, hg_far),
        flops=2 * TOK * 256 * 1024, nbytes=3 << 20,
    )
    return grad_up, grad_down, passed


def solution(mesh):
    fine = Mesh(mesh.devices.reshape(SHAPE), NAMES)
    return jax.shard_map(
        shards,
        mesh=fine,
        in_specs=(
            P(None, SECTION),
            P(SECTION, TENSOR),
            P(SECTION, TENSOR),
            P(SECTION, TENSOR),
            P(SECTION),
            P(SECTION),
            P(None, SECTION),
        ),
        out_specs=(P(SECTION, TENSOR), P(SECTION, TENSOR), P(None, SECTION)),
        check_vma=False,
    )
```

time: 545 us -> 140 us (0.26)
  the two profiles are of different devices: /device:TPU:24 before, /device:TPU:1 now
where the time goes in v1:
time: 140 us; the launch traced here: 139 us
  starting transfers between devices  38.7 us (28%)
  waiting for transfers between devices  37.2 us (27%)
  blocking collectives  28.2 us (20%)
  between operations  14.2 us (10%)
  Pallas kernels  11.4 us (8%)
  local copies, waits for them, and re-layouts  6.29 us (4%)
  other arithmetic  3.46 us (2%)
    ppermute x4, waiting for transfers between devices, shards(): lax.ppermute(summed, ('half', 'zh'), [(4 + i, (i + k) % 4) for i in range...  24.6 us
    ppermute x6, starting transfers between devices, swap(): return lax.ppermute(value, axis, [(0, 1), (1, 0)])  24.5 us
    all_to_all x1, blocking collectives, shards(): recv = lax.all_to_all(partial_act, CHIPS, 0, 0, tiled=True)  16.8 us
    all_to_all x1, blocking collectives, shards(): part = lax.all_to_all(part.reshape(4, 96, 512), 'x', 0, 0, tiled=True)  11.4 us
    pallas_call x7, Pallas kernels, call(): pl.pallas_call(kernel, out_shape=jax.ShapeDtypeStruct(shape, dtype), in_s...  11.4 us
    unnamed x11, local copies, waits for them, and re-layouts  5.22 us
    ppermute x4, starting transfers between devices, shards(): lax.ppermute(summed, ('half', 'zh'), [(4 + i, (i + k) % 4) for i in range...  5.17 us
    all_to_all x1, starting transfers between devices, shards(): lax.all_to_all(whole, ('core', 'x'), 0, 0, tiled=True).reshape(TOK, 256)  4.87 us
  transfers between devices with their start and end apart: 13, of which 8 were waited for; matrix products, arithmetic and copies ran while one was open for 3% of the time, Pallas kernels for 4%

profile of v1, /device:TPU:1, one launch (start us, length us, event | category | flops | bytes accessed | tf_op | source)
XLA Modules:
  0.0 139.4 jit_solution(9059397480276001932)
XLA Ops:
  7.2 8.8 %collective-permute-start.1 = (bf16[256,1024]{1,0:T(8,128)(2,1)}, bf16[256,1024]{1,0:T(8,128)(2,1)S(1)}, u32[]{:S(2)}, u32[]{:S(2)}) collective-permute-start(bf16[256,1024]{1,0:T(8,128)(2,1)} %v.1), channel_id=1, source_target_pairs={{0,16},{16,0},{1,17},{17,1},{2,18},{18,2},{3,19},{19,3},{4,20},{20... | collective-permute-start | bytes 1572872 | tf_op jit(solution)/shard_map/ppermute | solution.py:40
  16.0 0.7 convert_bitcast_fusion.1
  16.6 0.7 fusion.21
  17.3 0.1 tile.10
  17.4 0.9 pad_maximum_fusion
  18.3 1.9 %collective-permute-start.2 = (bf16[64,1024]{1,0:T(8,128)(2,1)S(1)}, bf16[64,1024]{1,0:T(8,128)(2,1)S(1)}, u32[]{:S(2)}, u32[]{:S(2)}) collective-permute-start(bf16[64,1024]{1,0:T(8,128)(2,1)S(1)} %pad_maximum_fusion), channel_id=1, source_target_pairs={{0,256},{256,0},{1,257},{257,1},{2,258},{258,2},{3,259},{259,3},{4... | collective-permute-start | bytes 393224 | tf_op jit(solution)/shard_map/ppermute | solution.py:40
  20.3 0.9 constant_dynamic-slice_fusion
  21.2 1.9 %collective-permute-start = (bf16[384,256]{1,0:T(8,128)(2,1)S(1)}, bf16[384,256]{1,0:T(8,128)(2,1)S(1)}, u32[]{:S(2)}, u32[]{:S(2)}) collective-permute-start(bf16[384,256]{1,0:T(8,128)(2,1)S(1)} %constant_dynamic-slice_fusion), channel_id=1, source_target_pairs={{0,16},{16,0},{1,17},{17,1},{2,18},{18,2},{3,19},{19,3},{4,20},{20... | collective-permute-start | bytes 589832 | tf_op jit(solution)/shard_map/ppermute | solution.py:40
  23.1 3.1 %collective-permute-done.2.pack = bf16[64,1024]{1,0:T(8,128)(2,1)S(1)} collective-permute-done((bf16[64,1024]{1,0:T(8,128)(2,1)S(1)}, bf16[64,1024]{1,0:T(8,128)(2,1)S(1)}, u32[]{:S(2)}, u32[]{:S(2)}) %collective-permute-start.2) | collective-permute-done | bytes 131104 | tf_op jit(solution)/shard_map/ppermute | solution.py:40
  26.2 2.7 %collective-permute-start.3 = (bf16[64,1024]{1,0:T(8,128)(2,1)S(1)}, bf16[64,1024]{1,0:T(8,128)(2,1)S(1)}, u32[]{:S(2)}, u32[]{:S(2)}) collective-permute-start(bf16[64,1024]{1,0:T(8,128)(2,1)S(1)} %collective-permute-done.2.pack), channel_id=1, source_target_pairs={{0,16},{16,0},{1,17},{17,1},{2,18},{18,2},{3,19},{19,3},{4,20},{20... | collective-permute-start | bytes 393224 | tf_op jit(solution)/shard_map/ppermute | solution.py:40
  28.9 0.1 pad_add_fusion.pos
  29.0 0.0 collective-permute-done.g_far
  29.0 0.9 collective-permute-done.3.pack_far
  29.9 0.0 collective-permute-done.1.v_far
  29.9 0.0 copy-start
  29.9 1.0 copy-done
  30.9 0.0 copy-start.3
  30.9 1.0 copy-done.3
  31.9 1.2 shard_map.94
  33.1 16.8 %all_to_all.20.recv = bf16[8,512,128]{2,1,0:T(8,128)(2,1)S(1)} all-to-all(bf16[8,512,128]{2,1,0:T(8,128)(2,1)S(1)} %shard_map.94), channel_id=1, replica_groups=mesh['half'=2,'zb'=2,'y'=4,'core'=2,'zh'=4,'x'=4] {'zb','y'}, dimensions={0} | all-to-all | bytes 2097152 | tf_op jit(solution)/shard_map/all_to_all | solution.py:191
  49.9 1.9 %shard_map.95 = bf16[8,384,128]{2,1,0:T(8,128)(2,1)} custom-call(s32[3]{0:T(128)S(1)} %pad_add_fusion.pos, bf16[8,512,128]{2,1,0:T(8,128)(2,1)S(1)} %all_to_all.20.recv), custom_call_target="tpu_custom_call" | custom-call | flops 134217728 | bytes 2097152 | tf_op jit(solution)/shard_map/pallas_call | solution.py:28
  51.8 4.1 %all-to-all-start.1 = ((bf16[8,384,128]{2,1,0:T(8,128)(2,1)}), bf16[8,384,128]{2,1,0:T(8,128)(2,1)S(1)}, u32[]{:S(2)}, u32[]{:S(2)}) async-start(bf16[8,384,128]{2,1,0:T(8,128)(2,1)} %shard_map.95), calls=%async_computation.1 | async-start | bytes 1572864 | tf_op jit(solution)/shard_map/all_to_all | solution.py:193
  55.9 0.0 all-gather.2.cloned.1.call-start
  56.0 1.1 fusion.2
  57.1 0.0 copy-start.1
  57.1 0.0 all-gather.2.cloned.1.call-update
  57.1 3.7 %collective-permute-start.5 = (bf16[256,1024]{1,0:T(8,128)(2,1)}, bf16[256,1024]{1,0:T(8,128)(2,1)}, u32[]{:S(2)}, u32[]{:S(2)}) collective-permute-start(bf16[256,1024]{1,0:T(8,128)(2,1)} %u.1), channel_id=1, source_target_pairs={{0,16},{16,0},{1,17},{17,1},{2,18},{18,2},{3,19},{19,3},{4,20},{20... | collective-permute-start | bytes 1572872 | tf_op jit(solution)/shard_map/ppermute | solution.py:40
  60.8 4.4 %all-to-all-done.1.hg = bf16[8,384,128]{2,1,0:T(8,128)(2,1)S(1)} async-done(((bf16[8,384,128]{2,1,0:T(8,128)(2,1)}), bf16[8,384,128]{2,1,0:T(8,128)(2,1)S(1)}, u32[]{:S(2)}, u32[]{:S(2)}) %all-to-all-start.1) | async-done | bytes 786464 | tf_op jit(solution)/shard_map/all_to_all | solution.py:193
  65.3 5.5 %collective-permute-start.4 = (bf16[8,384,128]{2,1,0:T(8,128)(2,1)S(1)}, bf16[8,384,128]{2,1,0:T(8,128)(2,1)S(1)}, u32[]{:S(2)}, u32[]{:S(2)}) collective-permute-start(bf16[8,384,128]{2,1,0:T(8,128)(2,1)S(1)} %all-to-all-done.1.hg), channel_id=1, source_target_pairs={{0,16},{16,0},{1,17},{17,1},{2,18},{18,2},{3,19},{19,3},{4,20},{20... | collective-permute-start | bytes 2359304 | tf_op jit(solution)/shard_map/ppermute | solution.py:40
  70.8 0.0 collective-permute-done.5.u_far
  70.8 1.8 %shard_map.98 = bf16[384,512]{1,0:T(8,128)(2,1)S(1)} custom-call(s32[3]{0:T(128)S(1)} %pad_add_fusion.pos, bf16[8,384,128]{2,1,0:T(8,128)(2,1)S(1)} %all-to-all-done.1.hg, bf16[256,1024]{1,0:T(8,128)(2,1)} %u.1, bf16[256,1024]{1,0:T(8,128)(2,1)} %collective-permute-done.5.u_far), custom_call_target="tpu_custom_call" | custom-call | flops 402653184 | bytes 3145728 | tf_op jit(solution)/shard_map/pallas_call | solution.py:28
  72.6 11.4 %all_to_all.21.recv = bf16[4,96,512]{2,1,0:T(8,128)(2,1)S(1)} all-to-all(bf16[4,96,512]{2,1,0:T(8,128)(2,1)S(1)} %bitcast.15), channel_id=1, replica_groups=mesh['half'=2,'zb'=2,'y'=4,'core'=2,'zh'=4,'x'=4] {'x'}, dimensions={0} | all-to-all | bytes 786432 | tf_op jit(solution)/shard_map/all_to_all | solution.py:200
  84.0 0.0 copy-done.1
  84.0 0.6 shard_map.99
  84.6 1.3 collective-permute-start.6
  85.9 1.3 collective-permute-start.7
  87.2 1.3 collective-permute-start.8
  88.5 1.3 collective-permute-start.9
  89.8 2.2 %collective-permute-done.6.a = bf16[96,512]{1,0:T(8,128)(2,1)S(1)} collective-permute-done((bf16[96,512]{1,0:T(8,128)(2,1)S(1)}, bf16[96,512]{1,0:T(8,128)(2,1)S(1)}, u32[]{:S(2)}, u32[]{:S(2)}) %collective-permute-start.6) | collective-permute-done | bytes 98336 | tf_op jit(solution)/shard_map/ppermute | solution.py:203
  92.0 8.9 %collective-permute-done.7.b = bf16[96,512]{1,0:T(8,128)(2,1)S(1)} collective-permute-done((bf16[96,512]{1,0:T(8,128)(2,1)S(1)}, bf16[96,512]{1,0:T(8,128)(2,1)S(1)}, u32[]{:S(2)}, u32[]{:S(2)}) %collective-permute-start.7) | collective-permute-done | bytes 98336 | tf_op jit(solution)/shard_map/ppermute | solution.py:203
  100.9 5.9 %collective-permute-done.8.c = bf16[96,512]{1,0:T(8,128)(2,1)S(1)} collective-permute-done((bf16[96,512]{1,0:T(8,128)(2,1)S(1)}, bf16[96,512]{1,0:T(8,128)(2,1)S(1)}, u32[]{:S(2)}, u32[]{:S(2)}) %collective-permute-start.8) | collective-permute-done | bytes 98336 | tf_op jit(solution)/shard_map/ppermute | solution.py:203
  106.8 7.6 %collective-permute-done.9.d = bf16[96,512]{1,0:T(8,128)(2,1)S(1)} collective-permute-done((bf16[96,512]{1,0:T(8,128)(2,1)S(1)}, bf16[96,512]{1,0:T(8,128)(2,1)S(1)}, u32[]{:S(2)}, u32[]{:S(2)}) %collective-permute-start.9) | collective-permute-done | bytes 98336 | tf_op jit(solution)/shard_map/ppermute | solution.py:203
  114.4 1.3 shard_map.100
  115.7 4.9 %all-to-all-start.3 = ((bf16[8,96,256]{2,1,0:T(8,128)(2,1)}), bf16[8,96,256]{2,1,0:T(8,128)(2,1)}, u32[]{:S(2)}, u32[]{:S(2)}) async-start(bf16[8,96,256]{2,1,0:T(8,128)(2,1)} %shard_map.100), calls=%async_computation.3 | async-start | bytes 786432 | tf_op jit(solution)/shard_map/all_to_all | solution.py:207
  120.6 0.0 all-gather.2.cloned.1.call-done.act
  120.6 0.0 copy-start.2
  120.6 1.4 %copy-done.2 = bf16[768,1024]{1,0:T(8,128)(2,1)S(1)} copy-done((bf16[768,1024]{1,0:T(8,128)(2,1)S(1)}, bf16[768,1024]{1,0:T(8,128)(2,1)}, u32[]{:S(2)}) %copy-start.2) | copy-done | bytes 1572888
  122.0 0.0 copy-start.4
  122.0 2.4 %shard_map.97 = bf16[256,1024]{1,0:T(8,128)(2,1)} custom-call(s32[3]{0:T(128)S(1)} %pad_add_fusion.pos, bf16[8,512,128]{2,1,0:T(8,128)(2,1)S(1)} %all_to_all.20.recv, bf16[768,256]{1,0:T(8,128)(2,1)S(1)} %copy-done.1, bf16[768,1024]{1,0:T(8,128)(2,1)S(1)} %copy-done.2), custom_call_target="tpu_custom_call" | custom-call | flops 704643072 | bytes 4194304 | tf_op jit(solution)/shard_map/pallas_call | solution.py:28
  124.5 4.2 %all-to-all-done.3 = bf16[8,96,256]{2,1,0:T(8,128)(2,1)} async-done(((bf16[8,96,256]{2,1,0:T(8,128)(2,1)}), bf16[8,96,256]{2,1,0:T(8,128)(2,1)}, u32[]{:S(2)}, u32[]{:S(2)}) %all-to-all-start.3) | async-done | bytes 393248 | tf_op jit(solution)/shard_map/all_to_all | solution.py:207
  128.7 0.0 collective-permute-done.4.hg_far
  128.7 0.0 copy-done.4
  128.7 2.1 %shard_map.96 = bf16[256,1024]{1,0:T(8,128)(2,1)} custom-call(s32[3]{0:T(128)S(1)} %pad_add_fusion.pos, bf16[768,256]{1,0:T(8,128)(2,1)S(1)} %copy-done.4, bf16[8,384,128]{2,1,0:T(8,128)(2,1)S(1)} %all-to-all-done.1.hg, bf16[8,384,128]{2,1,0:T(8,128)(2,1)S(1)} %collective-permute-done.4.hg_far), custom_call_target="tpu_custom_call" | custom-call | flops 402653184 | bytes 3145728 | tf_op jit(solution)/shard_map/pallas_call | solution.py:28
  130.8 1.8 %copy.11 = bf16[768,256]{1,0:T(8,128)(2,1)} copy(bf16[768,256]{1,0:T(8,128)(2,1)} %bitcast.8) | data formatting | bytes 786432
  (2 shorter events, 0.0 us)
Async XLA Ops:
  7.2 22.7 %collective-permute-start.1 = (bf16[256,1024]{1,0:T(8,128)(2,1)}, bf16[256,1024]{1,0:T(8,128)(2,1)S(1)}, u32[]{:S(2)}, u32[]{:S(2)}) collective-permute-start(bf16[256,1024]{1,0:T(8,128)(2,1)} %v.1), channel_id=1, source_target_pairs={{0,16},{16,0},{1,17},{17,1},{2,18},{18,2},{3,19},{19,3},{4,20},{20... | collective-permute-start | bytes 1572872 | tf_op jit(solution)/shard_map/ppermute | solution.py:40
  18.3 7.9 %collective-permute-start.2 = (bf16[64,1024]{1,0:T(8,128)(2,1)S(1)}, bf16[64,1024]{1,0:T(8,128)(2,1)S(1)}, u32[]{:S(2)}, u32[]{:S(2)}) collective-permute-start(bf16[64,1024]{1,0:T(8,128)(2,1)S(1)} %pad_maximum_fusion), channel_id=1, source_target_pairs={{0,256},{256,0},{1,257},{257,1},{2,258},{258,2},{3,259},{259,3},{4... | collective-permute-start | bytes 393224 | tf_op jit(solution)/shard_map/ppermute | solution.py:40
  21.2 7.8 %collective-permute-start = (bf16[384,256]{1,0:T(8,128)(2,1)S(1)}, bf16[384,256]{1,0:T(8,128)(2,1)S(1)}, u32[]{:S(2)}, u32[]{:S(2)}) collective-permute-start(bf16[384,256]{1,0:T(8,128)(2,1)S(1)} %constant_dynamic-slice_fusion), channel_id=1, source_target_pairs={{0,16},{16,0},{1,17},{17,1},{2,18},{18,2},{3,19},{19,3},{4,20},{20... | collective-permute-start | bytes 589832 | tf_op jit(solution)/shard_map/ppermute | solution.py:40
  26.2 3.7 %collective-permute-start.3 = (bf16[64,1024]{1,0:T(8,128)(2,1)S(1)}, bf16[64,1024]{1,0:T(8,128)(2,1)S(1)}, u32[]{:S(2)}, u32[]{:S(2)}) collective-permute-start(bf16[64,1024]{1,0:T(8,128)(2,1)S(1)} %collective-permute-done.2.pack), channel_id=1, source_target_pairs={{0,16},{16,0},{1,17},{17,1},{2,18},{18,2},{3,19},{19,3},{4,20},{20... | collective-permute-start | bytes 393224 | tf_op jit(solution)/shard_map/ppermute | solution.py:40
  29.9 1.0 copy-start
  30.9 1.0 copy-start.3
  51.8 13.4 %all-to-all-start.1 = ((bf16[8,384,128]{2,1,0:T(8,128)(2,1)}), bf16[8,384,128]{2,1,0:T(8,128)(2,1)S(1)}, u32[]{:S(2)}, u32[]{:S(2)}) async-start(bf16[8,384,128]{2,1,0:T(8,128)(2,1)} %shard_map.95), calls=%async_computation.1 | async-start | bytes 1572864 | tf_op jit(solution)/shard_map/all_to_all | solution.py:193
  55.9 64.7 %all-gather.2.cloned.1.call-start = ((), (), s32[]{:S(2)}) async-start(), calls=%async_computation.4 | async-start | bytes 1671168 | tf_op jit(solution)/shard_map/all_gather | solution.py:185
  57.1 26.9 %copy-start.1 = (bf16[768,256]{1,0:T(8,128)(2,1)S(1)}, bf16[768,256]{1,0:T(8,128)(2,1)}, u32[]{:S(2)}) copy-start(bf16[768,256]{1,0:T(8,128)(2,1)} %g.5) | copy-start | bytes 1179652
  57.1 13.6 %collective-permute-start.5 = (bf16[256,1024]{1,0:T(8,128)(2,1)}, bf16[256,1024]{1,0:T(8,128)(2,1)}, u32[]{:S(2)}, u32[]{:S(2)}) collective-permute-start(bf16[256,1024]{1,0:T(8,128)(2,1)} %u.1), channel_id=1, source_target_pairs={{0,16},{16,0},{1,17},{17,1},{2,18},{18,2},{3,19},{19,3},{4,20},{20... | collective-permute-start | bytes 1572872 | tf_op jit(solution)/shard_map/ppermute | solution.py:40
  65.3 63.4 %collective-permute-start.4 = (bf16[8,384,128]{2,1,0:T(8,128)(2,1)S(1)}, bf16[8,384,128]{2,1,0:T(8,128)(2,1)S(1)}, u32[]{:S(2)}, u32[]{:S(2)}) collective-permute-start(bf16[8,384,128]{2,1,0:T(8,128)(2,1)S(1)} %all-to-all-done.1.hg), channel_id=1, source_target_pairs={{0,16},{16,0},{1,17},{17,1},{2,18},{18,2},{3,19},{19,3},{4,20},{20... | collective-permute-start | bytes 2359304 | tf_op jit(solution)/shard_map/ppermute | solution.py:40
  84.6 7.4 %collective-permute-start.6 = (bf16[96,512]{1,0:T(8,128)(2,1)S(1)}, bf16[96,512]{1,0:T(8,128)(2,1)S(1)}, u32[]{:S(2)}, u32[]{:S(2)}) collective-permute-start(bf16[96,512]{1,0:T(8,128)(2,1)S(1)} %shard_map.99), channel_id=1, source_target_pairs={{256,0},{260,4},{264,8},{268,12},{257,1},{261,5},{265,9},{269,13},... | collective-permute-start | bytes 294920 | tf_op jit(solution)/shard_map/ppermute | solution.py:203
  85.9 15.0 %collective-permute-start.7 = (bf16[96,512]{1,0:T(8,128)(2,1)S(1)}, bf16[96,512]{1,0:T(8,128)(2,1)S(1)}, u32[]{:S(2)}, u32[]{:S(2)}) collective-permute-start(bf16[96,512]{1,0:T(8,128)(2,1)S(1)} %shard_map.99), channel_id=1, source_target_pairs={{256,4},{260,8},{264,12},{268,0},{257,5},{261,9},{265,13},{269,1},... | collective-permute-start | bytes 294920 | tf_op jit(solution)/shard_map/ppermute | solution.py:203
  87.2 19.6 %collective-permute-start.8 = (bf16[96,512]{1,0:T(8,128)(2,1)S(1)}, bf16[96,512]{1,0:T(8,128)(2,1)S(1)}, u32[]{:S(2)}, u32[]{:S(2)}) collective-permute-start(bf16[96,512]{1,0:T(8,128)(2,1)S(1)} %shard_map.99), channel_id=1, source_target_pairs={{256,8},{260,12},{264,0},{268,4},{257,9},{261,13},{265,1},{269,5},... | collective-permute-start | bytes 294920 | tf_op jit(solution)/shard_map/ppermute | solution.py:203
  88.5 25.9 %collective-permute-start.9 = (bf16[96,512]{1,0:T(8,128)(2,1)S(1)}, bf16[96,512]{1,0:T(8,128)(2,1)S(1)}, u32[]{:S(2)}, u32[]{:S(2)}) collective-permute-start(bf16[96,512]{1,0:T(8,128)(2,1)S(1)} %shard_map.99), channel_id=1, source_target_pairs={{256,12},{260,0},{264,4},{268,8},{257,13},{261,1},{265,5},{269,9},... | collective-permute-start | bytes 294920 | tf_op jit(solution)/shard_map/ppermute | solution.py:203
  115.7 12.9 %all-to-all-start.3 = ((bf16[8,96,256]{2,1,0:T(8,128)(2,1)}), bf16[8,96,256]{2,1,0:T(8,128)(2,1)}, u32[]{:S(2)}, u32[]{:S(2)}) async-start(bf16[8,96,256]{2,1,0:T(8,128)(2,1)} %shard_map.100), calls=%async_computation.3 | async-start | bytes 786432 | tf_op jit(solution)/shard_map/all_to_all | solution.py:207
  120.6 1.4 %copy-start.2 = (bf16[768,1024]{1,0:T(8,128)(2,1)S(1)}, bf16[768,1024]{1,0:T(8,128)(2,1)}, u32[]{:S(2)}) copy-start(bf16[768,1024]{1,0:T(8,128)(2,1)} %all-gather.2.cloned.1.call-done.act) | copy-start | bytes 4718596
  122.0 6.7 %copy-start.4 = (bf16[768,256]{1,0:T(8,128)(2,1)S(1)}, bf16[768,256]{1,0:T(8,128)(2,1)}, u32[]{:S(2)}) copy-start(bf16[768,256]{1,0:T(8,128)(2,1)} %x.3) | copy-start | bytes 1179652
Sparse Core Ops, SparseCore 0:
  59.5 46.6 all-gather.1

commit v2 on v1

v2 whole, which is shorter than its diff:
```python
import jax
import jax.numpy as jnp
from jax import lax
from jax.experimental import pallas as pl
from jax.experimental.pallas import tpu as pltpu
from jax.sharding import Mesh, PartitionSpec as P

SHAPE = (2, 2, 4, 2, 4, 4)
NAMES = ("half", "zb", "y", "core", "zh", "x")
SECTION = ("half", "zb", "y", "core")
TENSOR = ("zh", "x")
CHIPS = ("zb", "y")
F32 = jnp.float32
BF16 = jnp.bfloat16
TOK = 768
HALF = 384
OWN = 48
PACK = 64
STACK = 608
VMEM = pl.BlockSpec(memory_space=pltpu.VMEM)
ANY = pl.BlockSpec(memory_space=pl.ANY)
HBM = pl.BlockSpec(memory_space=pltpu.HBM)
DMA = pltpu.SemaphoreType.DMA


def call(kernel, outs, ins, scratch=(), flops=0, nbytes=0, vmem=48, **kwargs):
    many = isinstance(outs, list)
    shapes = [jax.ShapeDtypeStruct(shape, dtype) for shape, dtype in (outs if many else [outs])]
    kwargs.setdefault("in_specs", [VMEM] * len(ins))
    kwargs.setdefault("out_specs", [VMEM] * len(shapes) if many else VMEM)
    return pl.pallas_call(
        kernel,
        out_shape=shapes if many else shapes[0],
        scratch_shapes=list(scratch),
        compiler_params=pltpu.CompilerParams(vmem_limit_bytes=vmem << 20),
        cost_estimate=pl.CostEstimate(flops=flops, bytes_accessed=nbytes, transcendentals=0),
        **kwargs,
    )(*ins)


def swap(value, axis):
    return lax.ppermute(value, axis, [(0, 1), (1, 0)])


def dot(a, b, ca, cb):
    return lax.dot_general(a, b, (((ca,), (cb,)), ((), ())), preferred_element_type=F32)


def run(copies):
    for copy in copies:
        copy.start()
    for copy in copies:
        copy.wait()


def prepare(codes, rows, scales, g, v, u, pack, stack, mine, row_held, scale_held, sems):
    core = lax.axis_index("core")
    near_at, far_at = core * HALF, (1 - core) * HALF
    copies = [
        pltpu.make_async_copy(codes, pack.at[pl.ds(0, OWN), :], sems.at[0]),
        pltpu.make_async_copy(v, stack.at[pl.ds(0, 256), :], sems.at[1]),
        pltpu.make_async_copy(u, stack.at[pl.ds(256, 256), :], sems.at[2]),
        pltpu.make_async_copy(g.at[pl.ds(pl.multiple_of(near_at, HALF), HALF), :], mine, sems.at[3]),
    ]
    for k in range(4):
        copies.append(
            pltpu.make_async_copy(
                g.at[pl.ds(pl.multiple_of(far_at + 96 * k, 96), 96), :],
                stack.at[pl.ds(512, 96), pl.ds(256 * k, 256)],
                sems.at[4 + k],
            )
        )
    lists = [
        pltpu.make_async_copy(rows, row_held, sems.at[8]),
        pltpu.make_async_copy(scales, scale_held, sems.at[9]),
    ]
    for copy in lists + copies:
        copy.start()
    for copy in lists:
        copy.wait()
    row = row_held[...].reshape(1, OWN)
    kind = lax.broadcasted_iota(jnp.int32, (PACK - OWN, 128), 0)

    def spread(line):
        line = jnp.pad(line.astype(F32), ((0, 0), (0, PACK - OWN)))
        return jnp.concatenate([line, line], axis=1)

    high, low, scale = spread(row >> 5), spread(row & 31), spread(scale_held[...].reshape(1, OWN))
    text = jnp.where(kind == 0, high, jnp.where(kind == 1, low, jnp.where(kind == 2, scale, 0.0)))
    text = text.astype(BF16)
    for i in range(8):
        pack[OWN:, 128 * i : 128 * i + 128] = text
    for copy in copies:
        copy.wait()


def front(mine, near, far, out):
    own = mine[...]
    other = jnp.concatenate([far[512:, 256 * k : 256 * k + 256] for k in range(4)], axis=0)
    for j in range(4):
        cols = slice(256 * j, 256 * j + 256)
        part = dot(own, near[:256, cols], 1, 0) + dot(other, far[:256, cols], 1, 0)
        part = part.astype(BF16)
        out[2 * j, :HALF, :] = part[:, :128]
        out[2 * j + 1, :HALF, :] = part[:, 128:]


def attach(pack, _, out, sems):
    run(
        [
            pltpu.make_async_copy(
                pack.at[:, pl.ds(128 * i, 128)], out.at[i, pl.ds(HALF, PACK), :], sems.at[i]
            )
            for i in range(8)
        ]
    )


def add_up(recv, act, packs):
    total = recv[0, :HALF, :].astype(F32)
    for i in range(1, 8):
        total = total + recv[i, :HALF, :].astype(F32)
    act[...] = total
    for i in range(8):
        packs[i] = recv[i, HALF:, :]


def slope(act, near, far, out):
    hidden = jnp.zeros((HALF, 128), F32)
    scale = jnp.zeros((HALF, 128), F32)
    token = lax.broadcasted_iota(jnp.int32, (HALF, 128), 0) + lax.axis_index("core") * HALF
    lane = lax.broadcasted_iota(jnp.int32, (1, 128), 1)
    valid = (lane % PACK) < OWN
    for i in range(8):
        text = jnp.where(
            lane < PACK, near[i, OWN:, :].astype(F32), far[i, OWN:, :].astype(F32)
        )
        rows = (text[0:1] * 32.0 + text[1:2]).astype(jnp.int32)
        hit = (token == rows) & valid
        codes = jnp.concatenate([near[i], far[i]], axis=0)
        hidden = hidden + dot(jnp.where(hit, 1.0, 0.0).astype(BF16), codes, 1, 0)
        scale = scale + jnp.where(hit, text[2:3], 0.0)
    hidden = hidden * jnp.sum(scale, axis=1, keepdims=True)
    density = jnp.exp(-0.5 * hidden * hidden) * 0.3989422804014327
    cumulative = 0.5 * (1.0 + lax.erf(hidden * 0.7071067811865476))
    grad = (act[...] * (cumulative + hidden * density)).astype(BF16)
    activated = (hidden * cumulative).astype(BF16)
    for i in range(8):
        out[i, :HALF, :] = grad
        out[i, HALF:, :] = activated


def input_part(both, near, far, out):
    core = lax.axis_index("core")
    rows = jnp.concatenate([both[i, :HALF, :] for i in range(8)], axis=1)
    near_at = pl.multiple_of(256 * core, 256)
    far_at = pl.multiple_of(256 * (1 - core), 256)
    out[:, pl.ds(near_at, 256)] = dot(rows, near[256:512, :], 1, 1).astype(BF16)
    out[:, pl.ds(far_at, 256)] = dot(rows, far[256:512, :], 1, 1).astype(BF16)


def add_x(recv, mine, far, out):
    core, x = lax.axis_index("core"), lax.axis_index("x")
    total = recv[0].astype(F32)
    for i in range(1, 4):
        total = total + recv[i].astype(F32)
    out[...] = total.astype(BF16)

    @pl.when(lax.axis_index("zh") == 0)
    def _():
        own = mine[pl.ds(pl.multiple_of(x * 96, 96), 96), :].astype(F32)
        other = far[512:, pl.ds(pl.multiple_of(x * 256, 256), 256)].astype(F32)
        left = jnp.where(core == 0, own, other)
        right = jnp.where(core == 0, other, own)
        out[...] = (total + jnp.concatenate([left, right], axis=1)).astype(BF16)


def add_z(_, a, b, c, d, out):
    total = a[...].astype(F32) + b[...].astype(F32) + c[...].astype(F32) + d[...].astype(F32)
    total = total.astype(BF16)
    for i in range(4):
        out[i] = total[:, :256]
        out[4 + i] = total[:, 256:]


def follow(*_):
    pass


def weights(x, g, both, both_far, grad_up, grad_down, after):
    core = lax.axis_index("core")
    after[...] = jnp.zeros_like(after)
    near_at = pl.multiple_of(core * HALF, HALF)
    far_at = pl.multiple_of((1 - core) * HALF, HALF)
    for left, rows, out in ((x, slice(0, HALF), grad_up), (g, slice(HALF, 2 * HALF), grad_down)):
        mine = left[pl.ds(near_at, HALF), :].T
        far = left[pl.ds(far_at, HALF), :].T
        for j in range(4):
            near_cols = jnp.concatenate([both[2 * j, rows, :], both[2 * j + 1, rows, :]], axis=1)
            far_cols = jnp.concatenate([both_far[2 * j, rows, :], both_far[2 * j + 1, rows, :]], axis=1)
            part = dot(mine, near_cols, 1, 0) + dot(far, far_cols, 1, 0)
            out[:, 256 * j : 256 * j + 256] = part.astype(BF16)


def shards(layer_input, w_up, w_down, parked_codes, parked_scales, parked_rows, incoming):
    pack, near, mine = call(
        prepare, [((PACK, 1024), BF16), ((STACK, 1024), BF16), ((HALF, 256), BF16)],
        (parked_codes, parked_rows, parked_scales, incoming, w_down, w_up),
        in_specs=[HBM] * 6, nbytes=5 << 20, vmem=60,
        scratch=(pltpu.VMEM((OWN,), jnp.int32), pltpu.VMEM((OWN,), BF16), DMA((10,))),
    )
    pack = swap(pack, "half")
    far = swap(near, "core")

    wide = HALF + PACK
    sent = call(
        front, ((8, wide, 128), BF16), (mine, near, far)
    )
    sent = call(
        attach, ((8, wide, 128), BF16), (pack, sent), scratch=(DMA((8,)),),
        nbytes=1 << 18, in_specs=[VMEM, ANY], out_specs=ANY, input_output_aliases={1: 0},
    )
    recv = lax.all_to_all(sent, CHIPS, 0, 0, tiled=True)
    act, packs = call(add_up, [((HALF, 128), F32), ((8, PACK, 128), BF16)], (recv,), nbytes=1 << 20)
    packs_far = swap(packs, "core")
    both = call(
        slope, ((8, 2 * HALF, 128), BF16), (act, packs, packs_far), flops=1 << 27, nbytes=2 << 20
    )
    both = lax.all_to_all(both, CHIPS, 0, 0, tiled=True)

    part = call(
        input_part, ((HALF, 512), BF16), (both, near, far),
        flops=2 * HALF * 512 * 1024, nbytes=3 << 20,
    )
    part = lax.all_to_all(part.reshape(4, 96, 512), "x", 0, 0, tiled=True)
    summed = call(add_x, ((96, 512), BF16), (part, mine, far), nbytes=1 << 20)
    got = [
        lax.ppermute(summed, ("half", "zh"), [(4 + i, (i + k) % 4) for i in range(4)])
        for k in range(4)
    ]
    later = call(
        follow, ((8, 2 * HALF, 128), BF16), (part, both), in_specs=[ANY, ANY], out_specs=ANY,
        input_output_aliases={1: 0},
    )
    later_far = swap(later, "core")
    grad_up, grad_down, after = call(
        weights, [((256, 1024), BF16), ((256, 1024), BF16), ((8, 128), F32)],
        (layer_input, incoming, later, later_far), flops=4 * TOK * 256 * 1024, nbytes=5 << 20,
    )
    whole = call(
        add_z, ((8, 96, 256), BF16), (after, *got), nbytes=1 << 20
    )
    passed = lax.all_to_all(whole, ("core", "x"), 0, 0, tiled=True).reshape(TOK, 256)
    return grad_up, grad_down, passed


def solution(mesh):
    fine = Mesh(mesh.devices.reshape(SHAPE), NAMES)
    return jax.shard_map(
        shards,
        mesh=fine,
        in_specs=(
            P(None, SECTION),
            P(SECTION, TENSOR),
            P(SECTION, TENSOR),
            P(SECTION, TENSOR),
            P(SECTION),
            P(SECTION),
            P(None, SECTION),
        ),
        out_specs=(P(SECTION, TENSOR), P(SECTION, TENSOR), P(None, SECTION)),
        check_vma=False,
    )
```

time: 140 us -> 120 us (0.86)
  the two profiles are of different devices: /device:TPU:1 before, /device:TPU:33 now
where the time goes in v2:
time: 120 us; the launch traced here: 119 us
  blocking collectives  61.2 us (51%)
  waiting for transfers between devices  25.7 us (21%)
  starting transfers between devices  21.8 us (18%)
  Pallas kernels  6.7 us (6%)
  local copies, waits for them, and re-layouts  2.97 us (2%)
    all_to_all x1, blocking collectives, shards(): both = lax.all_to_all(both, CHIPS, 0, 0, tiled=True)  23 us
    ppermute x4, waiting for transfers between devices, shards(): lax.ppermute(summed, ('half', 'zh'), [(4 + i, (i + k) % 4) for i in range...  21.7 us
    all_to_all x1, blocking collectives, shards(): recv = lax.all_to_all(sent, CHIPS, 0, 0, tiled=True)  17.4 us
    ppermute x4, starting transfers between devices, swap(): return lax.ppermute(value, axis, [(0, 1), (1, 0)])  16.7 us
    all_to_all x1, blocking collectives, shards(): lax.all_to_all(whole, ('core', 'x'), 0, 0, tiled=True).reshape(TOK, 256)  10.8 us
    all_to_all x1, blocking collectives, shards(): part = lax.all_to_all(part.reshape(4, 96, 512), 'x', 0, 0, tiled=True)  10 us
    pallas_call x10, Pallas kernels, call(): pl.pallas_call(kernel, out_shape=shapes if many else shapes[0], scratch_s...  6.7 us
    ppermute x4, starting transfers between devices, shards(): lax.ppermute(summed, ('half', 'zh'), [(4 + i, (i + k) % 4) for i in range...  5.17 us
  transfers between devices with their start and end apart: 8, of which 5 were waited for; matrix products, arithmetic and copies ran while one was open for 0% of the time, Pallas kernels for 2%

profile of v2, /device:TPU:33, one launch (start us, length us, event | category | flops | bytes accessed | tf_op | source)
XLA Modules:
  0.0 119.2 jit_solution(16928099042263076847)
XLA Ops:
  0.6 2.5 %shard_map.94 = (bf16[64,1024]{1,0:T(8,128)(2,1)}, bf16[608,1024]{1,0:T(8,128)(2,1)}, bf16[384,256]{1,0:T(8,128)(2,1)}) custom-call(bf16[48,1024]{1,0:T(8,128)(2,1)} %codes.1, s32[48]{0:T(128)} %rows.1, bf16[48]{0:T(256)(128)(2,1)} %scales.1, bf16[768,256]{1,0:T(8,128)(2,1)} %g.3, bf16[256,1024]{1,0:T(8,128)(2,1)} %v.1, bf16[256,1024]{1,0:T(8,128)(2,1)} %u.1), custom_call_target="tpu_custom_call" | custom-call | bytes 5242880 | tf_op jit(solution)/shard_map/pallas_call | solution.py:31
  3.2 2.6 %collective-permute-start.1 = (bf16[608,1024]{1,0:T(8,128)(2,1)}, bf16[608,1024]{1,0:T(8,128)(2,1)S(1)}, u32[]{:S(2)}, u32[]{:S(2)}) collective-permute-start(bf16[608,1024]{1,0:T(8,128)(2,1)} %get-tuple-element.13.near), channel_id=1, source_target_pairs={{0,16},{16,0},{1,17},{17,1},{2,18},{18,2},{3,19},{19,3},{4,20},{20... | collective-permute-start | bytes 3735560 | tf_op jit(solution)/shard_map/ppermute | solution.py:42
  5.8 4.9 %collective-permute-start = (bf16[64,1024]{1,0:T(8,128)(2,1)}, bf16[64,1024]{1,0:T(8,128)(2,1)S(1)}, u32[]{:S(2)}, u32[]{:S(2)}) collective-permute-start(bf16[64,1024]{1,0:T(8,128)(2,1)} %get-tuple-element.11), channel_id=1, source_target_pairs={{0,256},{256,0},{1,257},{257,1},{2,258},{258,2},{3,259},{259,3},{4... | collective-permute-start | bytes 393224 | tf_op jit(solution)/shard_map/ppermute | solution.py:42
  10.7 0.0 collective-permute-done.1.far
  10.7 0.0 copy-start
  10.7 1.3 %copy-done = bf16[608,1024]{1,0:T(8,128)(2,1)S(1)} copy-done((bf16[608,1024]{1,0:T(8,128)(2,1)S(1)}, bf16[608,1024]{1,0:T(8,128)(2,1)}, u32[]{:S(2)}) %copy-start) | copy-done | bytes 1245208
  12.0 0.0 copy-start.3
  12.0 0.9 copy-done.3
  12.9 0.6 shard_map.95._
  13.5 3.1 %collective-permute-done.pack = bf16[64,1024]{1,0:T(8,128)(2,1)S(1)} collective-permute-done((bf16[64,1024]{1,0:T(8,128)(2,1)}, bf16[64,1024]{1,0:T(8,128)(2,1)S(1)}, u32[]{:S(2)}, u32[]{:S(2)}) %collective-permute-start) | collective-permute-done | bytes 131104 | tf_op jit(solution)/shard_map/ppermute | solution.py:42
  16.6 0.1 shard_map.96
  16.7 17.4 %all_to_all.20.recv = bf16[8,448,128]{2,1,0:T(8,128)(2,1)S(1)} all-to-all(bf16[8,448,128]{2,1,0:T(8,128)(2,1)S(1)} %shard_map.96), channel_id=1, replica_groups=mesh['half'=2,'zb'=2,'y'=4,'core'=2,'zh'=4,'x'=4] {'zb','y'}, dimensions={0} | all-to-all | bytes 1835008 | tf_op jit(solution)/shard_map/all_to_all | solution.py:223
  34.1 0.1 shard_map.97
  34.2 3.9 %collective-permute-start.2 = (bf16[8,64,128]{2,1,0:T(8,128)(2,1)S(1)}, bf16[8,64,128]{2,1,0:T(8,128)(2,1)S(1)}, u32[]{:S(2)}, u32[]{:S(2)}) collective-permute-start(bf16[8,64,128]{2,1,0:T(8,128)(2,1)S(1)} %get-tuple-element.15.near), channel_id=1, source_target_pairs={{0,16},{16,0},{1,17},{17,1},{2,18},{18,2},{3,19},{19,3},{4,20},{20... | collective-permute-start | bytes 393224 | tf_op jit(solution)/shard_map/ppermute | solution.py:42
  38.1 1.0 collective-permute-done.2.far
  39.1 0.5 shard_map.98
  39.6 0.0 copy-start.1
  39.6 23.0 %all_to_all.21.both.__1_ = bf16[8,768,128]{2,1,0:T(8,128)(2,1)S(1)} all-to-all(bf16[8,768,128]{2,1,0:T(8,128)(2,1)S(1)} %shard_map.98), channel_id=1, replica_groups=mesh['half'=2,'zb'=2,'y'=4,'core'=2,'zh'=4,'x'=4] {'zb','y'}, dimensions={0} | all-to-all | bytes 3145728 | tf_op jit(solution)/shard_map/all_to_all | solution.py:229
  62.6 0.0 copy-done.1
  62.6 0.6 shard_map.99
  63.2 10.0 %all_to_all.22.__0_.recv = bf16[4,96,512]{2,1,0:T(8,128)(2,1)S(1)} all-to-all(bf16[4,96,512]{2,1,0:T(8,128)(2,1)S(1)} %bitcast.2), channel_id=1, replica_groups=mesh['half'=2,'zb'=2,'y'=4,'core'=2,'zh'=4,'x'=4] {'x'}, dimensions={0} | all-to-all | bytes 786432 | tf_op jit(solution)/shard_map/all_to_all | solution.py:235
  73.3 0.0 copy-start.4
  73.3 0.0 copy-start.2
  73.3 0.0 copy-start.5
  73.3 5.3 %collective-permute-start.3 = (bf16[8,768,128]{2,1,0:T(8,128)(2,1)S(1)}, bf16[8,768,128]{2,1,0:T(8,128)(2,1)S(1)}, u32[]{:S(2)}, u32[]{:S(2)}) collective-permute-start(bf16[8,768,128]{2,1,0:T(8,128)(2,1)S(1)} %shard_map.100.both), channel_id=1, source_target_pairs={{0,16},{16,0},{1,17},{17,1},{2,18},{18,2},{3,19},{19,3},{4,20},{20... | collective-permute-start | bytes 4718600 | tf_op jit(solution)/shard_map/ppermute | solution.py:42
  78.5 0.0 copy-done.4
  78.6 0.1 shard_map.102
  78.6 1.3 %collective-permute-start.7 = (bf16[96,512]{1,0:T(8,128)(2,1)S(1)}, bf16[96,512]{1,0:T(8,128)(2,1)S(1)}, u32[]{:S(2)}, u32[]{:S(2)}) collective-permute-start(bf16[96,512]{1,0:T(8,128)(2,1)S(1)} %shard_map.102), channel_id=1, source_target_pairs={{256,12},{260,0},{264,4},{268,8},{257,13},{261,1},{265,5},{269,9},... | collective-permute-start | bytes 294920 | tf_op jit(solution)/shard_map/ppermute | solution.py:238
  79.9 1.3 %collective-permute-start.6 = (bf16[96,512]{1,0:T(8,128)(2,1)S(1)}, bf16[96,512]{1,0:T(8,128)(2,1)S(1)}, u32[]{:S(2)}, u32[]{:S(2)}) collective-permute-start(bf16[96,512]{1,0:T(8,128)(2,1)S(1)} %shard_map.102), channel_id=1, source_target_pairs={{256,8},{260,12},{264,0},{268,4},{257,9},{261,13},{265,1},{269,5},... | collective-permute-start | bytes 294920 | tf_op jit(solution)/shard_map/ppermute | solution.py:238
  81.2 1.3 %collective-permute-start.5 = (bf16[96,512]{1,0:T(8,128)(2,1)S(1)}, bf16[96,512]{1,0:T(8,128)(2,1)S(1)}, u32[]{:S(2)}, u32[]{:S(2)}) collective-permute-start(bf16[96,512]{1,0:T(8,128)(2,1)S(1)} %shard_map.102), channel_id=1, source_target_pairs={{256,4},{260,8},{264,12},{268,0},{257,5},{261,9},{265,13},{269,1},... | collective-permute-start | bytes 294920 | tf_op jit(solution)/shard_map/ppermute | solution.py:238
  82.5 1.3 %collective-permute-start.4 = (bf16[96,512]{1,0:T(8,128)(2,1)S(1)}, bf16[96,512]{1,0:T(8,128)(2,1)S(1)}, u32[]{:S(2)}, u32[]{:S(2)}) collective-permute-start(bf16[96,512]{1,0:T(8,128)(2,1)S(1)} %shard_map.102), channel_id=1, source_target_pairs={{256,0},{260,4},{264,8},{268,12},{257,1},{261,5},{265,9},{269,13},... | collective-permute-start | bytes 294920 | tf_op jit(solution)/shard_map/ppermute | solution.py:238
  83.8 0.0 collective-permute-done.3.both_far
  83.8 0.0 copy-done.2
  83.9 0.0 copy-done.5
  83.9 2.1 %shard_map.101 = (bf16[256,1024]{1,0:T(8,128)(2,1)}, bf16[256,1024]{1,0:T(8,128)(2,1)}, f32[8,128]{1,0:T(8,128)S(1)}) custom-call(bf16[768,256]{1,0:T(8,128)(2,1)S(1)} %copy-done.5, bf16[768,256]{1,0:T(8,128)(2,1)S(1)} %copy-done.2, bf16[8,768,128]{2,1,0:T(8,128)(2,1)S(1)} %shard_map.100.both, bf16[8,768,128]{2,1,0:T(8,128)(2,1)S(1)} %collective-permute-done.3.both_far), custom_call_target="tpu_custom_call" | custom-call | flops 805306368 | bytes 5242880 | tf_op jit(solution)/shard_map/pallas_call | solution.py:31
  86.0 6.8 %collective-permute-done.7.d = bf16[96,512]{1,0:T(8,128)(2,1)S(1)} collective-permute-done((bf16[96,512]{1,0:T(8,128)(2,1)S(1)}, bf16[96,512]{1,0:T(8,128)(2,1)S(1)}, u32[]{:S(2)}, u32[]{:S(2)}) %collective-permute-start.7) | collective-permute-done | bytes 98336 | tf_op jit(solution)/shard_map/ppermute | solution.py:238
  92.7 11.1 %collective-permute-done.6.c = bf16[96,512]{1,0:T(8,128)(2,1)S(1)} collective-permute-done((bf16[96,512]{1,0:T(8,128)(2,1)S(1)}, bf16[96,512]{1,0:T(8,128)(2,1)S(1)}, u32[]{:S(2)}, u32[]{:S(2)}) %collective-permute-start.6) | collective-permute-done | bytes 98336 | tf_op jit(solution)/shard_map/ppermute | solution.py:238
  103.8 3.8 %collective-permute-done.5.b = bf16[96,512]{1,0:T(8,128)(2,1)S(1)} collective-permute-done((bf16[96,512]{1,0:T(8,128)(2,1)S(1)}, bf16[96,512]{1,0:T(8,128)(2,1)S(1)}, u32[]{:S(2)}, u32[]{:S(2)}) %collective-permute-start.5) | collective-permute-done | bytes 98336 | tf_op jit(solution)/shard_map/ppermute | solution.py:238
  107.7 0.0 collective-permute-done.4.a
  107.7 0.1 shard_map.103
  107.7 10.8 %all_to_all.23 = bf16[8,96,256]{2,1,0:T(8,128)(2,1)S(1)} all-to-all(bf16[8,96,256]{2,1,0:T(8,128)(2,1)S(1)} %shard_map.103), channel_id=1, replica_groups=mesh['half'=2,'zb'=2,'y'=4,'core'=2,'zh'=4,'x'=4] {'core','x'}, dimensions={0} | all-to-all | bytes 786432 | tf_op jit(solution)/shard_map/all_to_all | solution.py:253
  118.5 0.7 copy.15
  (1 shorter events, 0.0 us)
Async XLA Ops:
  3.2 7.5 %collective-permute-start.1 = (bf16[608,1024]{1,0:T(8,128)(2,1)}, bf16[608,1024]{1,0:T(8,128)(2,1)S(1)}, u32[]{:S(2)}, u32[]{:S(2)}) collective-permute-start(bf16[608,1024]{1,0:T(8,128)(2,1)} %get-tuple-element.13.near), channel_id=1, source_target_pairs={{0,16},{16,0},{1,17},{17,1},{2,18},{18,2},{3,19},{19,3},{4,20},{20... | collective-permute-start | bytes 3735560 | tf_op jit(solution)/shard_map/ppermute | solution.py:42
  5.8 10.8 %collective-permute-start = (bf16[64,1024]{1,0:T(8,128)(2,1)}, bf16[64,1024]{1,0:T(8,128)(2,1)S(1)}, u32[]{:S(2)}, u32[]{:S(2)}) collective-permute-start(bf16[64,1024]{1,0:T(8,128)(2,1)} %get-tuple-element.11), channel_id=1, source_target_pairs={{0,256},{256,0},{1,257},{257,1},{2,258},{258,2},{3,259},{259,3},{4... | collective-permute-start | bytes 393224 | tf_op jit(solution)/shard_map/ppermute | solution.py:42
  10.7 1.3 %copy-start = (bf16[608,1024]{1,0:T(8,128)(2,1)S(1)}, bf16[608,1024]{1,0:T(8,128)(2,1)}, u32[]{:S(2)}) copy-start(bf16[608,1024]{1,0:T(8,128)(2,1)} %get-tuple-element.13.near) | copy-start | bytes 3735556
  12.0 0.9 copy-start.3
  34.2 4.9 %collective-permute-start.2 = (bf16[8,64,128]{2,1,0:T(8,128)(2,1)S(1)}, bf16[8,64,128]{2,1,0:T(8,128)(2,1)S(1)}, u32[]{:S(2)}, u32[]{:S(2)}) collective-permute-start(bf16[8,64,128]{2,1,0:T(8,128)(2,1)S(1)} %get-tuple-element.15.near), channel_id=1, source_target_pairs={{0,16},{16,0},{1,17},{17,1},{2,18},{18,2},{3,19},{19,3},{4,20},{20... | collective-permute-start | bytes 393224 | tf_op jit(solution)/shard_map/ppermute | solution.py:42
  39.6 23.0 %copy-start.1 = (bf16[608,1024]{1,0:T(8,128)(2,1)S(1)}, bf16[608,1024]{1,0:T(8,128)(2,1)}, u32[]{:S(2)}) copy-start(bf16[608,1024]{1,0:T(8,128)(2,1)} %get-tuple-element.13.near) | copy-start | bytes 3735556
  73.3 5.3 %copy-start.4 = (bf16[384,256]{1,0:T(8,128)(2,1)S(1)}, bf16[384,256]{1,0:T(8,128)(2,1)}, u32[]{:S(2)}) copy-start(bf16[384,256]{1,0:T(8,128)(2,1)} %get-tuple-element.12.mine) | copy-start | bytes 589828
  73.3 10.6 %copy-start.2 = (bf16[768,256]{1,0:T(8,128)(2,1)S(1)}, bf16[768,256]{1,0:T(8,128)(2,1)}, u32[]{:S(2)}) copy-start(bf16[768,256]{1,0:T(8,128)(2,1)} %g.3) | copy-start | bytes 1179652
  73.3 10.6 %copy-start.5 = (bf16[768,256]{1,0:T(8,128)(2,1)S(1)}, bf16[768,256]{1,0:T(8,128)(2,1)}, u32[]{:S(2)}) copy-start(bf16[768,256]{1,0:T(8,128)(2,1)} %x.1) | copy-start | bytes 1179652
  73.3 10.6 %collective-permute-start.3 = (bf16[8,768,128]{2,1,0:T(8,128)(2,1)S(1)}, bf16[8,768,128]{2,1,0:T(8,128)(2,1)S(1)}, u32[]{:S(2)}, u32[]{:S(2)}) collective-permute-start(bf16[8,768,128]{2,1,0:T(8,128)(2,1)S(1)} %shard_map.100.both), channel_id=1, source_target_pairs={{0,16},{16,0},{1,17},{17,1},{2,18},{18,2},{3,19},{19,3},{4,20},{20... | collective-permute-start | bytes 4718600 | tf_op jit(solution)/shard_map/ppermute | solution.py:42
  78.6 14.1 %collective-permute-start.7 = (bf16[96,512]{1,0:T(8,128)(2,1)S(1)}, bf16[96,512]{1,0:T(8,128)(2,1)S(1)}, u32[]{:S(2)}, u32[]{:S(2)}) collective-permute-start(bf16[96,512]{1,0:T(8,128)(2,1)S(1)} %shard_map.102), channel_id=1, source_target_pairs={{256,12},{260,0},{264,4},{268,8},{257,13},{261,1},{265,5},{269,9},... | collective-permute-start | bytes 294920 | tf_op jit(solution)/shard_map/ppermute | solution.py:238
  79.9 23.9 %collective-permute-start.6 = (bf16[96,512]{1,0:T(8,128)(2,1)S(1)}, bf16[96,512]{1,0:T(8,128)(2,1)S(1)}, u32[]{:S(2)}, u32[]{:S(2)}) collective-permute-start(bf16[96,512]{1,0:T(8,128)(2,1)S(1)} %shard_map.102), channel_id=1, source_target_pairs={{256,8},{260,12},{264,0},{268,4},{257,9},{261,13},{265,1},{269,5},... | collective-permute-start | bytes 294920 | tf_op jit(solution)/shard_map/ppermute | solution.py:238
  81.2 26.4 %collective-permute-start.5 = (bf16[96,512]{1,0:T(8,128)(2,1)S(1)}, bf16[96,512]{1,0:T(8,128)(2,1)S(1)}, u32[]{:S(2)}, u32[]{:S(2)}) collective-permute-start(bf16[96,512]{1,0:T(8,128)(2,1)S(1)} %shard_map.102), channel_id=1, source_target_pairs={{256,4},{260,8},{264,12},{268,0},{257,5},{261,9},{265,13},{269,1},... | collective-permute-start | bytes 294920 | tf_op jit(solution)/shard_map/ppermute | solution.py:238
  82.5 25.1 %collective-permute-start.4 = (bf16[96,512]{1,0:T(8,128)(2,1)S(1)}, bf16[96,512]{1,0:T(8,128)(2,1)S(1)}, u32[]{:S(2)}, u32[]{:S(2)}) collective-permute-start(bf16[96,512]{1,0:T(8,128)(2,1)S(1)} %shard_map.102), channel_id=1, source_target_pairs={{256,0},{260,4},{264,8},{268,12},{257,1},{261,5},{265,9},{269,13},... | collective-permute-start | bytes 294920 | tf_op jit(solution)/shard_map/ppermute | solution.py:238

commit v3 on v2

v3 whole, which is shorter than its diff:
```python
import jax
import jax.numpy as jnp
from jax import lax
from jax.experimental import pallas as pl
from jax.experimental.pallas import tpu as pltpu
from jax.sharding import Mesh, PartitionSpec as P

SHAPE = (2, 2, 4, 2, 4, 4)
NAMES = ("half", "zb", "y", "core", "zh", "x")
SECTION = ("half", "zb", "y", "core")
TENSOR = ("zh", "x")
CHIPS = ("zb", "y")
F32 = jnp.float32
BF16 = jnp.bfloat16
TOK = 768
HALF = 384
OWN = 48
PACK = 64
STACK = 352
VMEM = pl.BlockSpec(memory_space=pltpu.VMEM)
ANY = pl.BlockSpec(memory_space=pl.ANY)
HBM = pl.BlockSpec(memory_space=pltpu.HBM)
DMA = pltpu.SemaphoreType.DMA


def call(kernel, outs, ins, scratch=(), flops=0, nbytes=0, vmem=48, **kwargs):
    many = isinstance(outs, list)
    shapes = [jax.ShapeDtypeStruct(shape, dtype) for shape, dtype in (outs if many else [outs])]
    kwargs.setdefault("in_specs", [VMEM] * len(ins))
    kwargs.setdefault("out_specs", [VMEM] * len(shapes) if many else VMEM)
    return pl.pallas_call(
        kernel,
        out_shape=shapes if many else shapes[0],
        scratch_shapes=list(scratch),
        compiler_params=pltpu.CompilerParams(vmem_limit_bytes=vmem << 20),
        cost_estimate=pl.CostEstimate(flops=flops, bytes_accessed=nbytes, transcendentals=0),
        **kwargs,
    )(*ins)


def swap(value, axis):
    return lax.ppermute(value, axis, [(0, 1), (1, 0)])


def dot(a, b, ca, cb):
    return lax.dot_general(a, b, (((ca,), (cb,)), ((), ())), preferred_element_type=F32)


def prepare(codes, rows, scales, g, v, packs, stack, row_held, scale_held, sems):
    far_at = (1 - lax.axis_index("core")) * HALF
    lists = [
        pltpu.make_async_copy(rows, row_held, sems.at[0]),
        pltpu.make_async_copy(scales, scale_held, sems.at[1]),
    ]
    cut = [
        pltpu.make_async_copy(
            codes.at[:, pl.ds(128 * i, 128)], packs.at[i, pl.ds(0, OWN), :], sems.at[2 + i]
        )
        for i in range(8)
    ]
    bulk = [pltpu.make_async_copy(v, stack.at[pl.ds(0, 256), :], sems.at[10])]
    for k in range(4):
        bulk.append(
            pltpu.make_async_copy(
                g.at[pl.ds(pl.multiple_of(far_at + 96 * k, 96), 96), :],
                stack.at[pl.ds(256, 96), pl.ds(256 * k, 256)],
                sems.at[11 + k],
            )
        )
    for copy in lists + cut + bulk:
        copy.start()
    for copy in lists:
        copy.wait()
    row = row_held[...].reshape(1, OWN)
    kind = lax.broadcasted_iota(jnp.int32, (PACK - OWN, 128), 0)

    def spread(line):
        line = jnp.pad(line.astype(F32), ((0, 0), (0, PACK - OWN)))
        return jnp.concatenate([line, line], axis=1)

    high, low, scale = spread(row >> 5), spread(row & 31), spread(scale_held[...].reshape(1, OWN))
    text = jnp.where(kind == 0, high, jnp.where(kind == 1, low, jnp.where(kind == 2, scale, 0.0)))
    text = text.astype(BF16)
    for i in range(16):
        packs[i, OWN:, :] = text
    for i in range(8):
        cut[i].wait()
        packs[8 + i, :OWN, :] = packs[i, :OWN, :]
    for copy in bulk:
        copy.wait()


def front(g, v, far, out, g_held, v_held, far_held, sems):
    near_at = pl.multiple_of(lax.axis_index("core") * HALF, HALF)
    copies = [
        pltpu.make_async_copy(g.at[pl.ds(near_at, HALF), :], g_held, sems.at[0]),
        pltpu.make_async_copy(v, v_held, sems.at[1]),
        pltpu.make_async_copy(far, far_held, sems.at[2]),
    ]
    for copy in copies:
        copy.start()
    for copy in copies:
        copy.wait()
    own = g_held[...]
    other = jnp.concatenate([far_held[256:, 256 * k : 256 * k + 256] for k in range(4)], axis=0)
    for j in range(4):
        cols = slice(256 * j, 256 * j + 256)
        part = dot(own, v_held[:, cols], 1, 0) + dot(other, far_held[:256, cols], 1, 0)
        part = part.astype(BF16)
        out[2 * j] = part[:, :128]
        out[2 * j + 1] = part[:, 128:]


def slope(recv, near, far, _, grads, activations):
    act = recv[0].astype(F32)
    for i in range(1, 8):
        act = act + recv[i].astype(F32)
    hidden = jnp.zeros((HALF, 128), F32)
    scale = jnp.zeros((HALF, 128), F32)
    token = lax.broadcasted_iota(jnp.int32, (HALF, 128), 0) + lax.axis_index("core") * HALF
    lane = lax.broadcasted_iota(jnp.int32, (1, 128), 1)
    valid = (lane % PACK) < OWN
    mirror = 8 * (1 - lax.axis_index("half"))
    for i in range(8):
        one, two = near[mirror + i], far[mirror + i]
        text = jnp.where(lane < PACK, one[OWN:].astype(F32), two[OWN:].astype(F32))
        rows = (text[0:1] * 32.0 + text[1:2]).astype(jnp.int32)
        hit = (token == rows) & valid
        codes = jnp.concatenate([one, two], axis=0)
        hidden = hidden + dot(jnp.where(hit, 1.0, 0.0).astype(BF16), codes, 1, 0)
        scale = scale + jnp.where(hit, text[2:3], 0.0)
    hidden = hidden * jnp.sum(scale, axis=1, keepdims=True)
    density = jnp.exp(-0.5 * hidden * hidden) * 0.3989422804014327
    cumulative = 0.5 * (1.0 + lax.erf(hidden * 0.7071067811865476))
    grad = (act * (cumulative + hidden * density)).astype(BF16)
    activated = (hidden * cumulative).astype(BF16)
    for i in range(8):
        grads[i] = grad
        activations[i] = activated


def input_part(hg, near, far, out):
    core = lax.axis_index("core")
    rows = jnp.concatenate([hg[i] for i in range(8)], axis=1)
    near_at = pl.multiple_of(256 * core, 256)
    far_at = pl.multiple_of(256 * (1 - core), 256)
    out[:, pl.ds(near_at, 256)] = dot(rows, near[...], 1, 1).astype(BF16)
    out[:, pl.ds(far_at, 256)] = dot(rows, far[...], 1, 1).astype(BF16)


def add_x(recv, g, far, out):
    core, x = lax.axis_index("core"), lax.axis_index("x")
    total = recv[0].astype(F32)
    for i in range(1, 4):
        total = total + recv[i].astype(F32)
    out[...] = total.astype(BF16)

    @pl.when(lax.axis_index("zh") == 0)
    def _():
        own = g[pl.ds(pl.multiple_of(core * HALF + x * 96, 96), 96), :].astype(F32)
        other = far[256:, pl.ds(pl.multiple_of(x * 256, 256), 256)].astype(F32)
        left = jnp.where(core == 0, own, other)
        right = jnp.where(core == 0, other, own)
        out[...] = (total + jnp.concatenate([left, right], axis=1)).astype(BF16)


def add_z(a, b, c, d, out):
    total = a[...].astype(F32) + b[...].astype(F32) + c[...].astype(F32) + d[...].astype(F32)
    total = total.astype(BF16)
    for i in range(4):
        out[i] = total[:, :256]
        out[4 + i] = total[:, 256:]


def finish(blocks, _, __, out):
    for i in range(8):
        out[96 * i : 96 * i + 96, :] = blocks[i]


def follow(*_):
    pass


def weights(left, near, far, out, after):
    after[...] = jnp.zeros_like(after)
    core = lax.axis_index("core")
    mine = left[pl.ds(pl.multiple_of(core * HALF, HALF), HALF), :].T
    other = left[pl.ds(pl.multiple_of((1 - core) * HALF, HALF), HALF), :].T
    for j in range(4):
        near_cols = jnp.concatenate([near[2 * j], near[2 * j + 1]], axis=1)
        far_cols = jnp.concatenate([far[2 * j], far[2 * j + 1]], axis=1)
        part = dot(mine, near_cols, 1, 0) + dot(other, far_cols, 1, 0)
        out[:, 256 * j : 256 * j + 256] = part.astype(BF16)


def shards(layer_input, w_up, w_down, parked_codes, parked_scales, parked_rows, incoming):
    packs, near = call(
        prepare, [((16, PACK, 128), BF16), ((STACK, 1024), BF16)],
        (parked_codes, parked_rows, parked_scales, incoming, w_down), in_specs=[HBM] * 5, nbytes=3 << 20,
        vmem=60, scratch=(pltpu.VMEM((OWN,), jnp.int32), pltpu.VMEM((OWN,), BF16), DMA((15,))),
    )
    packs = lax.all_to_all(packs, ("half",) + CHIPS, 0, 0, tiled=True)
    packs_far = swap(packs, "core")
    far = swap(near, "core")
    u_far = swap(w_up, "core")

    sent = call(
        front, ((8, HALF, 128), BF16), (incoming, w_down, far), in_specs=[HBM] * 3, vmem=60,
        scratch=(
            pltpu.VMEM((HALF, 256), BF16), pltpu.VMEM((256, 1024), BF16),
            pltpu.VMEM((STACK, 1024), BF16), DMA((3,)),
        ),
    )
    recv = lax.all_to_all(sent, CHIPS, 0, 0, tiled=True)
    share = ((8, HALF, 128), BF16)
    hg, act = call(
        slope, [share, share], (recv, packs, packs_far, u_far), flops=1 << 27, nbytes=2 << 20,
        in_specs=[VMEM] * 3 + [ANY],
    )
    hg = lax.all_to_all(hg, CHIPS, 0, 0, tiled=True)

    part = call(
        input_part, ((HALF, 512), BF16), (hg, w_up, u_far),
        flops=2 * HALF * 512 * 1024, nbytes=3 << 20,
    )
    hg = call(follow, share, (part, hg), in_specs=[ANY, ANY], out_specs=ANY, input_output_aliases={1: 0})
    hg_far = swap(hg, "core")
    part = lax.all_to_all(part.reshape(4, 96, 512), "x", 0, 0, tiled=True)
    summed = call(add_x, ((96, 512), BF16), (part, incoming, far), nbytes=1 << 20)
    got = [
        lax.ppermute(summed, ("half", "zh"), [(4 + i, (i + k) % 4) for i in range(4)])
        for k in range(4)
    ]
    act = call(follow, share, (summed, act), in_specs=[ANY, ANY], out_specs=ANY, input_output_aliases={1: 0}, nbytes=64 << 20)
    act = lax.all_to_all(act, CHIPS, 0, 0, tiled=True)
    whole = call(add_z, ((8, 96, 256), BF16), got)
    whole, act = call(
        follow, [((8, 96, 256), BF16), share], (whole, act), in_specs=[ANY] * 2, out_specs=[ANY] * 2,
        input_output_aliases={0: 0, 1: 1},
    )
    passed = lax.all_to_all(whole, ("core", "x"), 0, 0, tiled=True)
    (grad_up, up), (grad_down, down) = [
        call(
            weights, [((256, 1024), BF16), ((8, 128), F32)], (left, near, far),
            flops=2 * TOK * 256 * 1024, nbytes=3 << 20,
        )
        for left, near, far in ((layer_input, hg, hg_far), (incoming, act, swap(act, "core")))
    ]
    passed = call(finish, ((TOK, 256), BF16), (passed, up, down))
    return grad_up, grad_down, passed


def solution(mesh):
    fine = Mesh(mesh.devices.reshape(SHAPE), NAMES)
    return jax.shard_map(
        shards,
        mesh=fine,
        in_specs=(
            P(None, SECTION),
            P(SECTION, TENSOR),
            P(SECTION, TENSOR),
            P(SECTION, TENSOR),
            P(SECTION),
            P(SECTION),
            P(None, SECTION),
        ),
        out_specs=(P(SECTION, TENSOR), P(SECTION, TENSOR), P(None, SECTION)),
        check_vma=False,
    )
```

time: 120 us -> 113 us (0.942)
  the two profiles are of different devices: /device:TPU:33 before, /device:TPU:1 now
where the time goes in v3:
time: 113 us; the launch traced here: 112 us
  starting transfers between devices  47.8 us (42%)
  blocking collectives  25.6 us (23%)
  waiting for transfers between devices  23.7 us (21%)
  Pallas kernels  13.1 us (12%)
    ppermute x5, starting transfers between devices, swap(): return lax.ppermute(value, axis, [(0, 1), (1, 0)])  21.2 us
    all_to_all x1, blocking collectives, shards(): hg = lax.all_to_all(hg, CHIPS, 0, 0, tiled=True)  15.6 us
    pallas_call x12, Pallas kernels, call(): pl.pallas_call(kernel, out_shape=shapes if many else shapes[0], scratch_s...  13.1 us
    ppermute x4, waiting for transfers between devices, shards(): lax.ppermute(summed, ('half', 'zh'), [(4 + i, (i + k) % 4) for i in range...  10.9 us
    all_to_all x1, blocking collectives, shards(): part = lax.all_to_all(part.reshape(4, 96, 512), 'x', 0, 0, tiled=True)  10 us
    all_to_all x1, starting transfers between devices, shards(): packs = lax.all_to_all(packs, ('half',) + CHIPS, 0, 0, tiled=True)  9.2 us
    all_to_all x1, waiting for transfers between devices, shards(): recv = lax.all_to_all(sent, CHIPS, 0, 0, tiled=True)  5.34 us
    ppermute x4, starting transfers between devices, shards(): lax.ppermute(summed, ('half', 'zh'), [(4 + i, (i + k) % 4) for i in range...  5.17 us
  transfers between devices with their start and end apart: 13, of which 8 were waited for; matrix products, arithmetic and copies ran while one was open for 0% of the time, Pallas kernels for 7%

profile of v3, /device:TPU:1, one launch (start us, length us, event | category | flops | bytes accessed | tf_op | source)
XLA Modules:
  0.0 111.9 jit_solution(11799809882637536980)
XLA Ops:
  0.6 2.3 %shard_map.94 = (bf16[16,64,128]{2,1,0:T(8,128)(2,1)}, bf16[352,1024]{1,0:T(8,128)(2,1)}) custom-call(bf16[48,1024]{1,0:T(8,128)(2,1)} %codes.1, s32[48]{0:T(128)} %rows.1, bf16[48]{0:T(256)(128)(2,1)} %scales.1, bf16[768,256]{1,0:T(8,128)(2,1)} %left.3, bf16[256,1024]{1,0:T(8,128)(2,1)} %v.3), custom_call_target="tpu_custom_call" | custom-call | bytes 3145728 | tf_op jit(solution)/shard_map/pallas_call | solution.py:31
  2.9 9.2 %all-to-all-start.1 = ((bf16[16,64,128]{2,1,0:T(8,128)(2,1)}), bf16[16,64,128]{2,1,0:T(8,128)(2,1)S(1)}, u32[]{:S(2)}, u32[]{:S(2)}) async-start(bf16[16,64,128]{2,1,0:T(8,128)(2,1)} %get-tuple-element.14), calls=%async_computation.1 | async-start | bytes 524288 | tf_op jit(solution)/shard_map/all_to_all | solution.py:202
  12.1 3.1 %collective-permute-start = (bf16[352,1024]{1,0:T(8,128)(2,1)}, bf16[352,1024]{1,0:T(8,128)(2,1)S(1)}, u32[]{:S(2)}, u32[]{:S(2)}) collective-permute-start(bf16[352,1024]{1,0:T(8,128)(2,1)} %get-tuple-element.13), channel_id=1, source_target_pairs={{0,16},{16,0},{1,17},{17,1},{2,18},{18,2},{3,19},{19,3},{4,20},{20... | collective-permute-start | bytes 2162696 | tf_op jit(solution)/shard_map/ppermute | solution.py:42
  15.3 2.0 %collective-permute-done.far = bf16[352,1024]{1,0:T(8,128)(2,1)S(1)} collective-permute-done((bf16[352,1024]{1,0:T(8,128)(2,1)}, bf16[352,1024]{1,0:T(8,128)(2,1)S(1)}, u32[]{:S(2)}, u32[]{:S(2)}) %collective-permute-start) | collective-permute-done | bytes 720928 | tf_op jit(solution)/shard_map/ppermute | solution.py:42
  17.3 0.0 copy-start.1
  17.3 0.9 copy-done.1
  18.2 2.9 %shard_map.95 = bf16[8,384,128]{2,1,0:T(8,128)(2,1)} custom-call(bf16[768,256]{1,0:T(8,128)(2,1)} %left.3, bf16[256,1024]{1,0:T(8,128)(2,1)} %v.3, bf16[352,1024]{1,0:T(8,128)(2,1)} %copy-done.1), custom_call_target="tpu_custom_call" | custom-call | tf_op jit(solution)/shard_map/pallas_call | solution.py:31
  21.0 0.0 copy-start.3
  21.1 0.3 all-to-all-done.1.near
  21.4 5.1 %all-to-all-start = ((bf16[8,384,128]{2,1,0:T(8,128)(2,1)}), bf16[8,384,128]{2,1,0:T(8,128)(2,1)S(1)}, u32[]{:S(2)}, u32[]{:S(2)}) async-start(bf16[8,384,128]{2,1,0:T(8,128)(2,1)} %shard_map.95), calls=%async_computation | async-start | bytes 1572864 | tf_op jit(solution)/shard_map/all_to_all | solution.py:214
  26.4 0.0 copy-done.3
  26.4 2.8 %collective-permute-start.2 = (bf16[256,1024]{1,0:T(8,128)(2,1)S(1)}, bf16[256,1024]{1,0:T(8,128)(2,1)S(1)}, u32[]{:S(2)}, u32[]{:S(2)}) collective-permute-start(bf16[256,1024]{1,0:T(8,128)(2,1)S(1)} %copy-done.3), channel_id=1, source_target_pairs={{0,16},{16,0},{1,17},{17,1},{2,18},{18,2},{3,19},{19,3},{4,20},{20... | collective-permute-start | bytes 1572872 | tf_op jit(solution)/shard_map/ppermute | solution.py:42
  29.2 1.9 %collective-permute-start.1 = (bf16[16,64,128]{2,1,0:T(8,128)(2,1)S(1)}, bf16[16,64,128]{2,1,0:T(8,128)(2,1)S(1)}, u32[]{:S(2)}, u32[]{:S(2)}) collective-permute-start(bf16[16,64,128]{2,1,0:T(8,128)(2,1)S(1)} %all-to-all-done.1.near), channel_id=1, source_target_pairs={{0,16},{16,0},{1,17},{17,1},{2,18},{18,2},{3,19},{19,3},{4,20},{20... | collective-permute-start | bytes 786440 | tf_op jit(solution)/shard_map/ppermute | solution.py:42
  31.2 0.0 collective-permute-done.2._.far
  31.2 1.5 %collective-permute-done.1.far = bf16[16,64,128]{2,1,0:T(8,128)(2,1)S(1)} collective-permute-done((bf16[16,64,128]{2,1,0:T(8,128)(2,1)S(1)}, bf16[16,64,128]{2,1,0:T(8,128)(2,1)S(1)}, u32[]{:S(2)}, u32[]{:S(2)}) %collective-permute-start.1) | collective-permute-done | bytes 262176 | tf_op jit(solution)/shard_map/ppermute | solution.py:42
  32.7 5.3 %all-to-all-done.recv = bf16[8,384,128]{2,1,0:T(8,128)(2,1)S(1)} async-done(((bf16[8,384,128]{2,1,0:T(8,128)(2,1)}), bf16[8,384,128]{2,1,0:T(8,128)(2,1)S(1)}, u32[]{:S(2)}, u32[]{:S(2)}) %all-to-all-start) | async-done | bytes 786464 | tf_op jit(solution)/shard_map/all_to_all | solution.py:214
  38.0 1.5 %shard_map.96 = (bf16[8,384,128]{2,1,0:T(8,128)(2,1)S(1)}, bf16[8,384,128]{2,1,0:T(8,128)(2,1)}) custom-call(bf16[8,384,128]{2,1,0:T(8,128)(2,1)S(1)} %all-to-all-done.recv, bf16[16,64,128]{2,1,0:T(8,128)(2,1)S(1)} %all-to-all-done.1.near, bf16[16,64,128]{2,1,0:T(8,128)(2,1)S(1)} %collective-permute-done.1.far, ...), custom_call_target="tpu_custom_call" | custom-call | flops 134217728 | bytes 2097152 | tf_op jit(solution)/shard_map/pallas_call | solution.py:31
  39.5 15.6 %all_to_all.30.hg.__1_ = bf16[8,384,128]{2,1,0:T(8,128)(2,1)S(1)} all-to-all(bf16[8,384,128]{2,1,0:T(8,128)(2,1)S(1)} %get-tuple-element.15), channel_id=1, replica_groups=mesh['half'=2,'zb'=2,'y'=4,'core'=2,'zh'=4,'x'=4] {'zb','y'}, dimensions={0} | all-to-all | bytes 1572864 | tf_op jit(solution)/shard_map/all_to_all | solution.py:220
  55.1 0.0 copy-start.2
  55.1 0.6 shard_map.97.__0_
  55.7 0.0 copy-start
  55.7 10.0 %all_to_all.31.recv = bf16[4,96,512]{2,1,0:T(8,128)(2,1)S(1)} all-to-all(bf16[4,96,512]{2,1,0:T(8,128)(2,1)S(1)} %bitcast.1), channel_id=1, replica_groups=mesh['half'=2,'zb'=2,'y'=4,'core'=2,'zh'=4,'x'=4] {'x'}, dimensions={0} | all-to-all | bytes 786432 | tf_op jit(solution)/shard_map/all_to_all | solution.py:228
  65.7 0.0 copy-done.2
  65.7 0.0 copy-done
  65.7 0.1 shard_map.100.__0_
  65.8 3.6 %all-to-all-start.4 = ((bf16[8,384,128]{2,1,0:T(8,128)(2,1)}), bf16[8,384,128]{2,1,0:T(8,128)(2,1)S(1)}, u32[]{:S(2)}, u32[]{:S(2)}) async-start(bf16[8,384,128]{2,1,0:T(8,128)(2,1)} %shard_map.102), calls=%async_computation.4 | async-start | bytes 1572864 | tf_op jit(solution)/shard_map/all_to_all | solution.py:235
  69.4 1.3 %collective-permute-start.7 = (bf16[96,512]{1,0:T(8,128)(2,1)S(1)}, bf16[96,512]{1,0:T(8,128)(2,1)S(1)}, u32[]{:S(2)}, u32[]{:S(2)}) collective-permute-start(bf16[96,512]{1,0:T(8,128)(2,1)S(1)} %shard_map.100.__0_), channel_id=1, source_target_pairs={{256,12},{260,0},{264,4},{268,8},{257,13},{261,1},{265,5},{269,9},... | collective-permute-start | bytes 294920 | tf_op jit(solution)/shard_map/ppermute | solution.py:231
  70.7 1.3 %collective-permute-start.6 = (bf16[96,512]{1,0:T(8,128)(2,1)S(1)}, bf16[96,512]{1,0:T(8,128)(2,1)S(1)}, u32[]{:S(2)}, u32[]{:S(2)}) collective-permute-start(bf16[96,512]{1,0:T(8,128)(2,1)S(1)} %shard_map.100.__0_), channel_id=1, source_target_pairs={{256,8},{260,12},{264,0},{268,4},{257,9},{261,13},{265,1},{269,5},... | collective-permute-start | bytes 294920 | tf_op jit(solution)/shard_map/ppermute | solution.py:231
  72.0 1.3 %collective-permute-start.5 = (bf16[96,512]{1,0:T(8,128)(2,1)S(1)}, bf16[96,512]{1,0:T(8,128)(2,1)S(1)}, u32[]{:S(2)}, u32[]{:S(2)}) collective-permute-start(bf16[96,512]{1,0:T(8,128)(2,1)S(1)} %shard_map.100.__0_), channel_id=1, source_target_pairs={{256,4},{260,8},{264,12},{268,0},{257,5},{261,9},{265,13},{269,1},... | collective-permute-start | bytes 294920 | tf_op jit(solution)/shard_map/ppermute | solution.py:231
  73.3 1.3 %collective-permute-start.4 = (bf16[96,512]{1,0:T(8,128)(2,1)S(1)}, bf16[96,512]{1,0:T(8,128)(2,1)S(1)}, u32[]{:S(2)}, u32[]{:S(2)}) collective-permute-start(bf16[96,512]{1,0:T(8,128)(2,1)S(1)} %shard_map.100.__0_), channel_id=1, source_target_pairs={{256,0},{260,4},{264,8},{268,12},{257,1},{261,5},{265,9},{269,13},... | collective-permute-start | bytes 294920 | tf_op jit(solution)/shard_map/ppermute | solution.py:231
  74.6 5.6 %collective-permute-start.3 = (bf16[8,384,128]{2,1,0:T(8,128)(2,1)S(1)}, bf16[8,384,128]{2,1,0:T(8,128)(2,1)S(1)}, u32[]{:S(2)}, u32[]{:S(2)}) collective-permute-start(bf16[8,384,128]{2,1,0:T(8,128)(2,1)S(1)} %shard_map.98.near), channel_id=1, source_target_pairs={{0,16},{16,0},{1,17},{17,1},{2,18},{18,2},{3,19},{19,3},{4,20},{20... | collective-permute-start | bytes 2359304 | tf_op jit(solution)/shard_map/ppermute | solution.py:42
  80.2 1.2 %collective-permute-done.7.d = bf16[96,512]{1,0:T(8,128)(2,1)S(1)} collective-permute-done((bf16[96,512]{1,0:T(8,128)(2,1)S(1)}, bf16[96,512]{1,0:T(8,128)(2,1)S(1)}, u32[]{:S(2)}, u32[]{:S(2)}) %collective-permute-start.7) | collective-permute-done | bytes 98336 | tf_op jit(solution)/shard_map/ppermute | solution.py:231
  81.5 6.7 %collective-permute-done.6.c = bf16[96,512]{1,0:T(8,128)(2,1)S(1)} collective-permute-done((bf16[96,512]{1,0:T(8,128)(2,1)S(1)}, bf16[96,512]{1,0:T(8,128)(2,1)S(1)}, u32[]{:S(2)}, u32[]{:S(2)}) %collective-permute-start.6) | collective-permute-done | bytes 98336 | tf_op jit(solution)/shard_map/ppermute | solution.py:231
  88.2 2.9 %collective-permute-done.5.b = bf16[96,512]{1,0:T(8,128)(2,1)S(1)} collective-permute-done((bf16[96,512]{1,0:T(8,128)(2,1)S(1)}, bf16[96,512]{1,0:T(8,128)(2,1)S(1)}, u32[]{:S(2)}, u32[]{:S(2)}) %collective-permute-start.5) | collective-permute-done | bytes 98336 | tf_op jit(solution)/shard_map/ppermute | solution.py:231
  91.1 0.0 collective-permute-done.4.a
  91.1 0.8 shard_map.101.__0_
  91.9 0.0 all-to-all-done.4.__1_
  91.9 7.7 %collective-permute-start.8 = (bf16[8,384,128]{2,1,0:T(8,128)(2,1)S(1)}, bf16[8,384,128]{2,1,0:T(8,128)(2,1)}, u32[]{:S(2)}, u32[]{:S(2)}) collective-permute-start(bf16[8,384,128]{2,1,0:T(8,128)(2,1)S(1)} %get-tuple-element.18.near), channel_id=1, source_target_pairs={{0,16},{16,0},{1,17},{17,1},{2,18},{18,2},{3,19},{19,3},{4,20},{20... | collective-permute-start | bytes 2359304 | tf_op jit(solution)/shard_map/ppermute | solution.py:42
  99.6 0.0 copy-start.4
  99.7 3.5 %all-to-all-start.5 = ((bf16[8,96,256]{2,1,0:T(8,128)(2,1)}), bf16[8,96,256]{2,1,0:T(8,128)(2,1)S(1)}, u32[]{:S(2)}, u32[]{:S(2)}) async-start(bf16[8,96,256]{2,1,0:T(8,128)(2,1)} %get-tuple-element.20), calls=%async_computation.5 | async-start | bytes 786432 | tf_op jit(solution)/shard_map/all_to_all | solution.py:241
  103.2 0.0 collective-permute-done.3.far
  103.2 0.0 copy-done.4
  103.2 1.5 %shard_map.99 = (bf16[256,1024]{1,0:T(8,128)(2,1)}, f32[8,128]{1,0:T(8,128)S(1)}) custom-call(bf16[768,256]{1,0:T(8,128)(2,1)S(1)} %copy-done.4, bf16[8,384,128]{2,1,0:T(8,128)(2,1)S(1)} %shard_map.98.near, bf16[8,384,128]{2,1,0:T(8,128)(2,1)S(1)} %collective-permute-done.3.far), custom_call_target="tpu_custom_call" | custom-call | flops 402653184 | bytes 3145728 | tf_op jit(solution)/shard_map/pallas_call | solution.py:31
  104.8 0.0 collective-permute-done.8.far
  104.8 2.7 %shard_map.104 = (bf16[256,1024]{1,0:T(8,128)(2,1)}, f32[8,128]{1,0:T(8,128)S(1)}) custom-call(bf16[768,256]{1,0:T(8,128)(2,1)S(1)} %copy-done, bf16[8,384,128]{2,1,0:T(8,128)(2,1)S(1)} %get-tuple-element.18.near, bf16[8,384,128]{2,1,0:T(8,128)(2,1)} %collective-permute-done.8.far), custom_call_target="tpu_custom_call" | custom-call | flops 402653184 | bytes 3145728 | tf_op jit(solution)/shard_map/pallas_call | solution.py:31
  107.4 3.7 %all-to-all-done.5.blocks = bf16[8,96,256]{2,1,0:T(8,128)(2,1)S(1)} async-done(((bf16[8,96,256]{2,1,0:T(8,128)(2,1)}), bf16[8,96,256]{2,1,0:T(8,128)(2,1)S(1)}, u32[]{:S(2)}, u32[]{:S(2)}) %all-to-all-start.5) | async-done | bytes 393248 | tf_op jit(solution)/shard_map/all_to_all | solution.py:241
  111.2 0.8 shard_map.105
  (3 shorter events, 0.0 us)
Async XLA Ops:
  2.9 18.4 %all-to-all-start.1 = ((bf16[16,64,128]{2,1,0:T(8,128)(2,1)}), bf16[16,64,128]{2,1,0:T(8,128)(2,1)S(1)}, u32[]{:S(2)}, u32[]{:S(2)}) async-start(bf16[16,64,128]{2,1,0:T(8,128)(2,1)} %get-tuple-element.14), calls=%async_computation.1 | async-start | bytes 524288 | tf_op jit(solution)/shard_map/all_to_all | solution.py:202
  12.1 5.1 %collective-permute-start = (bf16[352,1024]{1,0:T(8,128)(2,1)}, bf16[352,1024]{1,0:T(8,128)(2,1)S(1)}, u32[]{:S(2)}, u32[]{:S(2)}) collective-permute-start(bf16[352,1024]{1,0:T(8,128)(2,1)} %get-tuple-element.13), channel_id=1, source_target_pairs={{0,16},{16,0},{1,17},{17,1},{2,18},{18,2},{3,19},{19,3},{4,20},{20... | collective-permute-start | bytes 2162696 | tf_op jit(solution)/shard_map/ppermute | solution.py:42
  17.3 0.9 copy-start.1
  21.0 5.4 %copy-start.3 = (bf16[256,1024]{1,0:T(8,128)(2,1)S(1)}, bf16[256,1024]{1,0:T(8,128)(2,1)}, u32[]{:S(2)}) copy-start(bf16[256,1024]{1,0:T(8,128)(2,1)} %near.1) | copy-start | bytes 1572868
  21.4 16.7 %all-to-all-start = ((bf16[8,384,128]{2,1,0:T(8,128)(2,1)}), bf16[8,384,128]{2,1,0:T(8,128)(2,1)S(1)}, u32[]{:S(2)}, u32[]{:S(2)}) async-start(bf16[8,384,128]{2,1,0:T(8,128)(2,1)} %shard_map.95), calls=%async_computation | async-start | bytes 1572864 | tf_op jit(solution)/shard_map/all_to_all | solution.py:214
  26.4 4.7 %collective-permute-start.2 = (bf16[256,1024]{1,0:T(8,128)(2,1)S(1)}, bf16[256,1024]{1,0:T(8,128)(2,1)S(1)}, u32[]{:S(2)}, u32[]{:S(2)}) collective-permute-start(bf16[256,1024]{1,0:T(8,128)(2,1)S(1)} %copy-done.3), channel_id=1, source_target_pairs={{0,16},{16,0},{1,17},{17,1},{2,18},{18,2},{3,19},{19,3},{4,20},{20... | collective-permute-start | bytes 1572872 | tf_op jit(solution)/shard_map/ppermute | solution.py:42
  29.2 3.4 %collective-permute-start.1 = (bf16[16,64,128]{2,1,0:T(8,128)(2,1)S(1)}, bf16[16,64,128]{2,1,0:T(8,128)(2,1)S(1)}, u32[]{:S(2)}, u32[]{:S(2)}) collective-permute-start(bf16[16,64,128]{2,1,0:T(8,128)(2,1)S(1)} %all-to-all-done.1.near), channel_id=1, source_target_pairs={{0,16},{16,0},{1,17},{17,1},{2,18},{18,2},{3,19},{19,3},{4,20},{20... | collective-permute-start | bytes 786440 | tf_op jit(solution)/shard_map/ppermute | solution.py:42
  55.1 10.6 %copy-start.2 = (bf16[352,1024]{1,0:T(8,128)(2,1)S(1)}, bf16[352,1024]{1,0:T(8,128)(2,1)}, u32[]{:S(2)}) copy-start(bf16[352,1024]{1,0:T(8,128)(2,1)} %copy-done.1) | copy-start | bytes 2162692
  55.7 10.0 %copy-start = (bf16[768,256]{1,0:T(8,128)(2,1)S(1)}, bf16[768,256]{1,0:T(8,128)(2,1)}, u32[]{:S(2)}) copy-start(bf16[768,256]{1,0:T(8,128)(2,1)} %left.3) | copy-start | bytes 1179652
  65.8 26.1 %all-to-all-start.4 = ((bf16[8,384,128]{2,1,0:T(8,128)(2,1)}), bf16[8,384,128]{2,1,0:T(8,128)(2,1)S(1)}, u32[]{:S(2)}, u32[]{:S(2)}) async-start(bf16[8,384,128]{2,1,0:T(8,128)(2,1)} %shard_map.102), calls=%async_computation.4 | async-start | bytes 1572864 | tf_op jit(solution)/shard_map/all_to_all | solution.py:235
  69.4 12.1 %collective-permute-start.7 = (bf16[96,512]{1,0:T(8,128)(2,1)S(1)}, bf16[96,512]{1,0:T(8,128)(2,1)S(1)}, u32[]{:S(2)}, u32[]{:S(2)}) collective-permute-start(bf16[96,512]{1,0:T(8,128)(2,1)S(1)} %shard_map.100.__0_), channel_id=1, source_target_pairs={{256,12},{260,0},{264,4},{268,8},{257,13},{261,1},{265,5},{269,9},... | collective-permute-start | bytes 294920 | tf_op jit(solution)/shard_map/ppermute | solution.py:231
  70.7 17.5 %collective-permute-start.6 = (bf16[96,512]{1,0:T(8,128)(2,1)S(1)}, bf16[96,512]{1,0:T(8,128)(2,1)S(1)}, u32[]{:S(2)}, u32[]{:S(2)}) collective-permute-start(bf16[96,512]{1,0:T(8,128)(2,1)S(1)} %shard_map.100.__0_), channel_id=1, source_target_pairs={{256,8},{260,12},{264,0},{268,4},{257,9},{261,13},{265,1},{269,5},... | collective-permute-start | bytes 294920 | tf_op jit(solution)/shard_map/ppermute | solution.py:231
  72.0 19.1 %collective-permute-start.5 = (bf16[96,512]{1,0:T(8,128)(2,1)S(1)}, bf16[96,512]{1,0:T(8,128)(2,1)S(1)}, u32[]{:S(2)}, u32[]{:S(2)}) collective-permute-start(bf16[96,512]{1,0:T(8,128)(2,1)S(1)} %shard_map.100.__0_), channel_id=1, source_target_pairs={{256,4},{260,8},{264,12},{268,0},{257,5},{261,9},{265,13},{269,1},... | collective-permute-start | bytes 294920 | tf_op jit(solution)/shard_map/ppermute | solution.py:231
  73.3 17.8 %collective-permute-start.4 = (bf16[96,512]{1,0:T(8,128)(2,1)S(1)}, bf16[96,512]{1,0:T(8,128)(2,1)S(1)}, u32[]{:S(2)}, u32[]{:S(2)}) collective-permute-start(bf16[96,512]{1,0:T(8,128)(2,1)S(1)} %shard_map.100.__0_), channel_id=1, source_target_pairs={{256,0},{260,4},{264,8},{268,12},{257,1},{261,5},{265,9},{269,13},... | collective-permute-start | bytes 294920 | tf_op jit(solution)/shard_map/ppermute | solution.py:231
  74.6 28.6 %collective-permute-start.3 = (bf16[8,384,128]{2,1,0:T(8,128)(2,1)S(1)}, bf16[8,384,128]{2,1,0:T(8,128)(2,1)S(1)}, u32[]{:S(2)}, u32[]{:S(2)}) collective-permute-start(bf16[8,384,128]{2,1,0:T(8,128)(2,1)S(1)} %shard_map.98.near), channel_id=1, source_target_pairs={{0,16},{16,0},{1,17},{17,1},{2,18},{18,2},{3,19},{19,3},{4,20},{20... | collective-permute-start | bytes 2359304 | tf_op jit(solution)/shard_map/ppermute | solution.py:42
  91.9 12.9 %collective-permute-start.8 = (bf16[8,384,128]{2,1,0:T(8,128)(2,1)S(1)}, bf16[8,384,128]{2,1,0:T(8,128)(2,1)}, u32[]{:S(2)}, u32[]{:S(2)}) collective-permute-start(bf16[8,384,128]{2,1,0:T(8,128)(2,1)S(1)} %get-tuple-element.18.near), channel_id=1, source_target_pairs={{0,16},{16,0},{1,17},{17,1},{2,18},{18,2},{3,19},{19,3},{4,20},{20... | collective-permute-start | bytes 2359304 | tf_op jit(solution)/shard_map/ppermute | solution.py:42
  99.6 3.6 %copy-start.4 = (bf16[768,256]{1,0:T(8,128)(2,1)S(1)}, bf16[768,256]{1,0:T(8,128)(2,1)}, u32[]{:S(2)}) copy-start(bf16[768,256]{1,0:T(8,128)(2,1)} %left.2) | copy-start | bytes 1179652
  99.7 11.5 %all-to-all-start.5 = ((bf16[8,96,256]{2,1,0:T(8,128)(2,1)}), bf16[8,96,256]{2,1,0:T(8,128)(2,1)S(1)}, u32[]{:S(2)}, u32[]{:S(2)}) async-start(bf16[8,96,256]{2,1,0:T(8,128)(2,1)} %get-tuple-element.20), calls=%async_computation.5 | async-start | bytes 786432 | tf_op jit(solution)/shard_map/all_to_all | solution.py:241

commit v4 on v3

--- a/solution.py
+++ b/solution.py
@@ -164,7 +164,7 @@
         out[...] = (total + jnp.concatenate([left, right], axis=1)).astype(BF16)
 
 
-def add_z(a, b, c, d, out):
+def add_z(_, __, a, b, c, d, out):
     total = a[...].astype(F32) + b[...].astype(F32) + c[...].astype(F32) + d[...].astype(F32)
     total = total.astype(BF16)
     for i in range(4):
@@ -172,7 +172,7 @@
         out[4 + i] = total[:, 256:]
 
 
-def finish(blocks, _, __, out):
+def finish(blocks, out):
     for i in range(8):
         out[96 * i : 96 * i + 96, :] = blocks[i]
 
@@ -219,34 +219,49 @@
     )
     hg = lax.all_to_all(hg, CHIPS, 0, 0, tiled=True)
 
-    part = call(
-        input_part, ((HALF, 512), BF16), (hg, w_up, u_far),
-        flops=2 * HALF * 512 * 1024, nbytes=3 << 20,
-    )
-    hg = call(follow, share, (part, hg), in_specs=[ANY, ANY], out_specs=ANY, input_output_aliases={1: 0})
-    hg_far = swap(hg, "core")
-    part = lax.all_to_all(part.reshape(4, 96, 512), "x", 0, 0, tiled=True)
-    summed = call(add_x, ((96, 512), BF16), (part, incoming, far), nbytes=1 << 20)
+    second = lax.axis_index("half") == 1
+
+    def reduce_x(hg, u, u_far, g, far):
+        part = call(
+            input_part, ((HALF, 512), BF16), (hg, u, u_far),
+            flops=2 * HALF * 512 * 1024, nbytes=3 << 20,
+        )
+        part = lax.all_to_all(part.reshape(4, 96, 512), "x", 0, 0, tiled=True)
+        return call(add_x, ((96, 512), BF16), (part, g, far), nbytes=1 << 20)
+
+    summed = lax.cond(
+        second, reduce_x, lambda *_: jnp.zeros((96, 512), BF16), hg, w_up, u_far, incoming, far
+    )
     got = [
         lax.ppermute(summed, ("half", "zh"), [(4 + i, (i + k) % 4) for i in range(4)])
         for k in range(4)
     ]
-    act = call(follow, share, (summed, act), in_specs=[ANY, ANY], out_specs=ANY, input_output_aliases={1: 0}, nbytes=64 << 20)
-    act = lax.all_to_all(act, CHIPS, 0, 0, tiled=True)
-    whole = call(add_z, ((8, 96, 256), BF16), got)
-    whole, act = call(
-        follow, [((8, 96, 256), BF16), share], (whole, act), in_specs=[ANY] * 2, out_specs=[ANY] * 2,
-        input_output_aliases={0: 0, 1: 1},
-    )
-    passed = lax.all_to_all(whole, ("core", "x"), 0, 0, tiled=True)
-    (grad_up, up), (grad_down, down) = [
-        call(
-            weights, [((256, 1024), BF16), ((8, 128), F32)], (left, near, far),
-            flops=2 * TOK * 256 * 1024, nbytes=3 << 20,
-        )
-        for left, near, far in ((layer_input, hg, hg_far), (incoming, act, swap(act, "core")))
-    ]
-    passed = call(finish, ((TOK, 256), BF16), (passed, up, down))
+
+    def gradients(hg, act, x, g):
+        act = lax.all_to_all(act, CHIPS, 0, 0, tiled=True)
+        def gradient(left, near):
+            return call(
+                weights, [((256, 1024), BF16), ((8, 128), F32)], (left, near, swap(near, "core")),
+                flops=2 * TOK * 256 * 1024, nbytes=3 << 20,
+            )
+
+        up, first = gradient(x, hg)
+        act = call(follow, share, (first, act), in_specs=[ANY, ANY], out_specs=ANY, input_output_aliases={1: 0})
+        down, last = gradient(g, act)
+        return up, down, first, last
+
+    def gradients_first(*operands):
+        return gradients(*operands)
+
+    grad_up, grad_down, *after = lax.cond(
+        second, gradients, gradients_first, hg, act, layer_input, incoming
+    )
+    whole = call(add_z, ((8, 96, 256), BF16), (*after, *got))
+
+    def spread_x(whole):
+        return call(finish, ((TOK, 256), BF16), (lax.all_to_all(whole, ("core", "x"), 0, 0, tiled=True),))
+
+    passed = lax.cond(second, lambda _: jnp.zeros((TOK, 256), BF16), spread_x, whole)
     return grad_up, grad_down, passed
 
 

time: 113 us -> 104 us (0.920)
  blocking collectives: 25.6 us -> 12.4 us
  waiting for transfers between devices: 23.7 us -> 33.1 us
  Pallas kernels: 13.1 us -> 9.99 us
  starting transfers between devices: 47.8 us -> 45.7 us
    all_to_all x2, waiting for transfers between devices: 3.71 us -> 22.6 us  [the longest x1 11.6 us: shards(): hg = lax.all_to_all(hg, CHIPS, 0, 0, tiled=True)]
    all_to_all x2 -> x1, blocking collectives: 25.6 us -> 12.4 us  [spread_x(): lax.all_to_all(whole, ('core', 'x'), 0, 0, tiled=True)]
    ppermute x4, waiting for transfers between devices: 10.9 us -> 0.01 us  [shards(): lax.ppermute(summed, ('half', 'zh'), [(4 + i, (i + k) % 4) for i in range...]
    ppermute x5, starting transfers between devices: 21.2 us -> 16.1 us  [swap(): return lax.ppermute(value, axis, [(0, 1), (1, 0)])]
    all_to_all x2, starting transfers between devices: 7.11 us -> 11 us  [the longest x1 6.77 us: shards(): hg = lax.all_to_all(hg, CHIPS, 0, 0, tiled=True)]
    ppermute x5, waiting for transfers between devices: 3.5 us -> 7.28 us  [swap(): return lax.ppermute(value, axis, [(0, 1), (1, 0)])]
    all_to_all x1, waiting for transfers between devices: 5.34 us -> 1.87 us  [shards(): recv = lax.all_to_all(sent, CHIPS, 0, 0, tiled=True)]
    pallas_call x12 -> x8, Pallas kernels: 13.1 us -> 9.99 us  [call(): pl.pallas_call(kernel, out_shape=shapes if many else shapes[0], scratch_s...]
  transfers between devices with their start and end apart: 13 -> 13, of which waited for: 8 -> 8; matrix products, arithmetic and copies ran while one was open for 0% -> 0% of each run, Pallas kernels for 7% -> 6%
where the time goes in v4:
time: 104 us; the launch traced here: 103 us
  starting transfers between devices  45.7 us (44%)
  waiting for transfers between devices  33.1 us (32%)
  blocking collectives  12.4 us (12%)
  Pallas kernels  9.99 us (10%)
  local copies, waits for them, and re-layouts  1.41 us (1%)
    ppermute x5, starting transfers between devices, swap(): return lax.ppermute(value, axis, [(0, 1), (1, 0)])  16.1 us
    all_to_all x1, blocking collectives, spread_x(): lax.all_to_all(whole, ('core', 'x'), 0, 0, tiled=True)  12.4 us
    all_to_all x1, waiting for transfers between devices, shards(): hg = lax.all_to_all(hg, CHIPS, 0, 0, tiled=True)  11.6 us
    all_to_all x1, waiting for transfers between devices, gradients(): act = lax.all_to_all(act, CHIPS, 0, 0, tiled=True)  11.1 us
    pallas_call x8, Pallas kernels, call(): pl.pallas_call(kernel, out_shape=shapes if many else shapes[0], scratch_s...  9.99 us
    all_to_all x1, starting transfers between devices, shards(): packs = lax.all_to_all(packs, ('half',) + CHIPS, 0, 0, tiled=True)  9.33 us
    ppermute x5, waiting for transfers between devices, swap(): return lax.ppermute(value, axis, [(0, 1), (1, 0)])  7.28 us
    all_to_all x1, starting transfers between devices, shards(): hg = lax.all_to_all(hg, CHIPS, 0, 0, tiled=True)  6.77 us
  transfers between devices with their start and end apart: 13, of which 8 were waited for; matrix products, arithmetic and copies ran while one was open for 0% of the time, Pallas kernels for 6%

profile of v4, /device:TPU:1, one launch (start us, length us, event | category | flops | bytes accessed | tf_op | source)
XLA Modules:
  0.0 103.5 jit_solution(14728026193335950055)
XLA Ops:
  0.6 2.3 %shard_map.94 = (bf16[16,64,128]{2,1,0:T(8,128)(2,1)}, bf16[352,1024]{1,0:T(8,128)(2,1)}) custom-call(bf16[48,1024]{1,0:T(8,128)(2,1)} %codes.1, s32[48]{0:T(128)} %rows.1, bf16[48]{0:T(256)(128)(2,1)} %scales.1, bf16[768,256]{1,0:T(8,128)(2,1)} %g.3, bf16[256,1024]{1,0:T(8,128)(2,1)} %v.3), custom_call_target="tpu_custom_call" | custom-call | bytes 3145728 | tf_op jit(solution)/shard_map/pallas_call | solution.py:31
  2.9 0.0 copy-start
  2.9 9.3 %all-to-all-start.5 = ((bf16[16,64,128]{2,1,0:T(8,128)(2,1)}), bf16[16,64,128]{2,1,0:T(8,128)(2,1)S(1)}, u32[]{:S(2)}, u32[]{:S(2)}) async-start(bf16[16,64,128]{2,1,0:T(8,128)(2,1)} %get-tuple-element.66), calls=%async_computation.5 | async-start | bytes 524288 | tf_op jit(solution)/shard_map/all_to_all | solution.py:202
  12.3 3.1 %collective-permute-start.4 = (bf16[352,1024]{1,0:T(8,128)(2,1)}, bf16[352,1024]{1,0:T(8,128)(2,1)S(1)}, u32[]{:S(2)}, u32[]{:S(2)}) collective-permute-start(bf16[352,1024]{1,0:T(8,128)(2,1)} %get-tuple-element.65), channel_id=1, source_target_pairs={{0,16},{16,0},{1,17},{17,1},{2,18},{18,2},{3,19},{19,3},{4,20},{20... | collective-permute-start | bytes 2162696 | tf_op jit(solution)/shard_map/ppermute | solution.py:42
  15.4 2.0 %collective-permute-done.4.far = bf16[352,1024]{1,0:T(8,128)(2,1)S(1)} collective-permute-done((bf16[352,1024]{1,0:T(8,128)(2,1)}, bf16[352,1024]{1,0:T(8,128)(2,1)S(1)}, u32[]{:S(2)}, u32[]{:S(2)}) %collective-permute-start.4) | collective-permute-done | bytes 720928 | tf_op jit(solution)/shard_map/ppermute | solution.py:42
  17.4 0.0 copy-done
  17.4 2.8 %shard_map.95 = bf16[8,384,128]{2,1,0:T(8,128)(2,1)} custom-call(bf16[768,256]{1,0:T(8,128)(2,1)S(1)} %copy-done, bf16[256,1024]{1,0:T(8,128)(2,1)} %v.3, bf16[352,1024]{1,0:T(8,128)(2,1)S(1)} %collective-permute-done.4.far), custom_call_target="tpu_custom_call" | custom-call | tf_op jit(solution)/shard_map/pallas_call | solution.py:31
  20.2 0.0 copy-start.2
  20.2 1.3 %all-to-all-done.5.near = bf16[16,64,128]{2,1,0:T(8,128)(2,1)S(1)} async-done(((bf16[16,64,128]{2,1,0:T(8,128)(2,1)}), bf16[16,64,128]{2,1,0:T(8,128)(2,1)S(1)}, u32[]{:S(2)}, u32[]{:S(2)}) %all-to-all-start.5) | async-done | bytes 262176 | tf_op jit(solution)/shard_map/all_to_all | solution.py:202
  21.5 4.1 %all-to-all-start.4 = ((bf16[8,384,128]{2,1,0:T(8,128)(2,1)}), bf16[8,384,128]{2,1,0:T(8,128)(2,1)S(1)}, u32[]{:S(2)}, u32[]{:S(2)}) async-start(bf16[8,384,128]{2,1,0:T(8,128)(2,1)} %shard_map.95), calls=%async_computation.4 | async-start | bytes 1572864 | tf_op jit(solution)/shard_map/all_to_all | solution.py:214
  25.6 0.0 copy-done.2
  25.6 3.8 %collective-permute-start.6 = (bf16[256,1024]{1,0:T(8,128)(2,1)S(1)}, bf16[256,1024]{1,0:T(8,128)(2,1)S(1)}, u32[]{:S(2)}, u32[]{:S(2)}) collective-permute-start(bf16[256,1024]{1,0:T(8,128)(2,1)S(1)} %copy-done.2), channel_id=1, source_target_pairs={{0,16},{16,0},{1,17},{17,1},{2,18},{18,2},{3,19},{19,3},{4,20},{20... | collective-permute-start | bytes 1572872 | tf_op jit(solution)/shard_map/ppermute | solution.py:42
  29.4 1.9 %collective-permute-start.5 = (bf16[16,64,128]{2,1,0:T(8,128)(2,1)S(1)}, bf16[16,64,128]{2,1,0:T(8,128)(2,1)S(1)}, u32[]{:S(2)}, u32[]{:S(2)}) collective-permute-start(bf16[16,64,128]{2,1,0:T(8,128)(2,1)S(1)} %all-to-all-done.5.near), channel_id=1, source_target_pairs={{0,16},{16,0},{1,17},{17,1},{2,18},{18,2},{3,19},{19,3},{4,20},{20... | collective-permute-start | bytes 786440 | tf_op jit(solution)/shard_map/ppermute | solution.py:42
  31.3 0.0 collective-permute-done.6._
  31.3 1.5 %collective-permute-done.5.far = bf16[16,64,128]{2,1,0:T(8,128)(2,1)S(1)} collective-permute-done((bf16[16,64,128]{2,1,0:T(8,128)(2,1)S(1)}, bf16[16,64,128]{2,1,0:T(8,128)(2,1)S(1)}, u32[]{:S(2)}, u32[]{:S(2)}) %collective-permute-start.5) | collective-permute-done | bytes 262176 | tf_op jit(solution)/shard_map/ppermute | solution.py:42
  32.8 1.9 %all-to-all-done.4.recv = bf16[8,384,128]{2,1,0:T(8,128)(2,1)S(1)} async-done(((bf16[8,384,128]{2,1,0:T(8,128)(2,1)}), bf16[8,384,128]{2,1,0:T(8,128)(2,1)S(1)}, u32[]{:S(2)}, u32[]{:S(2)}) %all-to-all-start.4) | async-done | bytes 786464 | tf_op jit(solution)/shard_map/all_to_all | solution.py:214
  34.7 1.8 %shard_map.96 = (bf16[8,384,128]{2,1,0:T(8,128)(2,1)}, bf16[8,384,128]{2,1,0:T(8,128)(2,1)}) custom-call(bf16[8,384,128]{2,1,0:T(8,128)(2,1)S(1)} %all-to-all-done.4.recv, bf16[16,64,128]{2,1,0:T(8,128)(2,1)S(1)} %all-to-all-done.5.near, bf16[16,64,128]{2,1,0:T(8,128)(2,1)S(1)} %collective-permute-done.5.far, bf16[256,1024]{1,0:T(8,128)(2,1)S(1)} %collective-permute-done.6._), custom_call_target="tpu_custom_call" | custom-call | flops 134217728 | bytes 2097152 | tf_op jit(solution)/shard_map/pallas_call | solution.py:31
  36.5 0.0 copy-start.3
  36.5 6.8 %all-to-all-start.6 = ((bf16[8,384,128]{2,1,0:T(8,128)(2,1)}), bf16[8,384,128]{2,1,0:T(8,128)(2,1)S(1)}, u32[]{:S(2)}, u32[]{:S(2)}) async-start(bf16[8,384,128]{2,1,0:T(8,128)(2,1)} %get-tuple-element.67), calls=%async_computation.6 | async-start | bytes 1572864 | tf_op jit(solution)/shard_map/all_to_all | solution.py:220
  43.3 11.6 %all-to-all-done.6 = bf16[8,384,128]{2,1,0:T(8,128)(2,1)S(1)} async-done(((bf16[8,384,128]{2,1,0:T(8,128)(2,1)}), bf16[8,384,128]{2,1,0:T(8,128)(2,1)S(1)}, u32[]{:S(2)}, u32[]{:S(2)}) %all-to-all-start.6) | async-done | bytes 786464 | tf_op jit(solution)/shard_map/all_to_all | solution.py:220
  54.8 0.0 copy-done.3
  54.8 0.0 copy-start.1
  54.8 0.7 conditional.4
  54.8 0.6 broadcast.4
  55.5 1.3 %collective-permute-start.10 = (bf16[96,512]{1,0:T(8,128)(2,1)}, bf16[96,512]{1,0:T(8,128)(2,1)S(1)}, u32[]{:S(2)}, u32[]{:S(2)}) collective-permute-start(bf16[96,512]{1,0:T(8,128)(2,1)} %get-tuple-element.81), channel_id=1, source_target_pairs={{256,12},{260,0},{264,4},{268,8},{257,13},{261,1},{265,5},{269,9},... | collective-permute-start | bytes 294920 | tf_op jit(solution)/shard_map/ppermute | solution.py:236
  56.8 1.3 %collective-permute-start.9 = (bf16[96,512]{1,0:T(8,128)(2,1)}, bf16[96,512]{1,0:T(8,128)(2,1)S(1)}, u32[]{:S(2)}, u32[]{:S(2)}) collective-permute-start(bf16[96,512]{1,0:T(8,128)(2,1)} %get-tuple-element.81), channel_id=1, source_target_pairs={{256,8},{260,12},{264,0},{268,4},{257,9},{261,13},{265,1},{269,5},... | collective-permute-start | bytes 294920 | tf_op jit(solution)/shard_map/ppermute | solution.py:236
  58.1 1.3 %collective-permute-start.8 = (bf16[96,512]{1,0:T(8,128)(2,1)}, bf16[96,512]{1,0:T(8,128)(2,1)S(1)}, u32[]{:S(2)}, u32[]{:S(2)}) collective-permute-start(bf16[96,512]{1,0:T(8,128)(2,1)} %get-tuple-element.81), channel_id=1, source_target_pairs={{256,4},{260,8},{264,12},{268,0},{257,5},{261,9},{265,13},{269,1},... | collective-permute-start | bytes 294920 | tf_op jit(solution)/shard_map/ppermute | solution.py:236
  59.4 1.3 %collective-permute-start.7 = (bf16[96,512]{1,0:T(8,128)(2,1)}, bf16[96,512]{1,0:T(8,128)(2,1)S(1)}, u32[]{:S(2)}, u32[]{:S(2)}) collective-permute-start(bf16[96,512]{1,0:T(8,128)(2,1)} %get-tuple-element.81), channel_id=1, source_target_pairs={{256,0},{260,4},{264,8},{268,12},{257,1},{261,5},{265,9},{269,13},... | collective-permute-start | bytes 294920 | tf_op jit(solution)/shard_map/ppermute | solution.py:236
  60.7 0.0 copy-done.1
  60.7 29.5 %conditional.3 = (bf16[256,1024]{1,0:T(8,128)(2,1)}, bf16[256,1024]{1,0:T(8,128)(2,1)}, f32[8,128]{1,0:T(8,128)S(1)}, f32[8,128]{1,0:T(8,128)S(1)}) conditional(s32[]{:T(128)} %convert_element_type.2, (bf16[8,384,128]{2,1,0:T(8,128)(2,1)S(1)}, bf16[768,256]{1,0:T(8,128)(2,1)S(1)}, bf16[8,384,128]{2,1,0:T(8,128)(2,1)}, ...), branch_computations={%region_0.0_spmd, %region_1.0_spmd} | conditional | flops 805306368 | bytes 14975176 | solution.py:256
  60.7 4.3 %all-to-all-start = ((bf16[8,384,128]{2,1,0:T(8,128)(2,1)}), bf16[8,384,128]{2,1,0:T(8,128)(2,1)S(1)}, u32[]{:S(2)}, u32[]{:S(2)}) async-start(bf16[8,384,128]{2,1,0:T(8,128)(2,1)} %get-tuple-element.38), calls=%async_computation | async-start | bytes 1572864 | tf_op jit(solution)/shard_map/cond/branch_0_fun/all_to_all | solution.py:241
  65.0 2.7 %collective-permute-start = (bf16[8,384,128]{2,1,0:T(8,128)(2,1)S(1)}, bf16[8,384,128]{2,1,0:T(8,128)(2,1)S(1)}, u32[]{:S(2)}, u32[]{:S(2)}) collective-permute-start(bf16[8,384,128]{2,1,0:T(8,128)(2,1)S(1)} %get-tuple-element.34.near), channel_id=1, source_target_pairs={{0,16},{16,0},{1,17},{17,1},{2,18},{18,2},{3,19},{19,3},{4,20},{20... | collective-permute-start | bytes 2359304 | tf_op jit(solution)/shard_map/cond/branch_0_fun/ppermute | solution.py:42
  67.6 1.9 %collective-permute-done.far = bf16[8,384,128]{2,1,0:T(8,128)(2,1)S(1)} collective-permute-done((bf16[8,384,128]{2,1,0:T(8,128)(2,1)S(1)}, bf16[8,384,128]{2,1,0:T(8,128)(2,1)S(1)}, u32[]{:S(2)}, u32[]{:S(2)}) %collective-permute-start) | collective-permute-done | bytes 786464 | tf_op jit(solution)/shard_map/cond/branch_0_fun/ppermute | solution.py:42
  69.5 1.5 %branch_0_fun.4 = (bf16[256,1024]{1,0:T(8,128)(2,1)}, f32[8,128]{1,0:T(8,128)S(1)}) custom-call(bf16[768,256]{1,0:T(8,128)(2,1)S(1)} %get-tuple-element.32.left, bf16[8,384,128]{2,1,0:T(8,128)(2,1)S(1)} %get-tuple-element.34.near, bf16[8,384,128]{2,1,0:T(8,128)(2,1)S(1)} %collective-permute-done.far), custom_call_target="tpu_custom_call" | custom-call | flops 402653184 | bytes 3145728 | tf_op jit(solution)/shard_map/cond/branch_0_fun/pallas_call | solution.py:31
  71.1 11.1 %all-to-all-done.__1_ = bf16[8,384,128]{2,1,0:T(8,128)(2,1)S(1)} async-done(((bf16[8,384,128]{2,1,0:T(8,128)(2,1)}), bf16[8,384,128]{2,1,0:T(8,128)(2,1)S(1)}, u32[]{:S(2)}, u32[]{:S(2)}) %all-to-all-start) | async-done | bytes 786464 | tf_op jit(solution)/shard_map/cond/branch_0_fun/all_to_all | solution.py:241
  82.2 4.6 %collective-permute-start.1 = (bf16[8,384,128]{2,1,0:T(8,128)(2,1)S(1)}, bf16[8,384,128]{2,1,0:T(8,128)(2,1)S(1)}, u32[]{:S(2)}, u32[]{:S(2)}) collective-permute-start(bf16[8,384,128]{2,1,0:T(8,128)(2,1)S(1)} %branch_0_fun.5.near), channel_id=1, source_target_pairs={{0,16},{16,0},{1,17},{17,1},{2,18},{18,2},{3,19},{19,3},{4,20},{20... | collective-permute-start | bytes 2359304 | tf_op jit(solution)/shard_map/cond/branch_0_fun/ppermute | solution.py:42
  86.8 1.9 %collective-permute-done.1.far = bf16[8,384,128]{2,1,0:T(8,128)(2,1)S(1)} collective-permute-done((bf16[8,384,128]{2,1,0:T(8,128)(2,1)S(1)}, bf16[8,384,128]{2,1,0:T(8,128)(2,1)S(1)}, u32[]{:S(2)}, u32[]{:S(2)}) %collective-permute-start.1) | collective-permute-done | bytes 786464 | tf_op jit(solution)/shard_map/cond/branch_0_fun/ppermute | solution.py:42
  88.6 1.5 %branch_0_fun.6 = (bf16[256,1024]{1,0:T(8,128)(2,1)}, f32[8,128]{1,0:T(8,128)S(1)}) custom-call(bf16[768,256]{1,0:T(8,128)(2,1)S(1)} %get-tuple-element.36.left, bf16[8,384,128]{2,1,0:T(8,128)(2,1)S(1)} %branch_0_fun.5.near, bf16[8,384,128]{2,1,0:T(8,128)(2,1)S(1)} %collective-permute-done.1.far), custom_call_target="tpu_custom_call" | custom-call | flops 402653184 | bytes 3145728 | tf_op jit(solution)/shard_map/cond/branch_0_fun/pallas_call | solution.py:31
  90.2 0.0 collective-permute-done.10.d
  90.2 0.0 collective-permute-done.9.c
  90.2 0.0 collective-permute-done.8.b
  90.2 0.0 collective-permute-done.7.a
  90.2 0.1 shard_map.97
  90.3 12.4 %conditional.5 = (bf16[768,256]{1,0:T(8,128)(2,1)S(1)}) conditional(s32[]{:T(128)} %convert_element_type.2, bf16[8,96,256]{2,1,0:T(8,128)(2,1)S(1)} %shard_map.97, () %tuple.31), branch_computations={%region_4.0_spmd, %region_5.0_spmd} | conditional | bytes 786440 | solution.py:264
  90.3 12.4 %all_to_all.32.blocks = bf16[8,96,256]{2,1,0:T(8,128)(2,1)S(1)} all-to-all(bf16[8,96,256]{2,1,0:T(8,128)(2,1)S(1)} %param.4), channel_id=1, replica_groups=mesh['half'=2,'zb'=2,'y'=4,'core'=2,'zh'=4,'x'=4] {'core','x'}, dimensions={0} | all-to-all | bytes 786432 | tf_op jit(solution)/shard_map/cond/branch_0_fun/all_to_all | solution.py:262
  102.7 0.0 copy-start.4
  102.7 0.7 copy-done.4
  (2 shorter events, 0.0 us)
Async XLA Ops:
  2.9 14.5 %copy-start = (bf16[768,256]{1,0:T(8,128)(2,1)S(1)}, bf16[768,256]{1,0:T(8,128)(2,1)}, u32[]{:S(2)}) copy-start(bf16[768,256]{1,0:T(8,128)(2,1)} %g.3) | copy-start | bytes 1179652
  2.9 18.6 %all-to-all-start.5 = ((bf16[16,64,128]{2,1,0:T(8,128)(2,1)}), bf16[16,64,128]{2,1,0:T(8,128)(2,1)S(1)}, u32[]{:S(2)}, u32[]{:S(2)}) async-start(bf16[16,64,128]{2,1,0:T(8,128)(2,1)} %get-tuple-element.66), calls=%async_computation.5 | async-start | bytes 524288 | tf_op jit(solution)/shard_map/all_to_all | solution.py:202
  12.3 5.1 %collective-permute-start.4 = (bf16[352,1024]{1,0:T(8,128)(2,1)}, bf16[352,1024]{1,0:T(8,128)(2,1)S(1)}, u32[]{:S(2)}, u32[]{:S(2)}) collective-permute-start(bf16[352,1024]{1,0:T(8,128)(2,1)} %get-tuple-element.65), channel_id=1, source_target_pairs={{0,16},{16,0},{1,17},{17,1},{2,18},{18,2},{3,19},{19,3},{4,20},{20... | collective-permute-start | bytes 2162696 | tf_op jit(solution)/shard_map/ppermute | solution.py:42
  20.2 5.4 %copy-start.2 = (bf16[256,1024]{1,0:T(8,128)(2,1)S(1)}, bf16[256,1024]{1,0:T(8,128)(2,1)}, u32[]{:S(2)}) copy-start(bf16[256,1024]{1,0:T(8,128)(2,1)} %param.14) | copy-start | bytes 1572868
  21.5 13.2 %all-to-all-start.4 = ((bf16[8,384,128]{2,1,0:T(8,128)(2,1)}), bf16[8,384,128]{2,1,0:T(8,128)(2,1)S(1)}, u32[]{:S(2)}, u32[]{:S(2)}) async-start(bf16[8,384,128]{2,1,0:T(8,128)(2,1)} %shard_map.95), calls=%async_computation.4 | async-start | bytes 1572864 | tf_op jit(solution)/shard_map/all_to_all | solution.py:214
  25.6 5.7 %collective-permute-start.6 = (bf16[256,1024]{1,0:T(8,128)(2,1)S(1)}, bf16[256,1024]{1,0:T(8,128)(2,1)S(1)}, u32[]{:S(2)}, u32[]{:S(2)}) collective-permute-start(bf16[256,1024]{1,0:T(8,128)(2,1)S(1)} %copy-done.2), channel_id=1, source_target_pairs={{0,16},{16,0},{1,17},{17,1},{2,18},{18,2},{3,19},{19,3},{4,20},{20... | collective-permute-start | bytes 1572872 | tf_op jit(solution)/shard_map/ppermute | solution.py:42
  29.4 3.4 %collective-permute-start.5 = (bf16[16,64,128]{2,1,0:T(8,128)(2,1)S(1)}, bf16[16,64,128]{2,1,0:T(8,128)(2,1)S(1)}, u32[]{:S(2)}, u32[]{:S(2)}) collective-permute-start(bf16[16,64,128]{2,1,0:T(8,128)(2,1)S(1)} %all-to-all-done.5.near), channel_id=1, source_target_pairs={{0,16},{16,0},{1,17},{17,1},{2,18},{18,2},{3,19},{19,3},{4,20},{20... | collective-permute-start | bytes 786440 | tf_op jit(solution)/shard_map/ppermute | solution.py:42
  36.5 18.3 %copy-start.3 = (bf16[256,1024]{1,0:T(8,128)(2,1)S(1)}, bf16[256,1024]{1,0:T(8,128)(2,1)}, u32[]{:S(2)}) copy-start(bf16[256,1024]{1,0:T(8,128)(2,1)} %param.14) | copy-start | bytes 1572868
  36.5 18.3 %all-to-all-start.6 = ((bf16[8,384,128]{2,1,0:T(8,128)(2,1)}), bf16[8,384,128]{2,1,0:T(8,128)(2,1)S(1)}, u32[]{:S(2)}, u32[]{:S(2)}) async-start(bf16[8,384,128]{2,1,0:T(8,128)(2,1)} %get-tuple-element.67), calls=%async_computation.6 | async-start | bytes 1572864 | tf_op jit(solution)/shard_map/all_to_all | solution.py:220
  54.8 5.8 %copy-start.1 = (bf16[768,256]{1,0:T(8,128)(2,1)S(1)}, bf16[768,256]{1,0:T(8,128)(2,1)}, u32[]{:S(2)}) copy-start(bf16[768,256]{1,0:T(8,128)(2,1)} %param.13) | copy-start | bytes 1179652
  55.5 34.7 %collective-permute-start.10 = (bf16[96,512]{1,0:T(8,128)(2,1)}, bf16[96,512]{1,0:T(8,128)(2,1)S(1)}, u32[]{:S(2)}, u32[]{:S(2)}) collective-permute-start(bf16[96,512]{1,0:T(8,128)(2,1)} %get-tuple-element.81), channel_id=1, source_target_pairs={{256,12},{260,0},{264,4},{268,8},{257,13},{261,1},{265,5},{269,9},... | collective-permute-start | bytes 294920 | tf_op jit(solution)/shard_map/ppermute | solution.py:236
  56.8 33.4 %collective-permute-start.9 = (bf16[96,512]{1,0:T(8,128)(2,1)}, bf16[96,512]{1,0:T(8,128)(2,1)S(1)}, u32[]{:S(2)}, u32[]{:S(2)}) collective-permute-start(bf16[96,512]{1,0:T(8,128)(2,1)} %get-tuple-element.81), channel_id=1, source_target_pairs={{256,8},{260,12},{264,0},{268,4},{257,9},{261,13},{265,1},{269,5},... | collective-permute-start | bytes 294920 | tf_op jit(solution)/shard_map/ppermute | solution.py:236
  58.1 32.1 %collective-permute-start.8 = (bf16[96,512]{1,0:T(8,128)(2,1)}, bf16[96,512]{1,0:T(8,128)(2,1)S(1)}, u32[]{:S(2)}, u32[]{:S(2)}) collective-permute-start(bf16[96,512]{1,0:T(8,128)(2,1)} %get-tuple-element.81), channel_id=1, source_target_pairs={{256,4},{260,8},{264,12},{268,0},{257,5},{261,9},{265,13},{269,1},... | collective-permute-start | bytes 294920 | tf_op jit(solution)/shard_map/ppermute | solution.py:236
  59.4 30.8 %collective-permute-start.7 = (bf16[96,512]{1,0:T(8,128)(2,1)}, bf16[96,512]{1,0:T(8,128)(2,1)S(1)}, u32[]{:S(2)}, u32[]{:S(2)}) collective-permute-start(bf16[96,512]{1,0:T(8,128)(2,1)} %get-tuple-element.81), channel_id=1, source_target_pairs={{256,0},{260,4},{264,8},{268,12},{257,1},{261,5},{265,9},{269,13},... | collective-permute-start | bytes 294920 | tf_op jit(solution)/shard_map/ppermute | solution.py:236
  60.7 21.5 %all-to-all-start = ((bf16[8,384,128]{2,1,0:T(8,128)(2,1)}), bf16[8,384,128]{2,1,0:T(8,128)(2,1)S(1)}, u32[]{:S(2)}, u32[]{:S(2)}) async-start(bf16[8,384,128]{2,1,0:T(8,128)(2,1)} %get-tuple-element.38), calls=%async_computation | async-start | bytes 1572864 | tf_op jit(solution)/shard_map/cond/branch_0_fun/all_to_all | solution.py:241
  65.0 4.6 %collective-permute-start = (bf16[8,384,128]{2,1,0:T(8,128)(2,1)S(1)}, bf16[8,384,128]{2,1,0:T(8,128)(2,1)S(1)}, u32[]{:S(2)}, u32[]{:S(2)}) collective-permute-start(bf16[8,384,128]{2,1,0:T(8,128)(2,1)S(1)} %get-tuple-element.34.near), channel_id=1, source_target_pairs={{0,16},{16,0},{1,17},{17,1},{2,18},{18,2},{3,19},{19,3},{4,20},{20... | collective-permute-start | bytes 2359304 | tf_op jit(solution)/shard_map/cond/branch_0_fun/ppermute | solution.py:42
  82.2 6.5 %collective-permute-start.1 = (bf16[8,384,128]{2,1,0:T(8,128)(2,1)S(1)}, bf16[8,384,128]{2,1,0:T(8,128)(2,1)S(1)}, u32[]{:S(2)}, u32[]{:S(2)}) collective-permute-start(bf16[8,384,128]{2,1,0:T(8,128)(2,1)S(1)} %branch_0_fun.5.near), channel_id=1, source_target_pairs={{0,16},{16,0},{1,17},{17,1},{2,18},{18,2},{3,19},{19,3},{4,20},{20... | collective-permute-start | bytes 2359304 | tf_op jit(solution)/shard_map/cond/branch_0_fun/ppermute | solution.py:42
  102.7 0.7 copy-start.4

commit v5 on v4

--- a/solution.py
+++ b/solution.py
@@ -90,28 +90,23 @@
         copy.wait()
 
 
-def front(g, v, far, out, g_held, v_held, far_held, sems):
-    near_at = pl.multiple_of(lax.axis_index("core") * HALF, HALF)
-    copies = [
-        pltpu.make_async_copy(g.at[pl.ds(near_at, HALF), :], g_held, sems.at[0]),
-        pltpu.make_async_copy(v, v_held, sems.at[1]),
-        pltpu.make_async_copy(far, far_held, sems.at[2]),
-    ]
-    for copy in copies:
-        copy.start()
-    for copy in copies:
-        copy.wait()
-    own = g_held[...]
-    other = jnp.concatenate([far_held[256:, 256 * k : 256 * k + 256] for k in range(4)], axis=0)
+def keep(_, g, v, mine, v_kept):
+    mine[...] = g[pl.ds(pl.multiple_of(lax.axis_index("core") * HALF, HALF), HALF), :]
+    v_kept[...] = v[...]
+
+
+def front(g, v, far, out):
+    own = g[...]
+    other = jnp.concatenate([far[256:, 256 * k : 256 * k + 256] for k in range(4)], axis=0)
     for j in range(4):
         cols = slice(256 * j, 256 * j + 256)
-        part = dot(own, v_held[:, cols], 1, 0) + dot(other, far_held[:256, cols], 1, 0)
+        part = dot(own, v[:, cols], 1, 0) + dot(other, far[:256, cols], 1, 0)
         part = part.astype(BF16)
         out[2 * j] = part[:, :128]
         out[2 * j + 1] = part[:, 128:]
 
 
-def slope(recv, near, far, _, grads, activations):
+def slope(recv, near, far, *outs):
     act = recv[0].astype(F32)
     for i in range(1, 8):
         act = act + recv[i].astype(F32)
@@ -135,8 +130,8 @@
     grad = (act * (cumulative + hidden * density)).astype(BF16)
     activated = (hidden * cumulative).astype(BF16)
     for i in range(8):
-        grads[i] = grad
-        activations[i] = activated
+        outs[0][i, :HALF, :] = grad
+        outs[-1][i, -HALF:, :] = activated
 
 
 def input_part(hg, near, far, out):
@@ -148,7 +143,7 @@
     out[:, pl.ds(far_at, 256)] = dot(rows, far[...], 1, 1).astype(BF16)
 
 
-def add_x(recv, g, far, out):
+def add_x(recv, mine, far, out):
     core, x = lax.axis_index("core"), lax.axis_index("x")
     total = recv[0].astype(F32)
     for i in range(1, 4):
@@ -157,7 +152,7 @@
 
     @pl.when(lax.axis_index("zh") == 0)
     def _():
-        own = g[pl.ds(pl.multiple_of(core * HALF + x * 96, 96), 96), :].astype(F32)
+        own = mine[pl.ds(pl.multiple_of(x * 96, 96), 96), :].astype(F32)
         other = far[256:, pl.ds(pl.multiple_of(x * 256, 256), 256)].astype(F32)
         left = jnp.where(core == 0, own, other)
         right = jnp.where(core == 0, other, own)
@@ -170,6 +165,11 @@
     for i in range(4):
         out[i] = total[:, :256]
         out[4 + i] = total[:, 256:]
+
+
+def split(both, first, last):
+    first[...] = both[:, :HALF, :]
+    last[...] = both[:, HALF:, :]
 
 
 def finish(blocks, out):
@@ -199,63 +199,62 @@
         (parked_codes, parked_rows, parked_scales, incoming, w_down), in_specs=[HBM] * 5, nbytes=3 << 20,
         vmem=60, scratch=(pltpu.VMEM((OWN,), jnp.int32), pltpu.VMEM((OWN,), BF16), DMA((15,))),
     )
+    ready = packs
     packs = lax.all_to_all(packs, ("half",) + CHIPS, 0, 0, tiled=True)
     packs_far = swap(packs, "core")
     far = swap(near, "core")
     u_far = swap(w_up, "core")
 
-    sent = call(
-        front, ((8, HALF, 128), BF16), (incoming, w_down, far), in_specs=[HBM] * 3, vmem=60,
-        scratch=(
-            pltpu.VMEM((HALF, 256), BF16), pltpu.VMEM((256, 1024), BF16),
-            pltpu.VMEM((STACK, 1024), BF16), DMA((3,)),
-        ),
+    mine, v = call(
+        keep, [((HALF, 256), BF16), ((256, 1024), BF16)], (ready, incoming, w_down), vmem=24,
+        in_specs=[ANY] + [VMEM] * 2,
     )
+    sent = call(front, ((8, HALF, 128), BF16), (mine, v, far), vmem=24)
     recv = lax.all_to_all(sent, CHIPS, 0, 0, tiled=True)
     share = ((8, HALF, 128), BF16)
-    hg, act = call(
-        slope, [share, share], (recv, packs, packs_far, u_far), flops=1 << 27, nbytes=2 << 20,
-        in_specs=[VMEM] * 3 + [ANY],
-    )
-    hg = lax.all_to_all(hg, CHIPS, 0, 0, tiled=True)
-
+    wide = ((256, 1024), BF16)
     second = lax.axis_index("half") == 1
 
-    def reduce_x(hg, u, u_far, g, far):
+    def to_x(recv, packs, packs_far, u, u_far):
+        hg, act = call(slope, [share, share], (recv, packs, packs_far), flops=1 << 27, nbytes=2 << 20)
+        hg = lax.all_to_all(hg, CHIPS, 0, 0, tiled=True)
         part = call(
             input_part, ((HALF, 512), BF16), (hg, u, u_far),
             flops=2 * HALF * 512 * 1024, nbytes=3 << 20,
         )
-        part = lax.all_to_all(part.reshape(4, 96, 512), "x", 0, 0, tiled=True)
-        return call(add_x, ((96, 512), BF16), (part, g, far), nbytes=1 << 20)
-
-    summed = lax.cond(
-        second, reduce_x, lambda *_: jnp.zeros((96, 512), BF16), hg, w_up, u_far, incoming, far
-    )
+        return lax.all_to_all(part.reshape(4, 96, 512), "x", 0, 0, tiled=True), hg, act
+
+    def gather_both(recv, packs, packs_far, *_):
+        both = call(
+            slope, [((8, 2 * HALF, 128), BF16)], (recv, packs, packs_far), flops=1 << 27, nbytes=2 << 20
+        )[0]
+        both = lax.all_to_all(both, CHIPS, 0, 0, tiled=True)
+        hg, act = call(split, [share, share], (both,))
+        return jnp.zeros((4, 96, 512), BF16), hg, act
+
+    part, hg, act = lax.cond(second, to_x, gather_both, recv, packs, packs_far, w_up, u_far)
+    summed = call(add_x, ((96, 512), BF16), (part, mine, far), nbytes=1 << 20)
     got = [
         lax.ppermute(summed, ("half", "zh"), [(4 + i, (i + k) % 4) for i in range(4)])
         for k in range(4)
     ]
 
+    def gradient(left, near):
+        return call(
+            weights, [wide, ((8, 128), F32)], (left, near, swap(near, "core")),
+            flops=2 * TOK * 256 * 1024, nbytes=3 << 20,
+        )
+
     def gradients(hg, act, x, g):
-        act = lax.all_to_all(act, CHIPS, 0, 0, tiled=True)
-        def gradient(left, near):
-            return call(
-                weights, [((256, 1024), BF16), ((8, 128), F32)], (left, near, swap(near, "core")),
-                flops=2 * TOK * 256 * 1024, nbytes=3 << 20,
-            )
-
         up, first = gradient(x, hg)
         act = call(follow, share, (first, act), in_specs=[ANY, ANY], out_specs=ANY, input_output_aliases={1: 0})
         down, last = gradient(g, act)
         return up, down, first, last
 
-    def gradients_first(*operands):
-        return gradients(*operands)
-
-    grad_up, grad_down, *after = lax.cond(
-        second, gradients, gradients_first, hg, act, layer_input, incoming
-    )
+    def gather_first(hg, act, x, g):
+        return gradients(hg, lax.all_to_all(act, CHIPS, 0, 0, tiled=True), x, g)
+
+    grad_up, grad_down, *after = lax.cond(second, gather_first, gradients, hg, act, layer_input, incoming)
     whole = call(add_z, ((8, 96, 256), BF16), (*after, *got))
 
     def spread_x(whole):

time: 104 us -> 103 us (level)
  blocking collectives: 12.4 us -> 40.3 us
  waiting for transfers between devices: 33.1 us -> 12.5 us
  starting transfers between devices: 45.7 us -> 34.5 us
  Pallas kernels: 9.99 us -> 11.9 us
    all_to_all x0 -> x1, blocking collectives: none -> 25.5 us  [gather_both(): both = lax.all_to_all(both, CHIPS, 0, 0, tiled=True)]
    all_to_all x2 -> x0, waiting for transfers between devices: 22.6 us -> none  [the longest x1 11.6 us: shards(): hg = lax.all_to_all(hg, CHIPS, 0, 0, tiled=True)]
    all_to_all x2 -> x0, starting transfers between devices: 11 us -> none  [the longest x1 6.77 us: shards(): hg = lax.all_to_all(hg, CHIPS, 0, 0, tiled=True)]
    ppermute x4, waiting for transfers between devices: 0.01 us -> 2.51 us  [shards(): lax.ppermute(summed, ('half', 'zh'), [(4 + i, (i + k) % 4) for i in range...]
    all_to_all x1, blocking collectives: 12.4 us -> 14.7 us  [spread_x(): lax.all_to_all(whole, ('core', 'x'), 0, 0, tiled=True)]
    pallas_call x8 -> x11, Pallas kernels: 9.99 us -> 11.9 us  [call(): pl.pallas_call(kernel, out_shape=shapes if many else shapes[0], scratch_s...]
    all_to_all x1, waiting for transfers between devices: 1.3 us -> 2.62 us  [shards(): packs = lax.all_to_all(packs, ('half',) + CHIPS, 0, 0, tiled=True)]
    all_to_all x1, waiting for transfers between devices: 1.87 us -> 0.67 us  [shards(): recv = lax.all_to_all(sent, CHIPS, 0, 0, tiled=True)]
  transfers between devices with their start and end apart: 13 -> 11, of which waited for: 8 -> 8; matrix products, arithmetic and copies ran while one was open for 0% -> 0% of each run, Pallas kernels for 6% -> 7%
where the time goes in v5:
time: 103 us; the launch traced here: 102 us
  blocking collectives  40.3 us (39%)
  starting transfers between devices  34.5 us (33%)
  waiting for transfers between devices  12.5 us (12%)
  Pallas kernels  11.9 us (12%)
  local copies, waits for them, and re-layouts  1.73 us (2%)
    all_to_all x1, blocking collectives, gather_both(): both = lax.all_to_all(both, CHIPS, 0, 0, tiled=True)  25.5 us
    ppermute x5, starting transfers between devices, swap(): return lax.ppermute(value, axis, [(0, 1), (1, 0)])  16.6 us
    all_to_all x1, blocking collectives, spread_x(): lax.all_to_all(whole, ('core', 'x'), 0, 0, tiled=True)  14.7 us
    pallas_call x11, Pallas kernels, call(): pl.pallas_call(kernel, out_shape=shapes if many else shapes[0], scratch_s...  11.9 us
    all_to_all x1, starting transfers between devices, shards(): packs = lax.all_to_all(packs, ('half',) + CHIPS, 0, 0, tiled=True)  9.2 us
    ppermute x5, waiting for transfers between devices, swap(): return lax.ppermute(value, axis, [(0, 1), (1, 0)])  6.68 us
    ppermute x4, starting transfers between devices, shards(): lax.ppermute(summed, ('half', 'zh'), [(4 + i, (i + k) % 4) for i in range...  5.17 us
    all_to_all x1, starting transfers between devices, shards(): recv = lax.all_to_all(sent, CHIPS, 0, 0, tiled=True)  3.55 us
  transfers between devices with their start and end apart: 11, of which 8 were waited for; matrix products, arithmetic and copies ran while one was open for 0% of the time, Pallas kernels for 7%

profile of v5, /device:TPU:1, one launch (start us, length us, event | category | flops | bytes accessed | tf_op | source)
XLA Modules:
  0.0 101.8 jit_solution(17296565044598005720)
XLA Ops:
  0.6 0.0 copy-start.2
  0.6 0.0 copy-start
  0.7 2.3 %shard_map.94 = (bf16[16,64,128]{2,1,0:T(8,128)(2,1)}, bf16[352,1024]{1,0:T(8,128)(2,1)}) custom-call(bf16[48,1024]{1,0:T(8,128)(2,1)} %codes.1, s32[48]{0:T(128)} %rows.1, bf16[48]{0:T(256)(128)(2,1)} %scales.1, bf16[768,256]{1,0:T(8,128)(2,1)} %g.3, bf16[256,1024]{1,0:T(8,128)(2,1)} %v.3), custom_call_target="tpu_custom_call" | custom-call | bytes 3145728 | tf_op jit(solution)/shard_map/pallas_call | solution.py:31
  3.0 9.2 %all-to-all-start.6 = ((bf16[16,64,128]{2,1,0:T(8,128)(2,1)}), bf16[16,64,128]{2,1,0:T(8,128)(2,1)S(1)}, u32[]{:S(2)}, u32[]{:S(2)}) async-start(bf16[16,64,128]{2,1,0:T(8,128)(2,1)} %get-tuple-element.78._), calls=%async_computation.6 | async-start | bytes 524288 | tf_op jit(solution)/shard_map/all_to_all | solution.py:203
  12.2 3.1 %collective-permute-start.4 = (bf16[352,1024]{1,0:T(8,128)(2,1)}, bf16[352,1024]{1,0:T(8,128)(2,1)S(1)}, u32[]{:S(2)}, u32[]{:S(2)}) collective-permute-start(bf16[352,1024]{1,0:T(8,128)(2,1)} %get-tuple-element.81), channel_id=1, source_target_pairs={{0,16},{16,0},{1,17},{17,1},{2,18},{18,2},{3,19},{19,3},{4,20},{20... | collective-permute-start | bytes 2162696 | tf_op jit(solution)/shard_map/ppermute | solution.py:42
  15.4 0.0 copy-done.2
  15.4 0.0 copy-done
  15.4 0.0 copy-start.1
  15.4 0.9 copy-done.1
  16.4 1.0 collective-permute-done.4.far
  17.4 0.0 copy-start.4
  17.4 1.5 %shard_map.96 = bf16[8,384,128]{2,1,0:T(8,128)(2,1)} custom-call(bf16[384,256]{1,0:T(8,128)(2,1)S(1)} %get-tuple-element.79.g.mine, bf16[256,1024]{1,0:T(8,128)(2,1)S(1)} %get-tuple-element.80.v, bf16[352,1024]{1,0:T(8,128)(2,1)S(1)} %collective-permute-done.4.far), custom_call_target="tpu_custom_call" | custom-call | tf_op jit(solution)/shard_map/pallas_call | solution.py:31
  18.8 2.6 %all-to-all-done.6 = bf16[16,64,128]{2,1,0:T(8,128)(2,1)S(1)} async-done(((bf16[16,64,128]{2,1,0:T(8,128)(2,1)}), bf16[16,64,128]{2,1,0:T(8,128)(2,1)S(1)}, u32[]{:S(2)}, u32[]{:S(2)}) %all-to-all-start.6) | async-done | bytes 262176 | tf_op jit(solution)/shard_map/all_to_all | solution.py:203
  21.4 3.5 %all-to-all-start.5 = ((bf16[8,384,128]{2,1,0:T(8,128)(2,1)}), bf16[8,384,128]{2,1,0:T(8,128)(2,1)S(1)}, u32[]{:S(2)}, u32[]{:S(2)}) async-start(bf16[8,384,128]{2,1,0:T(8,128)(2,1)} %shard_map.96), calls=%async_computation.5 | async-start | bytes 1572864 | tf_op jit(solution)/shard_map/all_to_all | solution.py:213
  25.0 0.0 copy-done.4
  25.0 4.3 %collective-permute-start.6 = (bf16[256,1024]{1,0:T(8,128)(2,1)S(1)}, bf16[256,1024]{1,0:T(8,128)(2,1)}, u32[]{:S(2)}, u32[]{:S(2)}) collective-permute-start(bf16[256,1024]{1,0:T(8,128)(2,1)S(1)} %copy-done.4), channel_id=1, source_target_pairs={{0,16},{16,0},{1,17},{17,1},{2,18},{18,2},{3,19},{19,3},{4,20},{20... | collective-permute-start | bytes 1572872 | tf_op jit(solution)/shard_map/ppermute | solution.py:42
  29.3 1.9 %collective-permute-start.5 = (bf16[16,64,128]{2,1,0:T(8,128)(2,1)S(1)}, bf16[16,64,128]{2,1,0:T(8,128)(2,1)S(1)}, u32[]{:S(2)}, u32[]{:S(2)}) collective-permute-start(bf16[16,64,128]{2,1,0:T(8,128)(2,1)S(1)} %all-to-all-done.6), channel_id=1, source_target_pairs={{0,16},{16,0},{1,17},{17,1},{2,18},{18,2},{3,19},{19,3},{4,20},{20... | collective-permute-start | bytes 786440 | tf_op jit(solution)/shard_map/ppermute | solution.py:42
  31.3 1.5 %collective-permute-done.5 = bf16[16,64,128]{2,1,0:T(8,128)(2,1)S(1)} collective-permute-done((bf16[16,64,128]{2,1,0:T(8,128)(2,1)S(1)}, bf16[16,64,128]{2,1,0:T(8,128)(2,1)S(1)}, u32[]{:S(2)}, u32[]{:S(2)}) %collective-permute-start.5) | collective-permute-done | bytes 262176 | tf_op jit(solution)/shard_map/ppermute | solution.py:42
  32.8 0.7 all-to-all-done.5
  33.4 0.0 collective-permute-done.6
  33.4 0.0 copy-start.3
  33.4 27.5 %conditional.3 = (bf16[4,96,512]{2,1,0:T(8,128)(2,1)S(1)}, bf16[8,384,128]{2,1,0:T(8,128)(2,1)}, bf16[8,384,128]{2,1,0:T(8,128)(2,1)}) conditional(s32[]{:T(128)} %convert_element_type.2, (bf16[8,384,128]{2,1,0:T(8,128)(2,1)S(1)}, bf16[16,64,128]{2,1,0:T(8,128)(2,1)S(1)}, bf16[16,64,128]{2,1,0:T(8,128)(2,1)S(1)}) %tuple.30, ...), branch_computations={%region_0.0_spmd, %region_1.0_spmd} | conditional | flops 536870912 | bytes 7602200 | solution.py:235
  33.4 0.6 branch_0_fun.6
  34.0 25.5 %all_to_all.30.both = bf16[8,768,128]{2,1,0:T(8,128)(2,1)S(1)} all-to-all(bf16[8,768,128]{2,1,0:T(8,128)(2,1)S(1)} %branch_0_fun.6), channel_id=1, replica_groups=mesh['half'=2,'zb'=2,'y'=4,'core'=2,'zh'=4,'x'=4] {'zb','y'}, dimensions={0} | all-to-all | bytes 3145728 | tf_op jit(solution)/shard_map/cond/branch_0_fun/all_to_all | solution.py:231
  59.6 1.3 %branch_0_fun.7 = (bf16[8,384,128]{2,1,0:T(8,128)(2,1)}, bf16[8,384,128]{2,1,0:T(8,128)(2,1)}) custom-call(bf16[8,768,128]{2,1,0:T(8,128)(2,1)S(1)} %all_to_all.30.both), custom_call_target="tpu_custom_call" | custom-call | tf_op jit(solution)/shard_map/cond/branch_0_fun/pallas_call | solution.py:31
  60.9 0.1 shard_map.97
  61.0 1.3 %collective-permute-start.10 = (bf16[96,512]{1,0:T(8,128)(2,1)S(1)}, bf16[96,512]{1,0:T(8,128)(2,1)S(1)}, u32[]{:S(2)}, u32[]{:S(2)}) collective-permute-start(bf16[96,512]{1,0:T(8,128)(2,1)S(1)} %shard_map.97), channel_id=1, source_target_pairs={{256,12},{260,0},{264,4},{268,8},{257,13},{261,1},{265,5},{269,9},... | collective-permute-start | bytes 294920 | tf_op jit(solution)/shard_map/ppermute | solution.py:238
  62.3 1.3 %collective-permute-start.9 = (bf16[96,512]{1,0:T(8,128)(2,1)S(1)}, bf16[96,512]{1,0:T(8,128)(2,1)S(1)}, u32[]{:S(2)}, u32[]{:S(2)}) collective-permute-start(bf16[96,512]{1,0:T(8,128)(2,1)S(1)} %shard_map.97), channel_id=1, source_target_pairs={{256,8},{260,12},{264,0},{268,4},{257,9},{261,13},{265,1},{269,5},... | collective-permute-start | bytes 294920 | tf_op jit(solution)/shard_map/ppermute | solution.py:238
  63.6 1.3 %collective-permute-start.8 = (bf16[96,512]{1,0:T(8,128)(2,1)S(1)}, bf16[96,512]{1,0:T(8,128)(2,1)S(1)}, u32[]{:S(2)}, u32[]{:S(2)}) collective-permute-start(bf16[96,512]{1,0:T(8,128)(2,1)S(1)} %shard_map.97), channel_id=1, source_target_pairs={{256,4},{260,8},{264,12},{268,0},{257,5},{261,9},{265,13},{269,1},... | collective-permute-start | bytes 294920 | tf_op jit(solution)/shard_map/ppermute | solution.py:238
  64.9 1.3 %collective-permute-start.7 = (bf16[96,512]{1,0:T(8,128)(2,1)S(1)}, bf16[96,512]{1,0:T(8,128)(2,1)S(1)}, u32[]{:S(2)}, u32[]{:S(2)}) collective-permute-start(bf16[96,512]{1,0:T(8,128)(2,1)S(1)} %shard_map.97), channel_id=1, source_target_pairs={{256,0},{260,4},{264,8},{268,12},{257,1},{261,5},{265,9},{269,13},... | collective-permute-start | bytes 294920 | tf_op jit(solution)/shard_map/ppermute | solution.py:238
  66.2 0.0 copy-done.3
  66.2 16.8 %conditional.4 = (bf16[256,1024]{1,0:T(8,128)(2,1)}, bf16[256,1024]{1,0:T(8,128)(2,1)}, f32[8,128]{1,0:T(8,128)}, f32[8,128]{1,0:T(8,128)S(1)}) conditional(s32[]{:T(128)} %convert_element_type.2, (bf16[8,384,128]{2,1,0:T(8,128)(2,1)}, bf16[768,256]{1,0:T(8,128)(2,1)S(1)}, bf16[8,384,128]{2,1,0:T(8,128)(2,1)}, ...), branch_computations={%region_2.0_spmd, %region_3.0_spmd} | conditional | flops 805306368 | bytes 14942352 | solution.py:257
  66.2 4.9 %collective-permute-start = (bf16[8,384,128]{2,1,0:T(8,128)(2,1)}, bf16[8,384,128]{2,1,0:T(8,128)(2,1)S(1)}, u32[]{:S(2)}, u32[]{:S(2)}) collective-permute-start(bf16[8,384,128]{2,1,0:T(8,128)(2,1)} %get-tuple-element.49.near), channel_id=1, source_target_pairs={{0,16},{16,0},{1,17},{17,1},{2,18},{18,2},{3,19},{19,3},{4,20},{20... | collective-permute-start | bytes 2359304 | tf_op jit(solution)/shard_map/cond/branch_0_fun/ppermute | solution.py:42
  71.2 2.1 %collective-permute-done.far = bf16[8,384,128]{2,1,0:T(8,128)(2,1)S(1)} collective-permute-done((bf16[8,384,128]{2,1,0:T(8,128)(2,1)}, bf16[8,384,128]{2,1,0:T(8,128)(2,1)S(1)}, u32[]{:S(2)}, u32[]{:S(2)}) %collective-permute-start) | collective-permute-done | bytes 786464 | tf_op jit(solution)/shard_map/cond/branch_0_fun/ppermute | solution.py:42
  73.3 2.7 %branch_0_fun.8 = (bf16[256,1024]{1,0:T(8,128)(2,1)}, f32[8,128]{1,0:T(8,128)}) custom-call(bf16[768,256]{1,0:T(8,128)(2,1)S(1)} %get-tuple-element.48.left, bf16[8,384,128]{2,1,0:T(8,128)(2,1)} %get-tuple-element.49.near, bf16[8,384,128]{2,1,0:T(8,128)(2,1)S(1)} %collective-permute-done.far), custom_call_target="tpu_custom_call" | custom-call | flops 402653184 | bytes 3145728 | tf_op jit(solution)/shard_map/cond/branch_0_fun/pallas_call | solution.py:31
  76.0 2.3 %collective-permute-start.1 = (bf16[8,384,128]{2,1,0:T(8,128)(2,1)}, bf16[8,384,128]{2,1,0:T(8,128)(2,1)S(1)}, u32[]{:S(2)}, u32[]{:S(2)}) collective-permute-start(bf16[8,384,128]{2,1,0:T(8,128)(2,1)} %branch_0_fun.9.near), channel_id=1, source_target_pairs={{0,16},{16,0},{1,17},{17,1},{2,18},{18,2},{3,19},{19,3},{4,20},{20... | collective-permute-start | bytes 2359304 | tf_op jit(solution)/shard_map/cond/branch_0_fun/ppermute | solution.py:42
  78.2 2.1 %collective-permute-done.1.far = bf16[8,384,128]{2,1,0:T(8,128)(2,1)S(1)} collective-permute-done((bf16[8,384,128]{2,1,0:T(8,128)(2,1)}, bf16[8,384,128]{2,1,0:T(8,128)(2,1)S(1)}, u32[]{:S(2)}, u32[]{:S(2)}) %collective-permute-start.1) | collective-permute-done | bytes 786464 | tf_op jit(solution)/shard_map/cond/branch_0_fun/ppermute | solution.py:42
  80.3 2.7 %branch_0_fun.10 = (bf16[256,1024]{1,0:T(8,128)(2,1)}, f32[8,128]{1,0:T(8,128)S(1)}) custom-call(bf16[768,256]{1,0:T(8,128)(2,1)S(1)} %get-tuple-element.51.left, bf16[8,384,128]{2,1,0:T(8,128)(2,1)} %branch_0_fun.9.near, bf16[8,384,128]{2,1,0:T(8,128)(2,1)S(1)} %collective-permute-done.1.far), custom_call_target="tpu_custom_call" | custom-call | flops 402653184 | bytes 3145728 | tf_op jit(solution)/shard_map/cond/branch_0_fun/pallas_call | solution.py:31
  83.0 0.0 collective-permute-done.10.d
  83.0 0.3 collective-permute-done.9.c
  83.3 0.0 collective-permute-done.8.b
  83.3 2.2 %collective-permute-done.7.a = bf16[96,512]{1,0:T(8,128)(2,1)S(1)} collective-permute-done((bf16[96,512]{1,0:T(8,128)(2,1)S(1)}, bf16[96,512]{1,0:T(8,128)(2,1)S(1)}, u32[]{:S(2)}, u32[]{:S(2)}) %collective-permute-start.7) | collective-permute-done | bytes 98336 | tf_op jit(solution)/shard_map/ppermute | solution.py:238
  85.5 0.7 shard_map.98
  86.3 14.8 %conditional.5 = (bf16[768,256]{1,0:T(8,128)(2,1)S(1)}) conditional(s32[]{:T(128)} %convert_element_type.2, bf16[8,96,256]{2,1,0:T(8,128)(2,1)S(1)} %shard_map.98, () %tuple.33), branch_computations={%region_4.0_spmd, %region_5.0_spmd} | conditional | bytes 786440 | solution.py:263
  86.3 14.7 %all_to_all.33.blocks = bf16[8,96,256]{2,1,0:T(8,128)(2,1)S(1)} all-to-all(bf16[8,96,256]{2,1,0:T(8,128)(2,1)S(1)} %param.4), channel_id=1, replica_groups=mesh['half'=2,'zb'=2,'y'=4,'core'=2,'zh'=4,'x'=4] {'core','x'}, dimensions={0} | all-to-all | bytes 786432 | tf_op jit(solution)/shard_map/cond/branch_0_fun/all_to_all | solution.py:261
  101.1 0.0 copy-start.5
  101.1 0.7 copy-done.5
  (4 shorter events, 0.1 us)
Async XLA Ops:
  0.6 14.7 %copy-start.2 = (bf16[768,256]{1,0:T(8,128)(2,1)S(1)}, bf16[768,256]{1,0:T(8,128)(2,1)}, u32[]{:S(2)}) copy-start(bf16[768,256]{1,0:T(8,128)(2,1)} %g.3) | copy-start | bytes 1179652
  0.6 14.7 %copy-start = (bf16[256,1024]{1,0:T(8,128)(2,1)S(1)}, bf16[256,1024]{1,0:T(8,128)(2,1)}, u32[]{:S(2)}) copy-start(bf16[256,1024]{1,0:T(8,128)(2,1)} %v.3) | copy-start | bytes 1572868
  3.0 18.4 %all-to-all-start.6 = ((bf16[16,64,128]{2,1,0:T(8,128)(2,1)}), bf16[16,64,128]{2,1,0:T(8,128)(2,1)S(1)}, u32[]{:S(2)}, u32[]{:S(2)}) async-start(bf16[16,64,128]{2,1,0:T(8,128)(2,1)} %get-tuple-element.78._), calls=%async_computation.6 | async-start | bytes 524288 | tf_op jit(solution)/shard_map/all_to_all | solution.py:203
  12.2 5.1 %collective-permute-start.4 = (bf16[352,1024]{1,0:T(8,128)(2,1)}, bf16[352,1024]{1,0:T(8,128)(2,1)S(1)}, u32[]{:S(2)}, u32[]{:S(2)}) collective-permute-start(bf16[352,1024]{1,0:T(8,128)(2,1)} %get-tuple-element.81), channel_id=1, source_target_pairs={{0,16},{16,0},{1,17},{17,1},{2,18},{18,2},{3,19},{19,3},{4,20},{20... | collective-permute-start | bytes 2162696 | tf_op jit(solution)/shard_map/ppermute | solution.py:42
  15.4 1.0 copy-start.1
  17.4 7.6 %copy-start.4 = (bf16[256,1024]{1,0:T(8,128)(2,1)S(1)}, bf16[256,1024]{1,0:T(8,128)(2,1)}, u32[]{:S(2)}) copy-start(bf16[256,1024]{1,0:T(8,128)(2,1)} %param.14) | copy-start | bytes 1572868
  21.4 12.0 %all-to-all-start.5 = ((bf16[8,384,128]{2,1,0:T(8,128)(2,1)}), bf16[8,384,128]{2,1,0:T(8,128)(2,1)S(1)}, u32[]{:S(2)}, u32[]{:S(2)}) async-start(bf16[8,384,128]{2,1,0:T(8,128)(2,1)} %shard_map.96), calls=%async_computation.5 | async-start | bytes 1572864 | tf_op jit(solution)/shard_map/all_to_all | solution.py:213
  25.0 8.4 %collective-permute-start.6 = (bf16[256,1024]{1,0:T(8,128)(2,1)S(1)}, bf16[256,1024]{1,0:T(8,128)(2,1)}, u32[]{:S(2)}, u32[]{:S(2)}) collective-permute-start(bf16[256,1024]{1,0:T(8,128)(2,1)S(1)} %copy-done.4), channel_id=1, source_target_pairs={{0,16},{16,0},{1,17},{17,1},{2,18},{18,2},{3,19},{19,3},{4,20},{20... | collective-permute-start | bytes 1572872 | tf_op jit(solution)/shard_map/ppermute | solution.py:42
  29.3 3.4 %collective-permute-start.5 = (bf16[16,64,128]{2,1,0:T(8,128)(2,1)S(1)}, bf16[16,64,128]{2,1,0:T(8,128)(2,1)S(1)}, u32[]{:S(2)}, u32[]{:S(2)}) collective-permute-start(bf16[16,64,128]{2,1,0:T(8,128)(2,1)S(1)} %all-to-all-done.6), channel_id=1, source_target_pairs={{0,16},{16,0},{1,17},{17,1},{2,18},{18,2},{3,19},{19,3},{4,20},{20... | collective-permute-start | bytes 786440 | tf_op jit(solution)/shard_map/ppermute | solution.py:42
  33.4 32.8 %copy-start.3 = (bf16[768,256]{1,0:T(8,128)(2,1)S(1)}, bf16[768,256]{1,0:T(8,128)(2,1)}, u32[]{:S(2)}) copy-start(bf16[768,256]{1,0:T(8,128)(2,1)} %param.13) | copy-start | bytes 1179652
  61.0 22.0 %collective-permute-start.10 = (bf16[96,512]{1,0:T(8,128)(2,1)S(1)}, bf16[96,512]{1,0:T(8,128)(2,1)S(1)}, u32[]{:S(2)}, u32[]{:S(2)}) collective-permute-start(bf16[96,512]{1,0:T(8,128)(2,1)S(1)} %shard_map.97), channel_id=1, source_target_pairs={{256,12},{260,0},{264,4},{268,8},{257,13},{261,1},{265,5},{269,9},... | collective-permute-start | bytes 294920 | tf_op jit(solution)/shard_map/ppermute | solution.py:238
  62.3 21.0 %collective-permute-start.9 = (bf16[96,512]{1,0:T(8,128)(2,1)S(1)}, bf16[96,512]{1,0:T(8,128)(2,1)S(1)}, u32[]{:S(2)}, u32[]{:S(2)}) collective-permute-start(bf16[96,512]{1,0:T(8,128)(2,1)S(1)} %shard_map.97), channel_id=1, source_target_pairs={{256,8},{260,12},{264,0},{268,4},{257,9},{261,13},{265,1},{269,5},... | collective-permute-start | bytes 294920 | tf_op jit(solution)/shard_map/ppermute | solution.py:238
  63.6 19.7 %collective-permute-start.8 = (bf16[96,512]{1,0:T(8,128)(2,1)S(1)}, bf16[96,512]{1,0:T(8,128)(2,1)S(1)}, u32[]{:S(2)}, u32[]{:S(2)}) collective-permute-start(bf16[96,512]{1,0:T(8,128)(2,1)S(1)} %shard_map.97), channel_id=1, source_target_pairs={{256,4},{260,8},{264,12},{268,0},{257,5},{261,9},{265,13},{269,1},... | collective-permute-start | bytes 294920 | tf_op jit(solution)/shard_map/ppermute | solution.py:238
  64.9 20.6 %collective-permute-start.7 = (bf16[96,512]{1,0:T(8,128)(2,1)S(1)}, bf16[96,512]{1,0:T(8,128)(2,1)S(1)}, u32[]{:S(2)}, u32[]{:S(2)}) collective-permute-start(bf16[96,512]{1,0:T(8,128)(2,1)S(1)} %shard_map.97), channel_id=1, source_target_pairs={{256,0},{260,4},{264,8},{268,12},{257,1},{261,5},{265,9},{269,13},... | collective-permute-start | bytes 294920 | tf_op jit(solution)/shard_map/ppermute | solution.py:238
  66.2 7.1 %collective-permute-start = (bf16[8,384,128]{2,1,0:T(8,128)(2,1)}, bf16[8,384,128]{2,1,0:T(8,128)(2,1)S(1)}, u32[]{:S(2)}, u32[]{:S(2)}) collective-permute-start(bf16[8,384,128]{2,1,0:T(8,128)(2,1)} %get-tuple-element.49.near), channel_id=1, source_target_pairs={{0,16},{16,0},{1,17},{17,1},{2,18},{18,2},{3,19},{19,3},{4,20},{20... | collective-permute-start | bytes 2359304 | tf_op jit(solution)/shard_map/cond/branch_0_fun/ppermute | solution.py:42
  76.0 4.4 %collective-permute-start.1 = (bf16[8,384,128]{2,1,0:T(8,128)(2,1)}, bf16[8,384,128]{2,1,0:T(8,128)(2,1)S(1)}, u32[]{:S(2)}, u32[]{:S(2)}) collective-permute-start(bf16[8,384,128]{2,1,0:T(8,128)(2,1)} %branch_0_fun.9.near), channel_id=1, source_target_pairs={{0,16},{16,0},{1,17},{17,1},{2,18},{18,2},{3,19},{19,3},{4,20},{20... | collective-permute-start | bytes 2359304 | tf_op jit(solution)/shard_map/cond/branch_0_fun/ppermute | solution.py:42
  101.1 0.7 copy-start.5

commit v6 on v5

--- a/solution.py
+++ b/solution.py
@@ -255,12 +255,13 @@
         return gradients(hg, lax.all_to_all(act, CHIPS, 0, 0, tiled=True), x, g)
 
     grad_up, grad_down, *after = lax.cond(second, gather_first, gradients, hg, act, layer_input, incoming)
-    whole = call(add_z, ((8, 96, 256), BF16), (*after, *got))
-
-    def spread_x(whole):
-        return call(finish, ((TOK, 256), BF16), (lax.all_to_all(whole, ("core", "x"), 0, 0, tiled=True),))
-
-    passed = lax.cond(second, lambda _: jnp.zeros((TOK, 256), BF16), spread_x, whole)
+
+    def spread_x(after, got):
+        whole = call(add_z, ((8, 96, 256), BF16), (*after, *got), in_specs=[ANY] * 2 + [VMEM] * 4)
+        passed = lax.all_to_all(whole, ("core", "x"), 0, 0, tiled=True)
+        return call(finish, ((TOK, 256), BF16), (passed,))
+
+    passed = lax.cond(second, lambda *_: jnp.zeros((TOK, 256), BF16), spread_x, after, got)
     return grad_up, grad_down, passed
 
 

time: 103 us -> 102 us (level)
  no operation moved by 1% of the time
where the time goes in v6:
time: 102 us; the launch traced here: 101 us
  blocking collectives  40.2 us (39%)
  starting transfers between devices  34.5 us (34%)
  waiting for transfers between devices  12.6 us (12%)
  Pallas kernels  11.2 us (11%)
  local copies, waits for them, and re-layouts  1.73 us (2%)
    all_to_all x1, blocking collectives, gather_both(): both = lax.all_to_all(both, CHIPS, 0, 0, tiled=True)  25.5 us
    ppermute x5, starting transfers between devices, swap(): return lax.ppermute(value, axis, [(0, 1), (1, 0)])  16.6 us
    all_to_all x1, blocking collectives, spread_x(): passed = lax.all_to_all(whole, ('core', 'x'), 0, 0, tiled=True)  14.7 us
    pallas_call x11, Pallas kernels, call(): pl.pallas_call(kernel, out_shape=shapes if many else shapes[0], scratch_s...  11.2 us
    all_to_all x1, starting transfers between devices, shards(): packs = lax.all_to_all(packs, ('half',) + CHIPS, 0, 0, tiled=True)  9.2 us
    ppermute x5, waiting for transfers between devices, swap(): return lax.ppermute(value, axis, [(0, 1), (1, 0)])  6.68 us
    ppermute x4, starting transfers between devices, shards(): lax.ppermute(summed, ('half', 'zh'), [(4 + i, (i + k) % 4) for i in range...  5.17 us
    all_to_all x1, starting transfers between devices, shards(): recv = lax.all_to_all(sent, CHIPS, 0, 0, tiled=True)  3.55 us
  transfers between devices with their start and end apart: 11, of which 8 were waited for; matrix products, arithmetic and copies ran while one was open for 0% of the time, Pallas kernels for 7%

profile of v6, /device:TPU:1, one launch (start us, length us, event | category | flops | bytes accessed | tf_op | source)
XLA Modules:
  0.0 101.2 jit_solution(7118865890825112611)
XLA Ops:
  0.6 0.0 copy-start.2
  0.6 0.0 copy-start
  0.7 2.3 %shard_map.94 = (bf16[16,64,128]{2,1,0:T(8,128)(2,1)}, bf16[352,1024]{1,0:T(8,128)(2,1)}) custom-call(bf16[48,1024]{1,0:T(8,128)(2,1)} %codes.1, s32[48]{0:T(128)} %rows.1, bf16[48]{0:T(256)(128)(2,1)} %scales.1, bf16[768,256]{1,0:T(8,128)(2,1)} %g.3, bf16[256,1024]{1,0:T(8,128)(2,1)} %v.3), custom_call_target="tpu_custom_call" | custom-call | bytes 3145728 | tf_op jit(solution)/shard_map/pallas_call | solution.py:31
  3.0 9.2 %all-to-all-start.6 = ((bf16[16,64,128]{2,1,0:T(8,128)(2,1)}), bf16[16,64,128]{2,1,0:T(8,128)(2,1)S(1)}, u32[]{:S(2)}, u32[]{:S(2)}) async-start(bf16[16,64,128]{2,1,0:T(8,128)(2,1)} %get-tuple-element.95._), calls=%async_computation.6 | async-start | bytes 524288 | tf_op jit(solution)/shard_map/all_to_all | solution.py:203
  12.2 3.1 %collective-permute-start.4 = (bf16[352,1024]{1,0:T(8,128)(2,1)}, bf16[352,1024]{1,0:T(8,128)(2,1)S(1)}, u32[]{:S(2)}, u32[]{:S(2)}) collective-permute-start(bf16[352,1024]{1,0:T(8,128)(2,1)} %get-tuple-element.98), channel_id=1, source_target_pairs={{0,16},{16,0},{1,17},{17,1},{2,18},{18,2},{3,19},{19,3},{4,20},{20... | collective-permute-start | bytes 2162696 | tf_op jit(solution)/shard_map/ppermute | solution.py:42
  15.4 0.0 copy-done.2
  15.4 0.0 copy-done
  15.4 0.0 copy-start.1
  15.4 0.9 copy-done.1
  16.4 1.0 collective-permute-done.4.far
  17.4 1.5 %shard_map.96 = bf16[8,384,128]{2,1,0:T(8,128)(2,1)} custom-call(bf16[384,256]{1,0:T(8,128)(2,1)S(1)} %get-tuple-element.96.g.mine, bf16[256,1024]{1,0:T(8,128)(2,1)S(1)} %get-tuple-element.97.v, bf16[352,1024]{1,0:T(8,128)(2,1)S(1)} %collective-permute-done.4.far), custom_call_target="tpu_custom_call" | custom-call | tf_op jit(solution)/shard_map/pallas_call | solution.py:31
  18.8 2.6 %all-to-all-done.6 = bf16[16,64,128]{2,1,0:T(8,128)(2,1)S(1)} async-done(((bf16[16,64,128]{2,1,0:T(8,128)(2,1)}), bf16[16,64,128]{2,1,0:T(8,128)(2,1)S(1)}, u32[]{:S(2)}, u32[]{:S(2)}) %all-to-all-start.6) | async-done | bytes 262176 | tf_op jit(solution)/shard_map/all_to_all | solution.py:203
  21.4 3.5 %all-to-all-start.5 = ((bf16[8,384,128]{2,1,0:T(8,128)(2,1)}), bf16[8,384,128]{2,1,0:T(8,128)(2,1)S(1)}, u32[]{:S(2)}, u32[]{:S(2)}) async-start(bf16[8,384,128]{2,1,0:T(8,128)(2,1)} %shard_map.96), calls=%async_computation.5 | async-start | bytes 1572864 | tf_op jit(solution)/shard_map/all_to_all | solution.py:213
  25.0 4.3 %collective-permute-start.6 = (bf16[256,1024]{1,0:T(8,128)(2,1)}, bf16[256,1024]{1,0:T(8,128)(2,1)}, u32[]{:S(2)}, u32[]{:S(2)}) collective-permute-start(bf16[256,1024]{1,0:T(8,128)(2,1)} %param.14), channel_id=1, source_target_pairs={{0,16},{16,0},{1,17},{17,1},{2,18},{18,2},{3,19},{19,3},{4,20},{20... | collective-permute-start | bytes 1572872 | tf_op jit(solution)/shard_map/ppermute | solution.py:42
  29.3 1.9 %collective-permute-start.5 = (bf16[16,64,128]{2,1,0:T(8,128)(2,1)S(1)}, bf16[16,64,128]{2,1,0:T(8,128)(2,1)S(1)}, u32[]{:S(2)}, u32[]{:S(2)}) collective-permute-start(bf16[16,64,128]{2,1,0:T(8,128)(2,1)S(1)} %all-to-all-done.6), channel_id=1, source_target_pairs={{0,16},{16,0},{1,17},{17,1},{2,18},{18,2},{3,19},{19,3},{4,20},{20... | collective-permute-start | bytes 786440 | tf_op jit(solution)/shard_map/ppermute | solution.py:42
  31.3 1.5 %collective-permute-done.5 = bf16[16,64,128]{2,1,0:T(8,128)(2,1)S(1)} collective-permute-done((bf16[16,64,128]{2,1,0:T(8,128)(2,1)S(1)}, bf16[16,64,128]{2,1,0:T(8,128)(2,1)S(1)}, u32[]{:S(2)}, u32[]{:S(2)}) %collective-permute-start.5) | collective-permute-done | bytes 262176 | tf_op jit(solution)/shard_map/ppermute | solution.py:42
  32.7 0.7 all-to-all-done.5
  33.4 0.0 collective-permute-done.6
  33.4 0.0 copy-start.3
  33.4 27.5 %conditional.3 = (bf16[4,96,512]{2,1,0:T(8,128)(2,1)S(1)}, bf16[8,384,128]{2,1,0:T(8,128)(2,1)}, bf16[8,384,128]{2,1,0:T(8,128)(2,1)}) conditional(s32[]{:T(128)} %convert_element_type.2, (bf16[8,384,128]{2,1,0:T(8,128)(2,1)S(1)}, bf16[16,64,128]{2,1,0:T(8,128)(2,1)S(1)}, bf16[16,64,128]{2,1,0:T(8,128)(2,1)S(1)}) %tuple.30, ...), branch_computations={%region_0.0_spmd, %region_1.0_spmd} | conditional | flops 536870912 | bytes 7602200 | solution.py:235
  33.4 0.6 branch_0_fun.7
  34.0 25.5 %all_to_all.30.both = bf16[8,768,128]{2,1,0:T(8,128)(2,1)S(1)} all-to-all(bf16[8,768,128]{2,1,0:T(8,128)(2,1)S(1)} %branch_0_fun.7), channel_id=1, replica_groups=mesh['half'=2,'zb'=2,'y'=4,'core'=2,'zh'=4,'x'=4] {'zb','y'}, dimensions={0} | all-to-all | bytes 3145728 | tf_op jit(solution)/shard_map/cond/branch_0_fun/all_to_all | solution.py:231
  59.6 1.3 %branch_0_fun.8 = (bf16[8,384,128]{2,1,0:T(8,128)(2,1)}, bf16[8,384,128]{2,1,0:T(8,128)(2,1)}) custom-call(bf16[8,768,128]{2,1,0:T(8,128)(2,1)S(1)} %all_to_all.30.both), custom_call_target="tpu_custom_call" | custom-call | tf_op jit(solution)/shard_map/cond/branch_0_fun/pallas_call | solution.py:31
  60.9 0.1 shard_map.97
  61.0 1.3 %collective-permute-start.10 = (bf16[96,512]{1,0:T(8,128)(2,1)S(1)}, bf16[96,512]{1,0:T(8,128)(2,1)S(1)}, u32[]{:S(2)}, u32[]{:S(2)}) collective-permute-start(bf16[96,512]{1,0:T(8,128)(2,1)S(1)} %shard_map.97), channel_id=1, source_target_pairs={{256,12},{260,0},{264,4},{268,8},{257,13},{261,1},{265,5},{269,9},... | collective-permute-start | bytes 294920 | tf_op jit(solution)/shard_map/ppermute | solution.py:238
  62.3 1.3 %collective-permute-start.9 = (bf16[96,512]{1,0:T(8,128)(2,1)S(1)}, bf16[96,512]{1,0:T(8,128)(2,1)S(1)}, u32[]{:S(2)}, u32[]{:S(2)}) collective-permute-start(bf16[96,512]{1,0:T(8,128)(2,1)S(1)} %shard_map.97), channel_id=1, source_target_pairs={{256,8},{260,12},{264,0},{268,4},{257,9},{261,13},{265,1},{269,5},... | collective-permute-start | bytes 294920 | tf_op jit(solution)/shard_map/ppermute | solution.py:238
  63.6 1.3 %collective-permute-start.8 = (bf16[96,512]{1,0:T(8,128)(2,1)S(1)}, bf16[96,512]{1,0:T(8,128)(2,1)S(1)}, u32[]{:S(2)}, u32[]{:S(2)}) collective-permute-start(bf16[96,512]{1,0:T(8,128)(2,1)S(1)} %shard_map.97), channel_id=1, source_target_pairs={{256,4},{260,8},{264,12},{268,0},{257,5},{261,9},{265,13},{269,1},... | collective-permute-start | bytes 294920 | tf_op jit(solution)/shard_map/ppermute | solution.py:238
  64.9 1.3 %collective-permute-start.7 = (bf16[96,512]{1,0:T(8,128)(2,1)S(1)}, bf16[96,512]{1,0:T(8,128)(2,1)S(1)}, u32[]{:S(2)}, u32[]{:S(2)}) collective-permute-start(bf16[96,512]{1,0:T(8,128)(2,1)S(1)} %shard_map.97), channel_id=1, source_target_pairs={{256,0},{260,4},{264,8},{268,12},{257,1},{261,5},{265,9},{269,13},... | collective-permute-start | bytes 294920 | tf_op jit(solution)/shard_map/ppermute | solution.py:238
  66.2 0.0 copy-done.3
  66.2 16.8 %conditional.4 = (bf16[256,1024]{1,0:T(8,128)(2,1)}, bf16[256,1024]{1,0:T(8,128)(2,1)}, f32[8,128]{1,0:T(8,128)}, f32[8,128]{1,0:T(8,128)S(1)}) conditional(s32[]{:T(128)} %convert_element_type.2, (bf16[8,384,128]{2,1,0:T(8,128)(2,1)}, bf16[768,256]{1,0:T(8,128)(2,1)S(1)}, bf16[8,384,128]{2,1,0:T(8,128)(2,1)}, ...), branch_computations={%region_2.0_spmd, %region_3.0_spmd} | conditional | flops 805306368 | bytes 14942352 | solution.py:257
  66.2 4.9 %collective-permute-start = (bf16[8,384,128]{2,1,0:T(8,128)(2,1)}, bf16[8,384,128]{2,1,0:T(8,128)(2,1)S(1)}, u32[]{:S(2)}, u32[]{:S(2)}) collective-permute-start(bf16[8,384,128]{2,1,0:T(8,128)(2,1)} %get-tuple-element.60.near), channel_id=1, source_target_pairs={{0,16},{16,0},{1,17},{17,1},{2,18},{18,2},{3,19},{19,3},{4,20},{20... | collective-permute-start | bytes 2359304 | tf_op jit(solution)/shard_map/cond/branch_0_fun/ppermute | solution.py:42
  71.2 2.1 %collective-permute-done.far = bf16[8,384,128]{2,1,0:T(8,128)(2,1)S(1)} collective-permute-done((bf16[8,384,128]{2,1,0:T(8,128)(2,1)}, bf16[8,384,128]{2,1,0:T(8,128)(2,1)S(1)}, u32[]{:S(2)}, u32[]{:S(2)}) %collective-permute-start) | collective-permute-done | bytes 786464 | tf_op jit(solution)/shard_map/cond/branch_0_fun/ppermute | solution.py:42
  73.3 2.7 %branch_0_fun.9 = (bf16[256,1024]{1,0:T(8,128)(2,1)}, f32[8,128]{1,0:T(8,128)}) custom-call(bf16[768,256]{1,0:T(8,128)(2,1)S(1)} %get-tuple-element.59.left, bf16[8,384,128]{2,1,0:T(8,128)(2,1)} %get-tuple-element.60.near, bf16[8,384,128]{2,1,0:T(8,128)(2,1)S(1)} %collective-permute-done.far), custom_call_target="tpu_custom_call" | custom-call | flops 402653184 | bytes 3145728 | tf_op jit(solution)/shard_map/cond/branch_0_fun/pallas_call | solution.py:31
  76.0 2.3 %collective-permute-start.1 = (bf16[8,384,128]{2,1,0:T(8,128)(2,1)}, bf16[8,384,128]{2,1,0:T(8,128)(2,1)S(1)}, u32[]{:S(2)}, u32[]{:S(2)}) collective-permute-start(bf16[8,384,128]{2,1,0:T(8,128)(2,1)} %branch_0_fun.10.near), channel_id=1, source_target_pairs={{0,16},{16,0},{1,17},{17,1},{2,18},{18,2},{3,19},{19,3},{4,20},{20... | collective-permute-start | bytes 2359304 | tf_op jit(solution)/shard_map/cond/branch_0_fun/ppermute | solution.py:42
  78.2 2.1 %collective-permute-done.1.far = bf16[8,384,128]{2,1,0:T(8,128)(2,1)S(1)} collective-permute-done((bf16[8,384,128]{2,1,0:T(8,128)(2,1)}, bf16[8,384,128]{2,1,0:T(8,128)(2,1)S(1)}, u32[]{:S(2)}, u32[]{:S(2)}) %collective-permute-start.1) | collective-permute-done | bytes 786464 | tf_op jit(solution)/shard_map/cond/branch_0_fun/ppermute | solution.py:42
  80.3 2.7 %branch_0_fun.11 = (bf16[256,1024]{1,0:T(8,128)(2,1)}, f32[8,128]{1,0:T(8,128)S(1)}) custom-call(bf16[768,256]{1,0:T(8,128)(2,1)S(1)} %get-tuple-element.62.left, bf16[8,384,128]{2,1,0:T(8,128)(2,1)} %branch_0_fun.10.near, bf16[8,384,128]{2,1,0:T(8,128)(2,1)S(1)} %collective-permute-done.1.far), custom_call_target="tpu_custom_call" | custom-call | flops 402653184 | bytes 3145728 | tf_op jit(solution)/shard_map/cond/branch_0_fun/pallas_call | solution.py:31
  83.0 0.0 collective-permute-done.10
  83.0 0.6 collective-permute-done.9
  83.6 0.0 collective-permute-done.8
  83.6 2.1 %collective-permute-done.7 = bf16[96,512]{1,0:T(8,128)(2,1)S(1)} collective-permute-done((bf16[96,512]{1,0:T(8,128)(2,1)S(1)}, bf16[96,512]{1,0:T(8,128)(2,1)S(1)}, u32[]{:S(2)}, u32[]{:S(2)}) %collective-permute-start.7) | collective-permute-done | bytes 98336 | tf_op jit(solution)/shard_map/ppermute | solution.py:238
  85.7 14.8 %conditional.5 = (bf16[768,256]{1,0:T(8,128)(2,1)S(1)}) conditional(s32[]{:T(128)} %convert_element_type.2, (f32[8,128]{1,0:T(8,128)}, f32[8,128]{1,0:T(8,128)S(1)}, bf16[96,512]{1,0:T(8,128)(2,1)S(1)}, bf16[96,512]{1,0:T(8,128)(2,1)S(1)}, bf16[96,512]{1,0:T(8,128)(2,1)S(1)}, /*index=5*/bf16[96,512]{1,0:T(8,128)(2,1)S(1)}) %tuple.33, () %tuple.34), branch_computations={%region_4.0_spmd, %region_5.0_spmd} | conditional | bytes 786440 | solution.py:264
  85.7 0.1 branch_0_fun.12
  85.7 14.7 %all_to_all.33.blocks = bf16[8,96,256]{2,1,0:T(8,128)(2,1)S(1)} all-to-all(bf16[8,96,256]{2,1,0:T(8,128)(2,1)S(1)} %branch_0_fun.12), channel_id=1, replica_groups=mesh['half'=2,'zb'=2,'y'=4,'core'=2,'zh'=4,'x'=4] {'core','x'}, dimensions={0} | all-to-all | bytes 786432 | tf_op jit(solution)/shard_map/cond/branch_0_fun/all_to_all | solution.py:261
  100.4 0.0 copy-start.4
  100.5 0.7 copy-done.4
  (4 shorter events, 0.1 us)
Async XLA Ops:
  0.6 14.7 %copy-start.2 = (bf16[768,256]{1,0:T(8,128)(2,1)S(1)}, bf16[768,256]{1,0:T(8,128)(2,1)}, u32[]{:S(2)}) copy-start(bf16[768,256]{1,0:T(8,128)(2,1)} %g.3) | copy-start | bytes 1179652
  0.6 14.7 %copy-start = (bf16[256,1024]{1,0:T(8,128)(2,1)S(1)}, bf16[256,1024]{1,0:T(8,128)(2,1)}, u32[]{:S(2)}) copy-start(bf16[256,1024]{1,0:T(8,128)(2,1)} %v.3) | copy-start | bytes 1572868
  3.0 18.4 %all-to-all-start.6 = ((bf16[16,64,128]{2,1,0:T(8,128)(2,1)}), bf16[16,64,128]{2,1,0:T(8,128)(2,1)S(1)}, u32[]{:S(2)}, u32[]{:S(2)}) async-start(bf16[16,64,128]{2,1,0:T(8,128)(2,1)} %get-tuple-element.95._), calls=%async_computation.6 | async-start | bytes 524288 | tf_op jit(solution)/shard_map/all_to_all | solution.py:203
  12.2 5.1 %collective-permute-start.4 = (bf16[352,1024]{1,0:T(8,128)(2,1)}, bf16[352,1024]{1,0:T(8,128)(2,1)S(1)}, u32[]{:S(2)}, u32[]{:S(2)}) collective-permute-start(bf16[352,1024]{1,0:T(8,128)(2,1)} %get-tuple-element.98), channel_id=1, source_target_pairs={{0,16},{16,0},{1,17},{17,1},{2,18},{18,2},{3,19},{19,3},{4,20},{20... | collective-permute-start | bytes 2162696 | tf_op jit(solution)/shard_map/ppermute | solution.py:42
  15.4 1.0 copy-start.1
  21.4 12.0 %all-to-all-start.5 = ((bf16[8,384,128]{2,1,0:T(8,128)(2,1)}), bf16[8,384,128]{2,1,0:T(8,128)(2,1)S(1)}, u32[]{:S(2)}, u32[]{:S(2)}) async-start(bf16[8,384,128]{2,1,0:T(8,128)(2,1)} %shard_map.96), calls=%async_computation.5 | async-start | bytes 1572864 | tf_op jit(solution)/shard_map/all_to_all | solution.py:213
  25.0 8.4 %collective-permute-start.6 = (bf16[256,1024]{1,0:T(8,128)(2,1)}, bf16[256,1024]{1,0:T(8,128)(2,1)}, u32[]{:S(2)}, u32[]{:S(2)}) collective-permute-start(bf16[256,1024]{1,0:T(8,128)(2,1)} %param.14), channel_id=1, source_target_pairs={{0,16},{16,0},{1,17},{17,1},{2,18},{18,2},{3,19},{19,3},{4,20},{20... | collective-permute-start | bytes 1572872 | tf_op jit(solution)/shard_map/ppermute | solution.py:42
  29.3 3.4 %collective-permute-start.5 = (bf16[16,64,128]{2,1,0:T(8,128)(2,1)S(1)}, bf16[16,64,128]{2,1,0:T(8,128)(2,1)S(1)}, u32[]{:S(2)}, u32[]{:S(2)}) collective-permute-start(bf16[16,64,128]{2,1,0:T(8,128)(2,1)S(1)} %all-to-all-done.6), channel_id=1, source_target_pairs={{0,16},{16,0},{1,17},{17,1},{2,18},{18,2},{3,19},{19,3},{4,20},{20... | collective-permute-start | bytes 786440 | tf_op jit(solution)/shard_map/ppermute | solution.py:42
  33.4 32.8 %copy-start.3 = (bf16[768,256]{1,0:T(8,128)(2,1)S(1)}, bf16[768,256]{1,0:T(8,128)(2,1)}, u32[]{:S(2)}) copy-start(bf16[768,256]{1,0:T(8,128)(2,1)} %param.13) | copy-start | bytes 1179652
  61.0 22.0 %collective-permute-start.10 = (bf16[96,512]{1,0:T(8,128)(2,1)S(1)}, bf16[96,512]{1,0:T(8,128)(2,1)S(1)}, u32[]{:S(2)}, u32[]{:S(2)}) collective-permute-start(bf16[96,512]{1,0:T(8,128)(2,1)S(1)} %shard_map.97), channel_id=1, source_target_pairs={{256,12},{260,0},{264,4},{268,8},{257,13},{261,1},{265,5},{269,9},... | collective-permute-start | bytes 294920 | tf_op jit(solution)/shard_map/ppermute | solution.py:238
  62.3 21.3 %collective-permute-start.9 = (bf16[96,512]{1,0:T(8,128)(2,1)S(1)}, bf16[96,512]{1,0:T(8,128)(2,1)S(1)}, u32[]{:S(2)}, u32[]{:S(2)}) collective-permute-start(bf16[96,512]{1,0:T(8,128)(2,1)S(1)} %shard_map.97), channel_id=1, source_target_pairs={{256,8},{260,12},{264,0},{268,4},{257,9},{261,13},{265,1},{269,5},... | collective-permute-start | bytes 294920 | tf_op jit(solution)/shard_map/ppermute | solution.py:238
  63.6 20.0 %collective-permute-start.8 = (bf16[96,512]{1,0:T(8,128)(2,1)S(1)}, bf16[96,512]{1,0:T(8,128)(2,1)S(1)}, u32[]{:S(2)}, u32[]{:S(2)}) collective-permute-start(bf16[96,512]{1,0:T(8,128)(2,1)S(1)} %shard_map.97), channel_id=1, source_target_pairs={{256,4},{260,8},{264,12},{268,0},{257,5},{261,9},{265,13},{269,1},... | collective-permute-start | bytes 294920 | tf_op jit(solution)/shard_map/ppermute | solution.py:238
  64.9 20.8 %collective-permute-start.7 = (bf16[96,512]{1,0:T(8,128)(2,1)S(1)}, bf16[96,512]{1,0:T(8,128)(2,1)S(1)}, u32[]{:S(2)}, u32[]{:S(2)}) collective-permute-start(bf16[96,512]{1,0:T(8,128)(2,1)S(1)} %shard_map.97), channel_id=1, source_target_pairs={{256,0},{260,4},{264,8},{268,12},{257,1},{261,5},{265,9},{269,13},... | collective-permute-start | bytes 294920 | tf_op jit(solution)/shard_map/ppermute | solution.py:238
  66.2 7.1 %collective-permute-start = (bf16[8,384,128]{2,1,0:T(8,128)(2,1)}, bf16[8,384,128]{2,1,0:T(8,128)(2,1)S(1)}, u32[]{:S(2)}, u32[]{:S(2)}) collective-permute-start(bf16[8,384,128]{2,1,0:T(8,128)(2,1)} %get-tuple-element.60.near), channel_id=1, source_target_pairs={{0,16},{16,0},{1,17},{17,1},{2,18},{18,2},{3,19},{19,3},{4,20},{20... | collective-permute-start | bytes 2359304 | tf_op jit(solution)/shard_map/cond/branch_0_fun/ppermute | solution.py:42
  76.0 4.4 %collective-permute-start.1 = (bf16[8,384,128]{2,1,0:T(8,128)(2,1)}, bf16[8,384,128]{2,1,0:T(8,128)(2,1)S(1)}, u32[]{:S(2)}, u32[]{:S(2)}) collective-permute-start(bf16[8,384,128]{2,1,0:T(8,128)(2,1)} %branch_0_fun.10.near), channel_id=1, source_target_pairs={{0,16},{16,0},{1,17},{17,1},{2,18},{18,2},{3,19},{19,3},{4,20},{20... | collective-permute-start | bytes 2359304 | tf_op jit(solution)/shard_map/cond/branch_0_fun/ppermute | solution.py:42
  100.4 0.7 copy-start.4

commit v7 on v6

--- a/solution.py
+++ b/solution.py
@@ -129,9 +129,26 @@
     cumulative = 0.5 * (1.0 + lax.erf(hidden * 0.7071067811865476))
     grad = (act * (cumulative + hidden * density)).astype(BF16)
     activated = (hidden * cumulative).astype(BF16)
-    for i in range(8):
-        outs[0][i, :HALF, :] = grad
-        outs[-1][i, -HALF:, :] = activated
+    if len(outs) == 1:
+        for i in range(8):
+            outs[0][i, :HALF, :] = grad
+            outs[0][i, HALF:, :] = activated
+        return
+    grads, blocks, held, sem = outs
+    held[...] = activated
+    copy = pltpu.make_async_copy(held, blocks.at[0], sem)
+    copy.start()
+    for i in range(8):
+        grads[i] = grad
+    copy.wait()
+
+
+def spread(blocks, out, held, sem):
+    copy = pltpu.make_async_copy(blocks.at[0], held, sem)
+    copy.start()
+    copy.wait()
+    for i in range(8):
+        out[i] = held[...]
 
 
 def input_part(hg, near, far, out):
@@ -216,7 +233,10 @@
     second = lax.axis_index("half") == 1
 
     def to_x(recv, packs, packs_far, u, u_far):
-        hg, act = call(slope, [share, share], (recv, packs, packs_far), flops=1 << 27, nbytes=2 << 20)
+        hg, act = call(
+            slope, [share, share], (recv, packs, packs_far), flops=1 << 27, nbytes=2 << 20,
+            out_specs=[VMEM, HBM], scratch=(pltpu.VMEM((HALF, 128), BF16), DMA),
+        )
         hg = lax.all_to_all(hg, CHIPS, 0, 0, tiled=True)
         part = call(
             input_part, ((HALF, 512), BF16), (hg, u, u_far),
@@ -252,6 +272,7 @@
         return up, down, first, last
 
     def gather_first(hg, act, x, g):
+        act = call(spread, share, (act,), in_specs=[HBM], scratch=(pltpu.VMEM((HALF, 128), BF16), DMA))
         return gradients(hg, lax.all_to_all(act, CHIPS, 0, 0, tiled=True), x, g)
 
     grad_up, grad_down, *after = lax.cond(second, gather_first, gradients, hg, act, layer_input, incoming)

time: 102 us -> 102 us (level)
  Pallas kernels: 11.2 us -> 9.93 us
  waiting for transfers between devices: 12.6 us -> 13.8 us
    ppermute x4, waiting for transfers between devices: 2.65 us -> 4.06 us  [shards(): lax.ppermute(summed, ('half', 'zh'), [(4 + i, (i + k) % 4) for i in range...]
    pallas_call x11, Pallas kernels: 11.2 us -> 9.93 us  [call(): pl.pallas_call(kernel, out_shape=shapes if many else shapes[0], scratch_s...]
  transfers between devices with their start and end apart: 11 -> 11, of which waited for: 8 -> 8; matrix products, arithmetic and copies ran while one was open for 0% -> 0% of each run, Pallas kernels for 7% -> 6%
where the time goes in v7:
time: 102 us; the launch traced here: 101 us
  blocking collectives  40.2 us (39%)
  starting transfers between devices  34.5 us (34%)
  waiting for transfers between devices  13.8 us (14%)
  Pallas kernels  9.93 us (10%)
  local copies, waits for them, and re-layouts  1.73 us (2%)
    all_to_all x1, blocking collectives, gather_both(): both = lax.all_to_all(both, CHIPS, 0, 0, tiled=True)  25.5 us
    ppermute x5, starting transfers between devices, swap(): return lax.ppermute(value, axis, [(0, 1), (1, 0)])  16.6 us
    all_to_all x1, blocking collectives, spread_x(): passed = lax.all_to_all(whole, ('core', 'x'), 0, 0, tiled=True)  14.7 us
    pallas_call x11, Pallas kernels, call(): pl.pallas_call(kernel, out_shape=shapes if many else shapes[0], scratch_s...  9.93 us
    all_to_all x1, starting transfers between devices, shards(): packs = lax.all_to_all(packs, ('half',) + CHIPS, 0, 0, tiled=True)  9.2 us
    ppermute x5, waiting for transfers between devices, swap(): return lax.ppermute(value, axis, [(0, 1), (1, 0)])  6.47 us
    ppermute x4, starting transfers between devices, shards(): lax.ppermute(summed, ('half', 'zh'), [(4 + i, (i + k) % 4) for i in range...  5.17 us
    ppermute x4, waiting for transfers between devices, shards(): lax.ppermute(summed, ('half', 'zh'), [(4 + i, (i + k) % 4) for i in range...  4.06 us
  transfers between devices with their start and end apart: 11, of which 8 were waited for; matrix products, arithmetic and copies ran while one was open for 0% of the time, Pallas kernels for 6%

profile of v7, /device:TPU:1, one launch (start us, length us, event | category | flops | bytes accessed | tf_op | source)
XLA Modules:
  0.0 101.0 jit_solution(1353687573526348394)
XLA Ops:
  0.6 0.0 copy-start.2
  0.6 0.0 copy-start
  0.7 2.3 %shard_map.94 = (bf16[16,64,128]{2,1,0:T(8,128)(2,1)}, bf16[352,1024]{1,0:T(8,128)(2,1)}) custom-call(bf16[48,1024]{1,0:T(8,128)(2,1)} %codes.1, s32[48]{0:T(128)} %rows.1, bf16[48]{0:T(256)(128)(2,1)} %scales.1, bf16[768,256]{1,0:T(8,128)(2,1)} %g.3, bf16[256,1024]{1,0:T(8,128)(2,1)} %v.3), custom_call_target="tpu_custom_call" | custom-call | bytes 3145728 | tf_op jit(solution)/shard_map/pallas_call | solution.py:31
  3.0 9.2 %all-to-all-start.6 = ((bf16[16,64,128]{2,1,0:T(8,128)(2,1)}), bf16[16,64,128]{2,1,0:T(8,128)(2,1)S(1)}, u32[]{:S(2)}, u32[]{:S(2)}) async-start(bf16[16,64,128]{2,1,0:T(8,128)(2,1)} %get-tuple-element.95._), calls=%async_computation.6 | async-start | bytes 524288 | tf_op jit(solution)/shard_map/all_to_all | solution.py:220
  12.2 3.1 %collective-permute-start.4 = (bf16[352,1024]{1,0:T(8,128)(2,1)}, bf16[352,1024]{1,0:T(8,128)(2,1)S(1)}, u32[]{:S(2)}, u32[]{:S(2)}) collective-permute-start(bf16[352,1024]{1,0:T(8,128)(2,1)} %get-tuple-element.98), channel_id=1, source_target_pairs={{0,16},{16,0},{1,17},{17,1},{2,18},{18,2},{3,19},{19,3},{4,20},{20... | collective-permute-start | bytes 2162696 | tf_op jit(solution)/shard_map/ppermute | solution.py:42
  15.3 0.0 copy-done.2
  15.4 0.0 copy-done
  15.4 0.0 copy-start.1
  15.4 0.9 copy-done.1
  16.4 1.0 collective-permute-done.4.far
  17.4 1.5 %shard_map.96 = bf16[8,384,128]{2,1,0:T(8,128)(2,1)} custom-call(bf16[384,256]{1,0:T(8,128)(2,1)S(1)} %get-tuple-element.96.g.mine, bf16[256,1024]{1,0:T(8,128)(2,1)S(1)} %get-tuple-element.97.v, bf16[352,1024]{1,0:T(8,128)(2,1)S(1)} %collective-permute-done.4.far), custom_call_target="tpu_custom_call" | custom-call | tf_op jit(solution)/shard_map/pallas_call | solution.py:31
  18.8 0.0 copy-start.4
  18.8 2.6 %all-to-all-done.6 = bf16[16,64,128]{2,1,0:T(8,128)(2,1)S(1)} async-done(((bf16[16,64,128]{2,1,0:T(8,128)(2,1)}), bf16[16,64,128]{2,1,0:T(8,128)(2,1)S(1)}, u32[]{:S(2)}, u32[]{:S(2)}) %all-to-all-start.6) | async-done | bytes 262176 | tf_op jit(solution)/shard_map/all_to_all | solution.py:220
  21.4 3.5 %all-to-all-start.5 = ((bf16[8,384,128]{2,1,0:T(8,128)(2,1)}), bf16[8,384,128]{2,1,0:T(8,128)(2,1)S(1)}, u32[]{:S(2)}, u32[]{:S(2)}) async-start(bf16[8,384,128]{2,1,0:T(8,128)(2,1)} %shard_map.96), calls=%async_computation.5 | async-start | bytes 1572864 | tf_op jit(solution)/shard_map/all_to_all | solution.py:230
  25.0 0.0 copy-done.4
  25.0 4.3 %collective-permute-start.6 = (bf16[256,1024]{1,0:T(8,128)(2,1)S(1)}, bf16[256,1024]{1,0:T(8,128)(2,1)}, u32[]{:S(2)}, u32[]{:S(2)}) collective-permute-start(bf16[256,1024]{1,0:T(8,128)(2,1)S(1)} %copy-done.4), channel_id=1, source_target_pairs={{0,16},{16,0},{1,17},{17,1},{2,18},{18,2},{3,19},{19,3},{4,20},{20... | collective-permute-start | bytes 1572872 | tf_op jit(solution)/shard_map/ppermute | solution.py:42
  29.3 1.9 %collective-permute-start.5 = (bf16[16,64,128]{2,1,0:T(8,128)(2,1)S(1)}, bf16[16,64,128]{2,1,0:T(8,128)(2,1)S(1)}, u32[]{:S(2)}, u32[]{:S(2)}) collective-permute-start(bf16[16,64,128]{2,1,0:T(8,128)(2,1)S(1)} %all-to-all-done.6), channel_id=1, source_target_pairs={{0,16},{16,0},{1,17},{17,1},{2,18},{18,2},{3,19},{19,3},{4,20},{20... | collective-permute-start | bytes 786440 | tf_op jit(solution)/shard_map/ppermute | solution.py:42
  31.2 1.5 %collective-permute-done.5 = bf16[16,64,128]{2,1,0:T(8,128)(2,1)S(1)} collective-permute-done((bf16[16,64,128]{2,1,0:T(8,128)(2,1)S(1)}, bf16[16,64,128]{2,1,0:T(8,128)(2,1)S(1)}, u32[]{:S(2)}, u32[]{:S(2)}) %collective-permute-start.5) | collective-permute-done | bytes 262176 | tf_op jit(solution)/shard_map/ppermute | solution.py:42
  32.7 0.7 all-to-all-done.5
  33.4 0.0 collective-permute-done.6
  33.4 27.2 %conditional.3 = (bf16[4,96,512]{2,1,0:T(8,128)(2,1)S(1)}, bf16[8,384,128]{2,1,0:T(8,128)(2,1)}, bf16[8,384,128]{2,1,0:T(8,128)(2,1)S(1)}) conditional(s32[]{:T(128)} %convert_element_type.2, (bf16[8,384,128]{2,1,0:T(8,128)(2,1)S(1)}, bf16[16,64,128]{2,1,0:T(8,128)(2,1)S(1)}, bf16[16,64,128]{2,1,0:T(8,128)(2,1)S(1)}) %tuple.30, ...), branch_computations={%region_0.0_spmd, %region_1.0_spmd} | conditional | flops 536870912 | bytes 11796560 | solution.py:255
  33.4 0.6 branch_0_fun.7
  34.0 25.5 %all_to_all.30.both = bf16[8,768,128]{2,1,0:T(8,128)(2,1)S(1)} all-to-all(bf16[8,768,128]{2,1,0:T(8,128)(2,1)S(1)} %branch_0_fun.7), channel_id=1, replica_groups=mesh['half'=2,'zb'=2,'y'=4,'core'=2,'zh'=4,'x'=4] {'zb','y'}, dimensions={0} | all-to-all | bytes 3145728 | tf_op jit(solution)/shard_map/cond/branch_0_fun/all_to_all | solution.py:251
  59.6 1.0 branch_0_fun.8
  60.6 0.1 shard_map.97
  60.7 1.3 %collective-permute-start.10 = (bf16[96,512]{1,0:T(8,128)(2,1)S(1)}, bf16[96,512]{1,0:T(8,128)(2,1)S(1)}, u32[]{:S(2)}, u32[]{:S(2)}) collective-permute-start(bf16[96,512]{1,0:T(8,128)(2,1)S(1)} %shard_map.97), channel_id=1, source_target_pairs={{256,12},{260,0},{264,4},{268,8},{257,13},{261,1},{265,5},{269,9},... | collective-permute-start | bytes 294920 | tf_op jit(solution)/shard_map/ppermute | solution.py:258
  62.0 1.3 %collective-permute-start.9 = (bf16[96,512]{1,0:T(8,128)(2,1)S(1)}, bf16[96,512]{1,0:T(8,128)(2,1)S(1)}, u32[]{:S(2)}, u32[]{:S(2)}) collective-permute-start(bf16[96,512]{1,0:T(8,128)(2,1)S(1)} %shard_map.97), channel_id=1, source_target_pairs={{256,8},{260,12},{264,0},{268,4},{257,9},{261,13},{265,1},{269,5},... | collective-permute-start | bytes 294920 | tf_op jit(solution)/shard_map/ppermute | solution.py:258
  63.3 1.3 %collective-permute-start.8 = (bf16[96,512]{1,0:T(8,128)(2,1)S(1)}, bf16[96,512]{1,0:T(8,128)(2,1)S(1)}, u32[]{:S(2)}, u32[]{:S(2)}) collective-permute-start(bf16[96,512]{1,0:T(8,128)(2,1)S(1)} %shard_map.97), channel_id=1, source_target_pairs={{256,4},{260,8},{264,12},{268,0},{257,5},{261,9},{265,13},{269,1},... | collective-permute-start | bytes 294920 | tf_op jit(solution)/shard_map/ppermute | solution.py:258
  64.6 1.3 %collective-permute-start.7 = (bf16[96,512]{1,0:T(8,128)(2,1)S(1)}, bf16[96,512]{1,0:T(8,128)(2,1)S(1)}, u32[]{:S(2)}, u32[]{:S(2)}) collective-permute-start(bf16[96,512]{1,0:T(8,128)(2,1)S(1)} %shard_map.97), channel_id=1, source_target_pairs={{256,0},{260,4},{264,8},{268,12},{257,1},{261,5},{265,9},{269,13},... | collective-permute-start | bytes 294920 | tf_op jit(solution)/shard_map/ppermute | solution.py:258
  65.9 15.6 %conditional.4 = (bf16[256,1024]{1,0:T(8,128)(2,1)}, bf16[256,1024]{1,0:T(8,128)(2,1)}, f32[8,128]{1,0:T(8,128)}, f32[8,128]{1,0:T(8,128)S(1)}) conditional(s32[]{:T(128)} %convert_element_type.2, (bf16[8,384,128]{2,1,0:T(8,128)(2,1)}, bf16[768,256]{1,0:T(8,128)(2,1)}, bf16[8,384,128]{2,1,0:T(8,128)(2,1)S(1)}, ...), branch_computations={%region_2.0_spmd, %region_3.0_spmd} | conditional | flops 805306368 | bytes 16515244 | solution.py:278
  65.9 4.9 %collective-permute-start = (bf16[8,384,128]{2,1,0:T(8,128)(2,1)}, bf16[8,384,128]{2,1,0:T(8,128)(2,1)S(1)}, u32[]{:S(2)}, u32[]{:S(2)}) collective-permute-start(bf16[8,384,128]{2,1,0:T(8,128)(2,1)} %get-tuple-element.60.near), channel_id=1, source_target_pairs={{0,16},{16,0},{1,17},{17,1},{2,18},{18,2},{3,19},{19,3},{4,20},{20... | collective-permute-start | bytes 2359304 | tf_op jit(solution)/shard_map/cond/branch_0_fun/ppermute | solution.py:42
  70.9 2.1 %collective-permute-done.far = bf16[8,384,128]{2,1,0:T(8,128)(2,1)S(1)} collective-permute-done((bf16[8,384,128]{2,1,0:T(8,128)(2,1)}, bf16[8,384,128]{2,1,0:T(8,128)(2,1)S(1)}, u32[]{:S(2)}, u32[]{:S(2)}) %collective-permute-start) | collective-permute-done | bytes 786464 | tf_op jit(solution)/shard_map/cond/branch_0_fun/ppermute | solution.py:42
  73.0 2.8 %branch_0_fun.9 = (bf16[256,1024]{1,0:T(8,128)(2,1)}, f32[8,128]{1,0:T(8,128)}) custom-call(bf16[768,256]{1,0:T(8,128)(2,1)} %get-tuple-element.59.left, bf16[8,384,128]{2,1,0:T(8,128)(2,1)} %get-tuple-element.60.near, bf16[8,384,128]{2,1,0:T(8,128)(2,1)S(1)} %collective-permute-done.far), custom_call_target="tpu_custom_call" | custom-call | flops 402653184 | bytes 3145728 | tf_op jit(solution)/shard_map/cond/branch_0_fun/pallas_call | solution.py:31
  75.8 2.3 %collective-permute-start.1 = (bf16[8,384,128]{2,1,0:T(8,128)(2,1)S(1)}, bf16[8,384,128]{2,1,0:T(8,128)(2,1)S(1)}, u32[]{:S(2)}, u32[]{:S(2)}) collective-permute-start(bf16[8,384,128]{2,1,0:T(8,128)(2,1)S(1)} %branch_0_fun.10.near), channel_id=1, source_target_pairs={{0,16},{16,0},{1,17},{17,1},{2,18},{18,2},{3,19},{19,3},{4,20},{20... | collective-permute-start | bytes 2359304 | tf_op jit(solution)/shard_map/cond/branch_0_fun/ppermute | solution.py:42
  78.0 1.9 %collective-permute-done.1.far = bf16[8,384,128]{2,1,0:T(8,128)(2,1)S(1)} collective-permute-done((bf16[8,384,128]{2,1,0:T(8,128)(2,1)S(1)}, bf16[8,384,128]{2,1,0:T(8,128)(2,1)S(1)}, u32[]{:S(2)}, u32[]{:S(2)}) %collective-permute-start.1) | collective-permute-done | bytes 786464 | tf_op jit(solution)/shard_map/cond/branch_0_fun/ppermute | solution.py:42
  79.9 1.5 %branch_0_fun.11 = (bf16[256,1024]{1,0:T(8,128)(2,1)}, f32[8,128]{1,0:T(8,128)S(1)}) custom-call(bf16[768,256]{1,0:T(8,128)(2,1)S(1)} %get-tuple-element.62.left, bf16[8,384,128]{2,1,0:T(8,128)(2,1)S(1)} %branch_0_fun.10.near, bf16[8,384,128]{2,1,0:T(8,128)(2,1)S(1)} %collective-permute-done.1.far), custom_call_target="tpu_custom_call" | custom-call | flops 402653184 | bytes 3145728 | tf_op jit(solution)/shard_map/cond/branch_0_fun/pallas_call | solution.py:31
  81.5 0.0 collective-permute-done.10
  81.5 2.0 %collective-permute-done.9 = bf16[96,512]{1,0:T(8,128)(2,1)S(1)} collective-permute-done((bf16[96,512]{1,0:T(8,128)(2,1)S(1)}, bf16[96,512]{1,0:T(8,128)(2,1)S(1)}, u32[]{:S(2)}, u32[]{:S(2)}) %collective-permute-start.9) | collective-permute-done | bytes 98336 | tf_op jit(solution)/shard_map/ppermute | solution.py:258
  83.4 0.0 collective-permute-done.8
  83.4 2.1 %collective-permute-done.7 = bf16[96,512]{1,0:T(8,128)(2,1)S(1)} collective-permute-done((bf16[96,512]{1,0:T(8,128)(2,1)S(1)}, bf16[96,512]{1,0:T(8,128)(2,1)S(1)}, u32[]{:S(2)}, u32[]{:S(2)}) %collective-permute-start.7) | collective-permute-done | bytes 98336 | tf_op jit(solution)/shard_map/ppermute | solution.py:258
  85.5 14.8 %conditional.5 = (bf16[768,256]{1,0:T(8,128)(2,1)S(1)}) conditional(s32[]{:T(128)} %convert_element_type.2, (f32[8,128]{1,0:T(8,128)}, f32[8,128]{1,0:T(8,128)S(1)}, bf16[96,512]{1,0:T(8,128)(2,1)S(1)}, bf16[96,512]{1,0:T(8,128)(2,1)S(1)}, bf16[96,512]{1,0:T(8,128)(2,1)S(1)}, /*index=5*/bf16[96,512]{1,0:T(8,128)(2,1)S(1)}) %tuple.33, () %tuple.34), branch_computations={%region_4.0_spmd, %region_5.0_spmd} | conditional | bytes 786440 | solution.py:285
  85.5 0.1 branch_0_fun.12
  85.6 14.7 %all_to_all.33.blocks = bf16[8,96,256]{2,1,0:T(8,128)(2,1)S(1)} all-to-all(bf16[8,96,256]{2,1,0:T(8,128)(2,1)S(1)} %branch_0_fun.12), channel_id=1, replica_groups=mesh['half'=2,'zb'=2,'y'=4,'core'=2,'zh'=4,'x'=4] {'core','x'}, dimensions={0} | all-to-all | bytes 786432 | tf_op jit(solution)/shard_map/cond/branch_0_fun/all_to_all | solution.py:282
  100.3 0.0 copy-start.7
  100.3 0.7 copy-done.7
  (4 shorter events, 0.1 us)
Async XLA Ops:
  0.6 14.7 %copy-start.2 = (bf16[768,256]{1,0:T(8,128)(2,1)S(1)}, bf16[768,256]{1,0:T(8,128)(2,1)}, u32[]{:S(2)}) copy-start(bf16[768,256]{1,0:T(8,128)(2,1)} %g.3) | copy-start | bytes 1179652
  0.6 14.7 %copy-start = (bf16[256,1024]{1,0:T(8,128)(2,1)S(1)}, bf16[256,1024]{1,0:T(8,128)(2,1)}, u32[]{:S(2)}) copy-start(bf16[256,1024]{1,0:T(8,128)(2,1)} %v.3) | copy-start | bytes 1572868
  3.0 18.4 %all-to-all-start.6 = ((bf16[16,64,128]{2,1,0:T(8,128)(2,1)}), bf16[16,64,128]{2,1,0:T(8,128)(2,1)S(1)}, u32[]{:S(2)}, u32[]{:S(2)}) async-start(bf16[16,64,128]{2,1,0:T(8,128)(2,1)} %get-tuple-element.95._), calls=%async_computation.6 | async-start | bytes 524288 | tf_op jit(solution)/shard_map/all_to_all | solution.py:220
  12.2 5.1 %collective-permute-start.4 = (bf16[352,1024]{1,0:T(8,128)(2,1)}, bf16[352,1024]{1,0:T(8,128)(2,1)S(1)}, u32[]{:S(2)}, u32[]{:S(2)}) collective-permute-start(bf16[352,1024]{1,0:T(8,128)(2,1)} %get-tuple-element.98), channel_id=1, source_target_pairs={{0,16},{16,0},{1,17},{17,1},{2,18},{18,2},{3,19},{19,3},{4,20},{20... | collective-permute-start | bytes 2162696 | tf_op jit(solution)/shard_map/ppermute | solution.py:42
  15.4 1.0 copy-start.1
  18.8 6.2 %copy-start.4 = (bf16[256,1024]{1,0:T(8,128)(2,1)S(1)}, bf16[256,1024]{1,0:T(8,128)(2,1)}, u32[]{:S(2)}) copy-start(bf16[256,1024]{1,0:T(8,128)(2,1)} %param.14) | copy-start | bytes 1572868
  21.4 12.0 %all-to-all-start.5 = ((bf16[8,384,128]{2,1,0:T(8,128)(2,1)}), bf16[8,384,128]{2,1,0:T(8,128)(2,1)S(1)}, u32[]{:S(2)}, u32[]{:S(2)}) async-start(bf16[8,384,128]{2,1,0:T(8,128)(2,1)} %shard_map.96), calls=%async_computation.5 | async-start | bytes 1572864 | tf_op jit(solution)/shard_map/all_to_all | solution.py:230
  25.0 8.4 %collective-permute-start.6 = (bf16[256,1024]{1,0:T(8,128)(2,1)S(1)}, bf16[256,1024]{1,0:T(8,128)(2,1)}, u32[]{:S(2)}, u32[]{:S(2)}) collective-permute-start(bf16[256,1024]{1,0:T(8,128)(2,1)S(1)} %copy-done.4), channel_id=1, source_target_pairs={{0,16},{16,0},{1,17},{17,1},{2,18},{18,2},{3,19},{19,3},{4,20},{20... | collective-permute-start | bytes 1572872 | tf_op jit(solution)/shard_map/ppermute | solution.py:42
  29.3 3.4 %collective-permute-start.5 = (bf16[16,64,128]{2,1,0:T(8,128)(2,1)S(1)}, bf16[16,64,128]{2,1,0:T(8,128)(2,1)S(1)}, u32[]{:S(2)}, u32[]{:S(2)}) collective-permute-start(bf16[16,64,128]{2,1,0:T(8,128)(2,1)S(1)} %all-to-all-done.6), channel_id=1, source_target_pairs={{0,16},{16,0},{1,17},{17,1},{2,18},{18,2},{3,19},{19,3},{4,20},{20... | collective-permute-start | bytes 786440 | tf_op jit(solution)/shard_map/ppermute | solution.py:42
  60.7 20.8 %collective-permute-start.10 = (bf16[96,512]{1,0:T(8,128)(2,1)S(1)}, bf16[96,512]{1,0:T(8,128)(2,1)S(1)}, u32[]{:S(2)}, u32[]{:S(2)}) collective-permute-start(bf16[96,512]{1,0:T(8,128)(2,1)S(1)} %shard_map.97), channel_id=1, source_target_pairs={{256,12},{260,0},{264,4},{268,8},{257,13},{261,1},{265,5},{269,9},... | collective-permute-start | bytes 294920 | tf_op jit(solution)/shard_map/ppermute | solution.py:258
  62.0 21.5 %collective-permute-start.9 = (bf16[96,512]{1,0:T(8,128)(2,1)S(1)}, bf16[96,512]{1,0:T(8,128)(2,1)S(1)}, u32[]{:S(2)}, u32[]{:S(2)}) collective-permute-start(bf16[96,512]{1,0:T(8,128)(2,1)S(1)} %shard_map.97), channel_id=1, source_target_pairs={{256,8},{260,12},{264,0},{268,4},{257,9},{261,13},{265,1},{269,5},... | collective-permute-start | bytes 294920 | tf_op jit(solution)/shard_map/ppermute | solution.py:258
  63.3 20.2 %collective-permute-start.8 = (bf16[96,512]{1,0:T(8,128)(2,1)S(1)}, bf16[96,512]{1,0:T(8,128)(2,1)S(1)}, u32[]{:S(2)}, u32[]{:S(2)}) collective-permute-start(bf16[96,512]{1,0:T(8,128)(2,1)S(1)} %shard_map.97), channel_id=1, source_target_pairs={{256,4},{260,8},{264,12},{268,0},{257,5},{261,9},{265,13},{269,1},... | collective-permute-start | bytes 294920 | tf_op jit(solution)/shard_map/ppermute | solution.py:258
  64.6 20.9 %collective-permute-start.7 = (bf16[96,512]{1,0:T(8,128)(2,1)S(1)}, bf16[96,512]{1,0:T(8,128)(2,1)S(1)}, u32[]{:S(2)}, u32[]{:S(2)}) collective-permute-start(bf16[96,512]{1,0:T(8,128)(2,1)S(1)} %shard_map.97), channel_id=1, source_target_pairs={{256,0},{260,4},{264,8},{268,12},{257,1},{261,5},{265,9},{269,13},... | collective-permute-start | bytes 294920 | tf_op jit(solution)/shard_map/ppermute | solution.py:258
  65.9 7.1 %collective-permute-start = (bf16[8,384,128]{2,1,0:T(8,128)(2,1)}, bf16[8,384,128]{2,1,0:T(8,128)(2,1)S(1)}, u32[]{:S(2)}, u32[]{:S(2)}) collective-permute-start(bf16[8,384,128]{2,1,0:T(8,128)(2,1)} %get-tuple-element.60.near), channel_id=1, source_target_pairs={{0,16},{16,0},{1,17},{17,1},{2,18},{18,2},{3,19},{19,3},{4,20},{20... | collective-permute-start | bytes 2359304 | tf_op jit(solution)/shard_map/cond/branch_0_fun/ppermute | solution.py:42
  75.8 4.2 %collective-permute-start.1 = (bf16[8,384,128]{2,1,0:T(8,128)(2,1)S(1)}, bf16[8,384,128]{2,1,0:T(8,128)(2,1)S(1)}, u32[]{:S(2)}, u32[]{:S(2)}) collective-permute-start(bf16[8,384,128]{2,1,0:T(8,128)(2,1)S(1)} %branch_0_fun.10.near), channel_id=1, source_target_pairs={{0,16},{16,0},{1,17},{17,1},{2,18},{18,2},{3,19},{19,3},{4,20},{20... | collective-permute-start | bytes 2359304 | tf_op jit(solution)/shard_map/cond/branch_0_fun/ppermute | solution.py:42
  100.3 0.7 copy-start.7

commit v8 on v7

--- a/solution.py
+++ b/solution.py
@@ -23,7 +23,7 @@
 DMA = pltpu.SemaphoreType.DMA
 
 
-def call(kernel, outs, ins, scratch=(), flops=0, nbytes=0, vmem=48, **kwargs):
+def call(kernel, outs, ins, scratch=(), flops=0, nbytes=0, vmem=20, **kwargs):
     many = isinstance(outs, list)
     shapes = [jax.ShapeDtypeStruct(shape, dtype) for shape, dtype in (outs if many else [outs])]
     kwargs.setdefault("in_specs", [VMEM] * len(ins))

time: 102 us -> 102 us (level)
  no operation moved by 1% of the time
where the time goes in v8:
time: 102 us; the launch traced here: 101 us
  blocking collectives  40.2 us (39%)
  starting transfers between devices  34.5 us (34%)
  waiting for transfers between devices  13.8 us (14%)
  Pallas kernels  9.93 us (10%)
  local copies, waits for them, and re-layouts  1.73 us (2%)
    all_to_all x1, blocking collectives, gather_both(): both = lax.all_to_all(both, CHIPS, 0, 0, tiled=True)  25.5 us
    ppermute x5, starting transfers between devices, swap(): return lax.ppermute(value, axis, [(0, 1), (1, 0)])  16.6 us
    all_to_all x1, blocking collectives, spread_x(): passed = lax.all_to_all(whole, ('core', 'x'), 0, 0, tiled=True)  14.7 us
    pallas_call x11, Pallas kernels, call(): pl.pallas_call(kernel, out_shape=shapes if many else shapes[0], scratch_s...  9.93 us
    all_to_all x1, starting transfers between devices, shards(): packs = lax.all_to_all(packs, ('half',) + CHIPS, 0, 0, tiled=True)  9.2 us
    ppermute x5, waiting for transfers between devices, swap(): return lax.ppermute(value, axis, [(0, 1), (1, 0)])  6.47 us
    ppermute x4, starting transfers between devices, shards(): lax.ppermute(summed, ('half', 'zh'), [(4 + i, (i + k) % 4) for i in range...  5.17 us
    ppermute x4, waiting for transfers between devices, shards(): lax.ppermute(summed, ('half', 'zh'), [(4 + i, (i + k) % 4) for i in range...  4.06 us
  transfers between devices with their start and end apart: 11, of which 8 were waited for; matrix products, arithmetic and copies ran while one was open for 0% of the time, Pallas kernels for 6%

profile of v8, /device:TPU:1, one launch (start us, length us, event | category | flops | bytes accessed | tf_op | source)
XLA Modules:
  0.0 101.0 jit_solution(2496265777841454940)
XLA Ops:
  0.6 0.0 copy-start.2
  0.6 0.0 copy-start
  0.7 2.3 %shard_map.94 = (bf16[16,64,128]{2,1,0:T(8,128)(2,1)}, bf16[352,1024]{1,0:T(8,128)(2,1)}) custom-call(bf16[48,1024]{1,0:T(8,128)(2,1)} %codes.1, s32[48]{0:T(128)} %rows.1, bf16[48]{0:T(256)(128)(2,1)} %scales.1, bf16[768,256]{1,0:T(8,128)(2,1)} %g.3, bf16[256,1024]{1,0:T(8,128)(2,1)} %v.3), custom_call_target="tpu_custom_call" | custom-call | bytes 3145728 | tf_op jit(solution)/shard_map/pallas_call | solution.py:31
  3.0 9.2 %all-to-all-start.6 = ((bf16[16,64,128]{2,1,0:T(8,128)(2,1)}), bf16[16,64,128]{2,1,0:T(8,128)(2,1)S(1)}, u32[]{:S(2)}, u32[]{:S(2)}) async-start(bf16[16,64,128]{2,1,0:T(8,128)(2,1)} %get-tuple-element.95._), calls=%async_computation.6 | async-start | bytes 524288 | tf_op jit(solution)/shard_map/all_to_all | solution.py:220
  12.2 3.1 %collective-permute-start.4 = (bf16[352,1024]{1,0:T(8,128)(2,1)}, bf16[352,1024]{1,0:T(8,128)(2,1)S(1)}, u32[]{:S(2)}, u32[]{:S(2)}) collective-permute-start(bf16[352,1024]{1,0:T(8,128)(2,1)} %get-tuple-element.98), channel_id=1, source_target_pairs={{0,16},{16,0},{1,17},{17,1},{2,18},{18,2},{3,19},{19,3},{4,20},{20... | collective-permute-start | bytes 2162696 | tf_op jit(solution)/shard_map/ppermute | solution.py:42
  15.3 0.0 copy-done.2
  15.4 0.0 copy-done
  15.4 0.0 copy-start.1
  15.4 0.9 copy-done.1
  16.4 1.0 collective-permute-done.4.far
  17.4 1.5 %shard_map.96 = bf16[8,384,128]{2,1,0:T(8,128)(2,1)} custom-call(bf16[384,256]{1,0:T(8,128)(2,1)S(1)} %get-tuple-element.96.g.mine, bf16[256,1024]{1,0:T(8,128)(2,1)S(1)} %get-tuple-element.97.v, bf16[352,1024]{1,0:T(8,128)(2,1)S(1)} %collective-permute-done.4.far), custom_call_target="tpu_custom_call" | custom-call | tf_op jit(solution)/shard_map/pallas_call | solution.py:31
  18.8 0.0 copy-start.4
  18.8 2.6 %all-to-all-done.6 = bf16[16,64,128]{2,1,0:T(8,128)(2,1)S(1)} async-done(((bf16[16,64,128]{2,1,0:T(8,128)(2,1)}), bf16[16,64,128]{2,1,0:T(8,128)(2,1)S(1)}, u32[]{:S(2)}, u32[]{:S(2)}) %all-to-all-start.6) | async-done | bytes 262176 | tf_op jit(solution)/shard_map/all_to_all | solution.py:220
  21.4 3.5 %all-to-all-start.5 = ((bf16[8,384,128]{2,1,0:T(8,128)(2,1)}), bf16[8,384,128]{2,1,0:T(8,128)(2,1)S(1)}, u32[]{:S(2)}, u32[]{:S(2)}) async-start(bf16[8,384,128]{2,1,0:T(8,128)(2,1)} %shard_map.96), calls=%async_computation.5 | async-start | bytes 1572864 | tf_op jit(solution)/shard_map/all_to_all | solution.py:230
  25.0 0.0 copy-done.4
  25.0 4.3 %collective-permute-start.6 = (bf16[256,1024]{1,0:T(8,128)(2,1)S(1)}, bf16[256,1024]{1,0:T(8,128)(2,1)}, u32[]{:S(2)}, u32[]{:S(2)}) collective-permute-start(bf16[256,1024]{1,0:T(8,128)(2,1)S(1)} %copy-done.4), channel_id=1, source_target_pairs={{0,16},{16,0},{1,17},{17,1},{2,18},{18,2},{3,19},{19,3},{4,20},{20... | collective-permute-start | bytes 1572872 | tf_op jit(solution)/shard_map/ppermute | solution.py:42
  29.3 1.9 %collective-permute-start.5 = (bf16[16,64,128]{2,1,0:T(8,128)(2,1)S(1)}, bf16[16,64,128]{2,1,0:T(8,128)(2,1)S(1)}, u32[]{:S(2)}, u32[]{:S(2)}) collective-permute-start(bf16[16,64,128]{2,1,0:T(8,128)(2,1)S(1)} %all-to-all-done.6), channel_id=1, source_target_pairs={{0,16},{16,0},{1,17},{17,1},{2,18},{18,2},{3,19},{19,3},{4,20},{20... | collective-permute-start | bytes 786440 | tf_op jit(solution)/shard_map/ppermute | solution.py:42
  31.2 1.5 %collective-permute-done.5 = bf16[16,64,128]{2,1,0:T(8,128)(2,1)S(1)} collective-permute-done((bf16[16,64,128]{2,1,0:T(8,128)(2,1)S(1)}, bf16[16,64,128]{2,1,0:T(8,128)(2,1)S(1)}, u32[]{:S(2)}, u32[]{:S(2)}) %collective-permute-start.5) | collective-permute-done | bytes 262176 | tf_op jit(solution)/shard_map/ppermute | solution.py:42
  32.7 0.7 all-to-all-done.5
  33.4 0.0 collective-permute-done.6
  33.4 27.2 %conditional.3 = (bf16[4,96,512]{2,1,0:T(8,128)(2,1)S(1)}, bf16[8,384,128]{2,1,0:T(8,128)(2,1)}, bf16[8,384,128]{2,1,0:T(8,128)(2,1)S(1)}) conditional(s32[]{:T(128)} %convert_element_type.2, (bf16[8,384,128]{2,1,0:T(8,128)(2,1)S(1)}, bf16[16,64,128]{2,1,0:T(8,128)(2,1)S(1)}, bf16[16,64,128]{2,1,0:T(8,128)(2,1)S(1)}) %tuple.30, ...), branch_computations={%region_0.0_spmd, %region_1.0_spmd} | conditional | flops 536870912 | bytes 11796560 | solution.py:255
  33.4 0.6 branch_0_fun.7
  34.0 25.5 %all_to_all.30.both = bf16[8,768,128]{2,1,0:T(8,128)(2,1)S(1)} all-to-all(bf16[8,768,128]{2,1,0:T(8,128)(2,1)S(1)} %branch_0_fun.7), channel_id=1, replica_groups=mesh['half'=2,'zb'=2,'y'=4,'core'=2,'zh'=4,'x'=4] {'zb','y'}, dimensions={0} | all-to-all | bytes 3145728 | tf_op jit(solution)/shard_map/cond/branch_0_fun/all_to_all | solution.py:251
  59.6 1.0 branch_0_fun.8
  60.6 0.1 shard_map.97
  60.7 1.3 %collective-permute-start.10 = (bf16[96,512]{1,0:T(8,128)(2,1)S(1)}, bf16[96,512]{1,0:T(8,128)(2,1)S(1)}, u32[]{:S(2)}, u32[]{:S(2)}) collective-permute-start(bf16[96,512]{1,0:T(8,128)(2,1)S(1)} %shard_map.97), channel_id=1, source_target_pairs={{256,12},{260,0},{264,4},{268,8},{257,13},{261,1},{265,5},{269,9},... | collective-permute-start | bytes 294920 | tf_op jit(solution)/shard_map/ppermute | solution.py:258
  62.0 1.3 %collective-permute-start.9 = (bf16[96,512]{1,0:T(8,128)(2,1)S(1)}, bf16[96,512]{1,0:T(8,128)(2,1)S(1)}, u32[]{:S(2)}, u32[]{:S(2)}) collective-permute-start(bf16[96,512]{1,0:T(8,128)(2,1)S(1)} %shard_map.97), channel_id=1, source_target_pairs={{256,8},{260,12},{264,0},{268,4},{257,9},{261,13},{265,1},{269,5},... | collective-permute-start | bytes 294920 | tf_op jit(solution)/shard_map/ppermute | solution.py:258
  63.3 1.3 %collective-permute-start.8 = (bf16[96,512]{1,0:T(8,128)(2,1)S(1)}, bf16[96,512]{1,0:T(8,128)(2,1)S(1)}, u32[]{:S(2)}, u32[]{:S(2)}) collective-permute-start(bf16[96,512]{1,0:T(8,128)(2,1)S(1)} %shard_map.97), channel_id=1, source_target_pairs={{256,4},{260,8},{264,12},{268,0},{257,5},{261,9},{265,13},{269,1},... | collective-permute-start | bytes 294920 | tf_op jit(solution)/shard_map/ppermute | solution.py:258
  64.6 1.3 %collective-permute-start.7 = (bf16[96,512]{1,0:T(8,128)(2,1)S(1)}, bf16[96,512]{1,0:T(8,128)(2,1)S(1)}, u32[]{:S(2)}, u32[]{:S(2)}) collective-permute-start(bf16[96,512]{1,0:T(8,128)(2,1)S(1)} %shard_map.97), channel_id=1, source_target_pairs={{256,0},{260,4},{264,8},{268,12},{257,1},{261,5},{265,9},{269,13},... | collective-permute-start | bytes 294920 | tf_op jit(solution)/shard_map/ppermute | solution.py:258
  65.9 15.6 %conditional.4 = (bf16[256,1024]{1,0:T(8,128)(2,1)}, bf16[256,1024]{1,0:T(8,128)(2,1)}, f32[8,128]{1,0:T(8,128)}, f32[8,128]{1,0:T(8,128)S(1)}) conditional(s32[]{:T(128)} %convert_element_type.2, (bf16[8,384,128]{2,1,0:T(8,128)(2,1)}, bf16[768,256]{1,0:T(8,128)(2,1)}, bf16[8,384,128]{2,1,0:T(8,128)(2,1)S(1)}, ...), branch_computations={%region_2.0_spmd, %region_3.0_spmd} | conditional | flops 805306368 | bytes 16515244 | solution.py:278
  65.9 4.9 %collective-permute-start = (bf16[8,384,128]{2,1,0:T(8,128)(2,1)}, bf16[8,384,128]{2,1,0:T(8,128)(2,1)S(1)}, u32[]{:S(2)}, u32[]{:S(2)}) collective-permute-start(bf16[8,384,128]{2,1,0:T(8,128)(2,1)} %get-tuple-element.60.near), channel_id=1, source_target_pairs={{0,16},{16,0},{1,17},{17,1},{2,18},{18,2},{3,19},{19,3},{4,20},{20... | collective-permute-start | bytes 2359304 | tf_op jit(solution)/shard_map/cond/branch_0_fun/ppermute | solution.py:42
  70.9 2.1 %collective-permute-done.far = bf16[8,384,128]{2,1,0:T(8,128)(2,1)S(1)} collective-permute-done((bf16[8,384,128]{2,1,0:T(8,128)(2,1)}, bf16[8,384,128]{2,1,0:T(8,128)(2,1)S(1)}, u32[]{:S(2)}, u32[]{:S(2)}) %collective-permute-start) | collective-permute-done | bytes 786464 | tf_op jit(solution)/shard_map/cond/branch_0_fun/ppermute | solution.py:42
  73.0 2.8 %branch_0_fun.9 = (bf16[256,1024]{1,0:T(8,128)(2,1)}, f32[8,128]{1,0:T(8,128)}) custom-call(bf16[768,256]{1,0:T(8,128)(2,1)} %get-tuple-element.59.left, bf16[8,384,128]{2,1,0:T(8,128)(2,1)} %get-tuple-element.60.near, bf16[8,384,128]{2,1,0:T(8,128)(2,1)S(1)} %collective-permute-done.far), custom_call_target="tpu_custom_call" | custom-call | flops 402653184 | bytes 3145728 | tf_op jit(solution)/shard_map/cond/branch_0_fun/pallas_call | solution.py:31
  75.8 2.3 %collective-permute-start.1 = (bf16[8,384,128]{2,1,0:T(8,128)(2,1)S(1)}, bf16[8,384,128]{2,1,0:T(8,128)(2,1)S(1)}, u32[]{:S(2)}, u32[]{:S(2)}) collective-permute-start(bf16[8,384,128]{2,1,0:T(8,128)(2,1)S(1)} %branch_0_fun.10.near), channel_id=1, source_target_pairs={{0,16},{16,0},{1,17},{17,1},{2,18},{18,2},{3,19},{19,3},{4,20},{20... | collective-permute-start | bytes 2359304 | tf_op jit(solution)/shard_map/cond/branch_0_fun/ppermute | solution.py:42
  78.0 1.9 %collective-permute-done.1.far = bf16[8,384,128]{2,1,0:T(8,128)(2,1)S(1)} collective-permute-done((bf16[8,384,128]{2,1,0:T(8,128)(2,1)S(1)}, bf16[8,384,128]{2,1,0:T(8,128)(2,1)S(1)}, u32[]{:S(2)}, u32[]{:S(2)}) %collective-permute-start.1) | collective-permute-done | bytes 786464 | tf_op jit(solution)/shard_map/cond/branch_0_fun/ppermute | solution.py:42
  79.9 1.5 %branch_0_fun.11 = (bf16[256,1024]{1,0:T(8,128)(2,1)}, f32[8,128]{1,0:T(8,128)S(1)}) custom-call(bf16[768,256]{1,0:T(8,128)(2,1)S(1)} %get-tuple-element.62.left, bf16[8,384,128]{2,1,0:T(8,128)(2,1)S(1)} %branch_0_fun.10.near, bf16[8,384,128]{2,1,0:T(8,128)(2,1)S(1)} %collective-permute-done.1.far), custom_call_target="tpu_custom_call" | custom-call | flops 402653184 | bytes 3145728 | tf_op jit(solution)/shard_map/cond/branch_0_fun/pallas_call | solution.py:31
  81.5 0.0 collective-permute-done.10
  81.5 2.0 %collective-permute-done.9 = bf16[96,512]{1,0:T(8,128)(2,1)S(1)} collective-permute-done((bf16[96,512]{1,0:T(8,128)(2,1)S(1)}, bf16[96,512]{1,0:T(8,128)(2,1)S(1)}, u32[]{:S(2)}, u32[]{:S(2)}) %collective-permute-start.9) | collective-permute-done | bytes 98336 | tf_op jit(solution)/shard_map/ppermute | solution.py:258
  83.4 0.0 collective-permute-done.8
  83.4 2.1 %collective-permute-done.7 = bf16[96,512]{1,0:T(8,128)(2,1)S(1)} collective-permute-done((bf16[96,512]{1,0:T(8,128)(2,1)S(1)}, bf16[96,512]{1,0:T(8,128)(2,1)S(1)}, u32[]{:S(2)}, u32[]{:S(2)}) %collective-permute-start.7) | collective-permute-done | bytes 98336 | tf_op jit(solution)/shard_map/ppermute | solution.py:258
  85.5 14.8 %conditional.5 = (bf16[768,256]{1,0:T(8,128)(2,1)S(1)}) conditional(s32[]{:T(128)} %convert_element_type.2, (f32[8,128]{1,0:T(8,128)}, f32[8,128]{1,0:T(8,128)S(1)}, bf16[96,512]{1,0:T(8,128)(2,1)S(1)}, bf16[96,512]{1,0:T(8,128)(2,1)S(1)}, bf16[96,512]{1,0:T(8,128)(2,1)S(1)}, /*index=5*/bf16[96,512]{1,0:T(8,128)(2,1)S(1)}) %tuple.33, () %tuple.34), branch_computations={%region_4.0_spmd, %region_5.0_spmd} | conditional | bytes 786440 | solution.py:285
  85.5 0.1 branch_0_fun.12
  85.6 14.7 %all_to_all.33.blocks = bf16[8,96,256]{2,1,0:T(8,128)(2,1)S(1)} all-to-all(bf16[8,96,256]{2,1,0:T(8,128)(2,1)S(1)} %branch_0_fun.12), channel_id=1, replica_groups=mesh['half'=2,'zb'=2,'y'=4,'core'=2,'zh'=4,'x'=4] {'core','x'}, dimensions={0} | all-to-all | bytes 786432 | tf_op jit(solution)/shard_map/cond/branch_0_fun/all_to_all | solution.py:282
  100.3 0.0 copy-start.7
  100.3 0.7 copy-done.7
  (4 shorter events, 0.1 us)
Async XLA Ops:
  0.6 14.7 %copy-start.2 = (bf16[768,256]{1,0:T(8,128)(2,1)S(1)}, bf16[768,256]{1,0:T(8,128)(2,1)}, u32[]{:S(2)}) copy-start(bf16[768,256]{1,0:T(8,128)(2,1)} %g.3) | copy-start | bytes 1179652
  0.6 14.7 %copy-start = (bf16[256,1024]{1,0:T(8,128)(2,1)S(1)}, bf16[256,1024]{1,0:T(8,128)(2,1)}, u32[]{:S(2)}) copy-start(bf16[256,1024]{1,0:T(8,128)(2,1)} %v.3) | copy-start | bytes 1572868
  3.0 18.4 %all-to-all-start.6 = ((bf16[16,64,128]{2,1,0:T(8,128)(2,1)}), bf16[16,64,128]{2,1,0:T(8,128)(2,1)S(1)}, u32[]{:S(2)}, u32[]{:S(2)}) async-start(bf16[16,64,128]{2,1,0:T(8,128)(2,1)} %get-tuple-element.95._), calls=%async_computation.6 | async-start | bytes 524288 | tf_op jit(solution)/shard_map/all_to_all | solution.py:220
  12.2 5.1 %collective-permute-start.4 = (bf16[352,1024]{1,0:T(8,128)(2,1)}, bf16[352,1024]{1,0:T(8,128)(2,1)S(1)}, u32[]{:S(2)}, u32[]{:S(2)}) collective-permute-start(bf16[352,1024]{1,0:T(8,128)(2,1)} %get-tuple-element.98), channel_id=1, source_target_pairs={{0,16},{16,0},{1,17},{17,1},{2,18},{18,2},{3,19},{19,3},{4,20},{20... | collective-permute-start | bytes 2162696 | tf_op jit(solution)/shard_map/ppermute | solution.py:42
  15.4 1.0 copy-start.1
  18.8 6.2 %copy-start.4 = (bf16[256,1024]{1,0:T(8,128)(2,1)S(1)}, bf16[256,1024]{1,0:T(8,128)(2,1)}, u32[]{:S(2)}) copy-start(bf16[256,1024]{1,0:T(8,128)(2,1)} %param.14) | copy-start | bytes 1572868
  21.4 12.0 %all-to-all-start.5 = ((bf16[8,384,128]{2,1,0:T(8,128)(2,1)}), bf16[8,384,128]{2,1,0:T(8,128)(2,1)S(1)}, u32[]{:S(2)}, u32[]{:S(2)}) async-start(bf16[8,384,128]{2,1,0:T(8,128)(2,1)} %shard_map.96), calls=%async_computation.5 | async-start | bytes 1572864 | tf_op jit(solution)/shard_map/all_to_all | solution.py:230
  25.0 8.4 %collective-permute-start.6 = (bf16[256,1024]{1,0:T(8,128)(2,1)S(1)}, bf16[256,1024]{1,0:T(8,128)(2,1)}, u32[]{:S(2)}, u32[]{:S(2)}) collective-permute-start(bf16[256,1024]{1,0:T(8,128)(2,1)S(1)} %copy-done.4), channel_id=1, source_target_pairs={{0,16},{16,0},{1,17},{17,1},{2,18},{18,2},{3,19},{19,3},{4,20},{20... | collective-permute-start | bytes 1572872 | tf_op jit(solution)/shard_map/ppermute | solution.py:42
  29.3 3.4 %collective-permute-start.5 = (bf16[16,64,128]{2,1,0:T(8,128)(2,1)S(1)}, bf16[16,64,128]{2,1,0:T(8,128)(2,1)S(1)}, u32[]{:S(2)}, u32[]{:S(2)}) collective-permute-start(bf16[16,64,128]{2,1,0:T(8,128)(2,1)S(1)} %all-to-all-done.6), channel_id=1, source_target_pairs={{0,16},{16,0},{1,17},{17,1},{2,18},{18,2},{3,19},{19,3},{4,20},{20... | collective-permute-start | bytes 786440 | tf_op jit(solution)/shard_map/ppermute | solution.py:42
  60.7 20.8 %collective-permute-start.10 = (bf16[96,512]{1,0:T(8,128)(2,1)S(1)}, bf16[96,512]{1,0:T(8,128)(2,1)S(1)}, u32[]{:S(2)}, u32[]{:S(2)}) collective-permute-start(bf16[96,512]{1,0:T(8,128)(2,1)S(1)} %shard_map.97), channel_id=1, source_target_pairs={{256,12},{260,0},{264,4},{268,8},{257,13},{261,1},{265,5},{269,9},... | collective-permute-start | bytes 294920 | tf_op jit(solution)/shard_map/ppermute | solution.py:258
  62.0 21.5 %collective-permute-start.9 = (bf16[96,512]{1,0:T(8,128)(2,1)S(1)}, bf16[96,512]{1,0:T(8,128)(2,1)S(1)}, u32[]{:S(2)}, u32[]{:S(2)}) collective-permute-start(bf16[96,512]{1,0:T(8,128)(2,1)S(1)} %shard_map.97), channel_id=1, source_target_pairs={{256,8},{260,12},{264,0},{268,4},{257,9},{261,13},{265,1},{269,5},... | collective-permute-start | bytes 294920 | tf_op jit(solution)/shard_map/ppermute | solution.py:258
  63.3 20.2 %collective-permute-start.8 = (bf16[96,512]{1,0:T(8,128)(2,1)S(1)}, bf16[96,512]{1,0:T(8,128)(2,1)S(1)}, u32[]{:S(2)}, u32[]{:S(2)}) collective-permute-start(bf16[96,512]{1,0:T(8,128)(2,1)S(1)} %shard_map.97), channel_id=1, source_target_pairs={{256,4},{260,8},{264,12},{268,0},{257,5},{261,9},{265,13},{269,1},... | collective-permute-start | bytes 294920 | tf_op jit(solution)/shard_map/ppermute | solution.py:258
  64.6 20.9 %collective-permute-start.7 = (bf16[96,512]{1,0:T(8,128)(2,1)S(1)}, bf16[96,512]{1,0:T(8,128)(2,1)S(1)}, u32[]{:S(2)}, u32[]{:S(2)}) collective-permute-start(bf16[96,512]{1,0:T(8,128)(2,1)S(1)} %shard_map.97), channel_id=1, source_target_pairs={{256,0},{260,4},{264,8},{268,12},{257,1},{261,5},{265,9},{269,13},... | collective-permute-start | bytes 294920 | tf_op jit(solution)/shard_map/ppermute | solution.py:258
  65.9 7.1 %collective-permute-start = (bf16[8,384,128]{2,1,0:T(8,128)(2,1)}, bf16[8,384,128]{2,1,0:T(8,128)(2,1)S(1)}, u32[]{:S(2)}, u32[]{:S(2)}) collective-permute-start(bf16[8,384,128]{2,1,0:T(8,128)(2,1)} %get-tuple-element.60.near), channel_id=1, source_target_pairs={{0,16},{16,0},{1,17},{17,1},{2,18},{18,2},{3,19},{19,3},{4,20},{20... | collective-permute-start | bytes 2359304 | tf_op jit(solution)/shard_map/cond/branch_0_fun/ppermute | solution.py:42
  75.8 4.2 %collective-permute-start.1 = (bf16[8,384,128]{2,1,0:T(8,128)(2,1)S(1)}, bf16[8,384,128]{2,1,0:T(8,128)(2,1)S(1)}, u32[]{:S(2)}, u32[]{:S(2)}) collective-permute-start(bf16[8,384,128]{2,1,0:T(8,128)(2,1)S(1)} %branch_0_fun.10.near), channel_id=1, source_target_pairs={{0,16},{16,0},{1,17},{17,1},{2,18},{18,2},{3,19},{19,3},{4,20},{20... | collective-permute-start | bytes 2359304 | tf_op jit(solution)/shard_map/cond/branch_0_fun/ppermute | solution.py:42
  100.3 0.7 copy-start.7
